TPU v7x, 32 devices: a whole 2x2x4 slice. The times are simulated.
32 devices in a mesh: geom: 4 (over x, core), dom: 8 (over z, y).
Axes of the slice: x: 2, y: 2, z: 4, core: 2. Of those that a mesh axis runs over, the one named last changes fastest.
Arguments:
- h_in: bfloat16 [4, 4096, 512], P('geom', 'dom'), may hold values from -6 to 6
- edge_in: bfloat16 [4, 16384, 512], P('geom', 'dom'), may hold values from -6 to 6
- new_index: int32 [4, 4096], P('geom', 'dom'), may hold values from 0 to 4095, as said below
- source: int32 [4, 16384], P('geom', 'dom'), may hold values from 0 to 4095, as said below
- w_edge_in: bfloat16 [1536, 512], replicated, may hold values from -0.15625 to 0.15625
- w_edge_out: bfloat16 [512, 512], replicated, may hold values from -0.25 to 0.25
- w_node_in: bfloat16 [1024, 512], replicated, may hold values from -0.1875 to 0.1875
- w_node_out: bfloat16 [512, 512], replicated, may hold values from -0.25 to 0.25
- cot_nodes: bfloat16 [4, 4096, 512], P('geom', 'dom'), may hold values from -6 to 6
- cot_edges: bfloat16 [4, 16384, 512], P('geom', 'dom'), may hold values from -6 to 6
Outputs:
- node_new: bfloat16 [4, 4096, 512], P('geom', 'dom')
- edge_new: bfloat16 [4, 16384, 512], P('geom', 'dom')
- grad_in: bfloat16 [4, 4096, 512], P('geom', 'dom')
- grad_edge: bfloat16 [4, 16384, 512], P('geom', 'dom')
- weight_grads: float32 [3584, 512], P('dom')
Inputs may be any that keep to these rules, and one draw needn't show every extreme that they name: `new_index`: per geometry a permutation of the 4096 cells. The cells in rows k * 512 to (k + 1) * 512 - 1 of the old layout reach the rows of any one device of the new layout at most 96 times, exactly 96 times for some pairs. `source`: an edge of a cell in rows k * 512 to (k + 1) * 512 - 1 comes from a cell of the same range, of the last 64 cells of the range before, or of the first 64 cells of the range after.
All inputs are finite; a program needn't handle non-finite values.
Results may differ from a plain program's by a relative error of at most 0.019.
Values may be sent and summed in bfloat16 or wider, within the bound.
No kernel may reach another device: no remote copies, remote signals or barrier semaphores. Data moves between devices by JAX's collectives and lax.ppermute only.
A program may use at most 128 MiB of HBM per device.

v0:
```python
import functools
import math

import jax
import jax.numpy as jnp
from jax import lax
from jax.experimental import pallas as pl
from jax.experimental.pallas import tpu as pltpu
from jax.sharding import PartitionSpec as P

HB = 64
LANES = 128
EDGE_BLOCK = 512
MIB = 1024 * 1024
MAIN_LIMIT = 25
PREP_LIMIT = 20
PART, CORE, DOM_BIT, OWNER, GEOM_BITS = range(5)
F32 = jnp.float32
BF16 = jnp.bfloat16
VMEM = pltpu.VMEM
SMEM = pltpu.SMEM


def dot_nn(left, right):
    return lax.dot_general(left, right, (((1,), (0,)), ((), ())), preferred_element_type=F32)


def dot_nt(left, right):
    return lax.dot_general(left, right, (((1,), (1,)), ((), ())), preferred_element_type=F32)


def dot_tn(left, right):
    return lax.dot_general(left, right, (((0,), (0,)), ((), ())), preferred_element_type=F32)


def iota(shape, axis):
    return lax.broadcasted_iota(jnp.int32, shape, axis)


def hot(condition):
    return jnp.where(condition, 1.0, 0.0).astype(BF16)


def sigmoid(values):
    return 0.5 * jnp.tanh(0.5 * values) + 0.5


def normalize(values):
    center = values - jnp.mean(values, axis=-1, keepdims=True)
    inverse = lax.rsqrt(jnp.mean(center * center, axis=-1, keepdims=True) + 1e-05)
    return center * inverse, inverse


def normalize_back(normed, inverse, upstream):
    return inverse * (
        upstream
        - jnp.mean(upstream, axis=-1, keepdims=True)
        - normed * jnp.mean(upstream * normed, axis=-1, keepdims=True)
    )


def slots_of(index, me, part_count, cell_count):
    owner = jnp.zeros_like(index)
    for part in range(1, part_count):
        owner = owner + jnp.where(index >= part * cell_count, 1, 0)
    row = index - owner * cell_count
    ahead = owner - me
    ahead = jnp.where(ahead < 0, ahead + part_count, ahead)
    high = -(-part_count // 16) * 16
    member = hot(iota((high, cell_count), 0) == ahead)
    before = hot(iota((cell_count, cell_count), 0) < iota((cell_count, cell_count), 1))
    rank = jnp.sum(member.astype(F32) * dot_nn(member, before), axis=0, keepdims=True)
    return ahead * LANES + rank.astype(jnp.int32), row


def pack_kernel(part_count, capacity, scal, h_ref, index_ref, *outs):
    cell_count, width = h_ref.shape
    chunks = width // LANES
    slot, row = slots_of(index_ref[...], scal[PART], part_count, cell_count)
    kind = iota((16, cell_count), 0)
    coded = jnp.where(
        kind == 0, row >> 8, jnp.where(kind == 1, row & 255, jnp.where(kind == 2, 1, 0))
    )
    coded = coded.astype(F32).astype(BF16)
    cells = h_ref[...]
    for step in range(part_count):
        pick = hot(iota((LANES, cell_count), 0) + step * LANES == slot)
        rows = dot_nn(pick, cells).astype(BF16)
        for chunk in range(chunks):
            outs[step][chunk * capacity : (chunk + 1) * capacity, :] = rows[
                :capacity, chunk * LANES : (chunk + 1) * LANES
            ]
        outs[step][chunks * capacity :, :] = dot_nt(coded, pick).astype(BF16)
    outs[part_count][...] = jnp.zeros(outs[part_count].shape, F32)


def place(ids, cell_count):
    ids = ids.astype(F32)
    spot = ids[0:1] * 256.0 + ids[1:2] + (ids[2:3] - 1.0) * 65536.0
    return hot(iota((cell_count, LANES), 0) == spot.astype(jnp.int32))


def unpack_kernel(part_count, capacity, *refs):
    blocks = refs[:part_count]
    _, nodes_ref, head_ref, tail_ref, ids_ref, rows_ref, hot_ref = refs[part_count:]
    cell_count, width = nodes_ref.shape
    chunks = width // LANES
    for step in range(part_count):
        base = step * LANES
        ids = blocks[step][chunks * capacity :, :]
        ids_ref[step * 16 : (step + 1) * 16, :] = ids
        hot_ref[:, base : base + LANES] = place(ids, cell_count)
        for chunk in range(chunks):
            rows_ref[base : base + capacity, chunk * LANES : (chunk + 1) * LANES] = blocks[step][
                chunk * capacity : (chunk + 1) * capacity, :
            ]
        if capacity < LANES:
            rows_ref[base + capacity : base + LANES, :] = jnp.zeros(
                (LANES - capacity, width), BF16
            )
    nodes = dot_nn(hot_ref[...], rows_ref[...]).astype(BF16)
    nodes_ref[...] = nodes
    head_ref[...] = nodes[:HB]
    tail_ref[...] = nodes[cell_count - HB :]


def prep_kernel(
    fan_in,
    cell_count,
    scal,
    source_hbm,
    edges_hbm,
    cot_nodes_hbm,
    cot_edges_hbm,
    w_edge_in_hbm,
    w_edge_out_hbm,
    w_node_in_hbm,
    w_node_out_hbm,
    _,
    edges_ref,
    cot_nodes_ref,
    cot_edges_ref,
    w_edge_in_ref,
    w_edge_out_ref,
    w_node_in_ref,
    w_node_out_ref,
    gather_ref,
    scatter_ref,
    pre_ref,
    token_ref,
    source_ref,
    sems,
):
    edge_count, width = edges_ref.shape
    padded = cell_count + 2 * HB
    cells = EDGE_BLOCK // fan_in
    loads = [
        pltpu.make_async_copy(far, near, sems.at[at])
        for at, (far, near) in enumerate(
            (
                (source_hbm, source_ref),
                (edges_hbm, edges_ref),
                (w_edge_in_hbm, w_edge_in_ref),
                (w_edge_out_hbm, w_edge_out_ref),
                (w_node_in_hbm, w_node_in_ref),
                (w_node_out_hbm, w_node_out_ref),
                (cot_nodes_hbm, cot_nodes_ref),
                (cot_edges_hbm, cot_edges_ref),
            )
        )
    ]
    for load in loads:
        load.start()
    token_ref[...] = jnp.zeros(token_ref.shape, F32)
    loads[0].wait()
    offset = scal[PART] * cell_count - HB

    def hots(step, carry):
        rows = pl.ds(pl.multiple_of(step * EDGE_BLOCK, EDGE_BLOCK), EDGE_BLOCK)
        local = source_ref[:, rows] - offset
        scatter_ref[:, rows] = hot(iota((padded, EDGE_BLOCK), 0) == local)
        local = jnp.transpose(jnp.broadcast_to(local.astype(F32), (LANES, EDGE_BLOCK)))
        local = local.astype(jnp.int32)
        lane = iota((EDGE_BLOCK, LANES), 1)
        for at in range(0, padded, LANES):
            gather_ref[rows, at : at + LANES] = hot(local == lane + at)
        gather_ref[rows, padded:] = hot(
            iota((EDGE_BLOCK, cells), 0) // fan_in == iota((EDGE_BLOCK, cells), 1)
        )
        return carry

    lax.fori_loop(0, edge_count // EDGE_BLOCK, hots, 0)
    loads[1].wait()
    loads[2].wait()

    def first(step, carry):
        rows = pl.ds(pl.multiple_of(step * EDGE_BLOCK, EDGE_BLOCK), EDGE_BLOCK)
        pre_ref[rows, :] = dot_nn(edges_ref[rows, :], w_edge_in_ref[:width, :])
        return carry

    lax.fori_loop(0, edge_count // EDGE_BLOCK, first, 0)
    for load in loads[3:]:
        load.wait()


def main_kernel(
    fan_in,
    scale,
    scal,
    nodes_ref,
    prev_ref,
    next_ref,
    edges_ref,
    cot_nodes_ref,
    cot_edges_ref,
    w_edge_in_ref,
    w_edge_out_ref,
    w_node_in_ref,
    w_node_out_ref,
    gather_ref,
    scatter_ref,
    pre_ref,
    edge_new_hbm,
    node_new_hbm,
    pre_grad_ref,
    summed_grad_ref,
    to_prev_ref,
    to_next_ref,
    node_grad_ref,
    keep_ref,
    send_ref,
    node_new_ref,
    cells_ref,
    table_ref,
    recv_ref,
    hidden_ref,
    slope_ref,
    normed_ref,
    inverse_ref,
    summed_ref,
    post_grad_ref,
    received_ref,
    out_sems,
):
    cell_count, width = nodes_ref.shape
    edge_count = edges_ref.shape[0]
    steps = edge_count // EDGE_BLOCK
    padded = cell_count + 2 * HB
    cells = EDGE_BLOCK // fan_in
    half = width // 2
    inner = slice(HB, HB + cell_count)

    cells_ref[:HB, :] = prev_ref[...]
    cells_ref[inner, :] = nodes_ref[...]
    cells_ref[HB + cell_count :, :] = next_ref[...]
    table_ref[:padded, :] = dot_nn(cells_ref[...], w_edge_in_ref[width : 2 * width, :]).astype(BF16)
    recv_ref[...] = dot_nn(nodes_ref[...], w_edge_in_ref[2 * width :, :]).astype(BF16)
    collect = hot(iota((cells, EDGE_BLOCK), 0) == iota((cells, EDGE_BLOCK), 1) // fan_in)

    def forward(step, carry):
        spot = pl.ds(pl.multiple_of(step * cells, cells), cells)
        rows = pl.ds(pl.multiple_of(step * EDGE_BLOCK, EDGE_BLOCK), EDGE_BLOCK)
        table_ref[padded : padded + cells, :] = recv_ref[spot, :]
        edges = edges_ref[rows, :]
        pre = pre_ref[rows, :] + dot_nn(gather_ref[rows, :], table_ref[...])
        gate = sigmoid(pre)
        hidden = (pre * gate).astype(BF16)
        hidden_ref[rows, :] = hidden
        slope_ref[rows, :] = (gate * (1.0 + pre * (1.0 - gate))).astype(BF16)
        normed, inverse = normalize(dot_nn(hidden, w_edge_out_ref[...]))
        normed_ref[rows, :] = normed.astype(BF16)
        inverse_ref[rows, :] = inverse
        edge_new = (edges.astype(F32) + normed).astype(BF16)
        post_grad_ref[rows, :] = edge_new
        summed_ref[spot, :] = dot_nn(collect, edge_new).astype(BF16)
        return carry

    lax.fori_loop(0, steps, forward, 0)
    edge_store = pltpu.make_async_copy(post_grad_ref, edge_new_hbm, out_sems.at[0])
    edge_store.start()
    nodes = nodes_ref[...]
    summed = summed_ref[...]
    node_pre = dot_nn(nodes, w_node_in_ref[:width, :]) + dot_nn(summed, w_node_in_ref[width:, :])
    node_gate = sigmoid(node_pre)
    node_hidden = (node_pre * node_gate).astype(BF16)
    node_normed, node_inverse = normalize(dot_nn(node_hidden, w_node_out_ref[...]))
    node_new_ref[...] = (nodes.astype(F32) + node_normed).astype(BF16)
    node_store = pltpu.make_async_copy(node_new_ref, node_new_hbm, out_sems.at[1])
    node_store.start()
    upstream = cot_nodes_ref[...].astype(F32)
    node_post_grad = normalize_back(node_normed, node_inverse, upstream).astype(BF16)
    node_slope = node_gate * (1.0 + node_pre * (1.0 - node_gate))
    node_pre_grad = (dot_nt(node_post_grad, w_node_out_ref[...]) * node_slope).astype(BF16)
    summed_grad = dot_nt(node_pre_grad, w_node_in_ref[width:, :])
    high = summed_grad.astype(BF16)
    low = (summed_grad - high.astype(F32)).astype(BF16)
    for block in range(steps):
        at = slice(block * cells, (block + 1) * cells)
        summed_grad_ref[2 * block * cells : (2 * block + 1) * cells, :] = high[at]
        summed_grad_ref[(2 * block + 1) * cells : 2 * (block + 1) * cells, :] = low[at]
    node_grad_ref[...] = upstream + dot_nt(node_pre_grad, w_node_in_ref[:width, :])
    member = iota((EDGE_BLOCK, 2 * cells), 1)
    owner = iota((EDGE_BLOCK, 2 * cells), 0) // fan_in
    spread = hot((owner == member) | (owner + cells == member))

    edge_store.wait()

    def backward(step, carry):
        spot = pl.ds(pl.multiple_of(step * cells, cells), cells)
        pair = pl.ds(pl.multiple_of(step * 2 * cells, 2 * cells), 2 * cells)
        rows = pl.ds(pl.multiple_of(step * EDGE_BLOCK, EDGE_BLOCK), EDGE_BLOCK)
        upstream = cot_edges_ref[rows, :].astype(F32) + dot_nn(spread, summed_grad_ref[pair, :])
        post_grad = normalize_back(
            normed_ref[rows, :].astype(F32), inverse_ref[rows, :], upstream
        )
        post_grad = post_grad.astype(BF16)
        post_grad_ref[rows, :] = post_grad
        pre_grad = (dot_nt(post_grad, w_edge_out_ref[...]) * slope_ref[rows, :].astype(F32)).astype(
            BF16
        )
        pre_grad_ref[rows, :] = pre_grad
        received_ref[spot, :] = dot_nn(collect, pre_grad).astype(BF16)
        return carry

    lax.fori_loop(0, steps, backward, 0)
    first = scal[CORE] == 0

    def put(place_at, value):
        value = (value * scale).astype(BF16)
        rows = slice(place_at * width, (place_at + 1) * width)
        left = value[:, :half]
        right = value[:, half:]
        keep_ref[rows, :] = jnp.where(first, left, right)
        send_ref[rows, :] = jnp.where(first, right, left)

    sent = dot_nn(scatter_ref[...], pre_grad_ref[...]).astype(BF16)
    sender = dot_nt(sent, w_edge_in_ref[width : 2 * width, :])
    to_prev_ref[...] = sender[:HB].astype(BF16)
    to_next_ref[...] = sender[HB + cell_count :].astype(BF16)
    node_grad_ref[...] = (
        node_grad_ref[...]
        + dot_nt(received_ref[...], w_edge_in_ref[2 * width :, :])
        + sender[inner]
    )
    put(0, dot_tn(edges_ref[...], pre_grad_ref[...]))
    put(1, dot_tn(cells_ref[...], sent))
    put(2, dot_tn(nodes, received_ref[...]))
    put(3, dot_tn(hidden_ref[...], post_grad_ref[...]))
    put(4, dot_tn(nodes, node_pre_grad))
    put(5, dot_tn(summed, node_pre_grad))
    put(6, dot_tn(node_hidden, node_post_grad))
    node_store.wait()


def edge_kernel(
    fan_in,
    cot_ref,
    summed_grad_ref,
    pre_grad_ref,
    w_edge_in_ref,
    _,
    grad_edge_hbm,
    token_ref,
    grad_edge_ref,
    sems,
):
    edge_count, width = cot_ref.shape
    steps = edge_count // EDGE_BLOCK
    cells = EDGE_BLOCK // fan_in
    member = iota((EDGE_BLOCK, 2 * cells), 1)
    owner = iota((EDGE_BLOCK, 2 * cells), 0) // fan_in
    spread = hot((owner == member) | (owner + cells == member))
    stores = []
    for step in range(steps):
        rows = slice(step * EDGE_BLOCK, (step + 1) * EDGE_BLOCK)
        pair = slice(step * 2 * cells, (step + 1) * 2 * cells)
        upstream = cot_ref[rows, :].astype(F32) + dot_nn(spread, summed_grad_ref[pair, :])
        grad_edge_ref[rows, :] = (
            upstream + dot_nt(pre_grad_ref[rows, :], w_edge_in_ref[:width, :])
        ).astype(BF16)
        stores.append(
            pltpu.make_async_copy(
                grad_edge_ref.at[rows, :], grad_edge_hbm.at[rows, :], sems.at[step]
            )
        )
        stores[-1].start()
    token_ref[...] = jnp.zeros(token_ref.shape, F32)
    for store in stores:
        store.wait()


def return_kernel(
    part_count, capacity, scal, node_grad_ref, from_prev_ref, from_next_ref, ids_ref, out_ref, token_ref
):
    cell_count, width = node_grad_ref.shape
    chunks = width // LANES
    block_rows = chunks * capacity
    token_ref[...] = jnp.zeros(token_ref.shape, F32)
    first = node_grad_ref[:HB, :] + from_prev_ref[...].astype(F32)
    last = node_grad_ref[cell_count - HB :, :] + from_next_ref[...].astype(F32)
    grad = jnp.concatenate(
        [first, node_grad_ref[HB : cell_count - HB, :], last], axis=0
    ).astype(BF16)
    for step in range(part_count):
        pick = place(ids_ref[step * 16 : (step + 1) * 16, :], cell_count)
        rows = dot_tn(pick, grad).astype(BF16)
        owner = scal[PART] - step
        owner = jnp.where(owner < 0, owner + part_count, owner)
        for chunk in range(chunks):
            start = pl.multiple_of(owner * block_rows + chunk * capacity, 16)
            out_ref[pl.ds(start, capacity), :] = rows[
                :capacity, chunk * LANES : (chunk + 1) * LANES
            ]


def finish_kernel(
    part_count, capacity, scal, index_ref, block_ref, out_ref, token_ref, rows_ref, pick_ref
):
    cell_count, width = out_ref.shape
    chunks = width // LANES
    block_rows = chunks * capacity
    token_ref[...] = jnp.zeros(token_ref.shape, F32)
    slot, _ = slots_of(index_ref[...], scal[PART], part_count, cell_count)
    for step in range(part_count):
        base = step * LANES
        pick_ref[base : base + LANES, :] = hot(iota((LANES, cell_count), 0) + base == slot)
        owner = scal[PART] + step
        owner = jnp.where(owner >= part_count, owner - part_count, owner)
        for chunk in range(chunks):
            start = pl.multiple_of(owner * block_rows + chunk * capacity, 16)
            rows_ref[base : base + capacity, chunk * LANES : (chunk + 1) * LANES] = block_ref[
                pl.ds(start, capacity), :
            ]
        if capacity < LANES:
            rows_ref[base + capacity : base + LANES, :] = jnp.zeros(
                (LANES - capacity, width), BF16
            )
    out_ref[...] = dot_tn(pick_ref[...], rows_ref[...]).astype(BF16)


def shape(dims, kind=BF16):
    return jax.ShapeDtypeStruct(dims, kind)


def whole(count):
    return [pl.BlockSpec(memory_space=VMEM)] * count


def scalars():
    return pl.BlockSpec(memory_space=SMEM)


def params(limit):
    return pltpu.CompilerParams(vmem_limit_bytes=limit * MIB)


def cost(flops, bytes_accessed):
    return pl.CostEstimate(flops=flops, bytes_accessed=bytes_accessed, transcendentals=0)


def full(dims):
    return pl.BlockSpec(dims, lambda step: (0,) * len(dims))


def rows_spec(rows, columns):
    return pl.BlockSpec((rows, columns), lambda step: (step, 0))


def swap(value, axis, bit):
    count = lax.axis_size(axis)
    return lax.ppermute(value, axis, [(at, at ^ bit) for at in range(count)])


def take(value, kind, bit):
    if kind == "columns":
        half = value.shape[2] // 2
        parts = value[:, :, :half], value[:, :, half:]
    else:
        pairs = value.reshape((value.shape[0] // 2, 2) + value.shape[1:])
        parts = pairs[:, 0], pairs[:, 1]
    return jnp.where(bit == 0, parts[0], parts[1])


def core_kernel(kinds, bits, scal, keep_ref, got_ref, *refs):
    total_ref, left_ref, right_ref = refs[-3:]
    total = (keep_ref[...].astype(F32) + got_ref[...].astype(F32)).astype(BF16)
    total = total.reshape(total_ref.shape)
    total_ref[...] = total
    half = total.shape[1] // 2
    left_ref[...] = take(total[:, :half], kinds[0], 1 - scal[bits[0]])
    right_ref[...] = take(total[:, half:], kinds[1], 1 - scal[bits[1]])


def stage_kernel(part, kinds, bits, scal, value_ref, got_ref, *refs):
    total_ref, send_ref = refs[-2:]
    value = value_ref[...]
    if part is not None:
        half = value.shape[1] // 2
        value = value[:, part * half : (part + 1) * half]
    mine = take(value, kinds[0], scal[bits[0]]).astype(F32)
    total = (mine + got_ref[...].astype(F32)).astype(BF16)
    total_ref[...] = total
    send_ref[...] = take(total, kinds[1], 1 - scal[bits[1]])


def split_kernel(kinds, bits, scal, *refs):
    left_ref, left_got_ref, right_ref, right_got_ref = refs[:4]
    outs = refs[-(left_got_ref.shape[0]) :]
    left = take(left_ref[...], kinds[0], scal[bits[0]]).astype(F32)
    left = (left + left_got_ref[...].astype(F32)).astype(BF16)
    right = take(right_ref[...], kinds[1], scal[bits[1]]).astype(F32)
    right = (right + right_got_ref[...].astype(F32)).astype(BF16)
    half = left.shape[1]
    owner = scal[OWNER]
    for other, out in enumerate(outs):
        for at in range(len(outs)):

            @pl.when((owner ^ other) == at)
            def _(out=out, at=at):
                out[:half, :] = left[at]
                out[half:, :] = right[at]


def sum_kernel(*refs):
    total = refs[0][...].astype(F32)
    for ref in refs[1:-2]:
        total = total + ref[...].astype(F32)
    refs[-1][...] = total.astype(BF16)


def join_kernel(at, scal, mine_ref, theirs_ref, out_ref):
    mine = mine_ref[...]
    theirs = theirs_ref[...]
    columns = mine.shape[1]
    first = scal[at] == 0
    out_ref[:, :columns] = jnp.where(first, mine, theirs).astype(out_ref.dtype)
    out_ref[:, columns:] = jnp.where(first, theirs, mine).astype(out_ref.dtype)


def local_call(kernel, outs, name, *operands):
    return pl.pallas_call(
        kernel,
        out_shape=[near_shape(*out) for out in outs],
        in_specs=[scalars()] + whole(len(operands) - 1),
        out_specs=whole(len(outs)),
        compiler_params=params(24),
        name=name,
    )(*operands)


def halved(dims, kind):
    if kind == "columns":
        return (dims[0], dims[1], dims[2] // 2)
    return (dims[0] // 2,) + dims[1:]


def reduce_weights(scal, keep, got, geom_count, part_count, early, late):
    bits = []
    bit = 2
    while bit < geom_count:
        bits.append(bit)
        bit *= 2
    columns = [("columns", "geom", bit, GEOM_BITS + at) for at, bit in enumerate(bits)]
    owner = ("owners", "dom", 1, DOM_BIT)
    left = columns + [owner]
    right = [owner] + columns
    rows, width = keep.shape
    dims = (part_count, rows // part_count, width)
    piece = (part_count, rows // part_count // 2, width)
    total, send_left, send_right = local_call(
        functools.partial(core_kernel, (left[0][0], right[0][0]), (left[0][3], right[0][3])),
        [(dims,), (halved(piece, left[0][0]),), (halved(piece, right[0][0]),)],
        "core",
        scal,
        keep,
        got,
    )
    ends = []
    for part, chain, send in ((0, left, send_left), (1, right, send_right)):
        value = total
        now = piece
        for at in range(len(chain) - 1):
            kind, axis, bit, place_at = chain[at]
            follow = chain[at + 1]
            now = halved(now, kind)
            value, send = local_call(
                functools.partial(
                    stage_kernel,
                    part if at == 0 else None,
                    (kind, follow[0]),
                    (place_at, follow[3]),
                ),
                [(now,), (halved(now, follow[0]),)],
                "stage",
                scal,
                value,
                swap(send, axis, bit),
                *early,
            )
        if len(chain) == 1:
            half = rows // part_count // 2
            value = value[:, part * half : (part + 1) * half]
        ends.append((value, swap(send, chain[-1][1], chain[-1][2])))
        end = halved(now, chain[-1][0])
    out = (2 * end[1], end[2])
    owners = part_count // 2
    pieces = local_call(
        functools.partial(split_kernel, (left[-1][0], right[-1][0]), (left[-1][3], right[-1][3])),
        [(out,)] * owners,
        "split",
        scal,
        *ends[0],
        *ends[1],
    )
    got = [swap(pieces[other], "dom", 2 * other) for other in range(owners - 1, 0, -1)]
    total = pl.pallas_call(
        sum_kernel,
        out_shape=near_shape(out),
        in_specs=whole(owners + 1),
        out_specs=pl.BlockSpec(memory_space=VMEM),
        compiler_params=params(24),
        name="sum",
    )(pieces[0], *got, late)
    for place_at, bit in [(GEOM_BITS + at, bit) for at, bit in enumerate(bits)][::-1] + [
        (CORE, 1)
    ]:
        out = (out[0], 2 * out[1])
        last = bit == 1
        total = pl.pallas_call(
            functools.partial(join_kernel, place_at),
            out_shape=shape(out, F32) if last else near_shape(out),
            in_specs=[scalars()] + whole(2),
            out_specs=pl.BlockSpec(memory_space=VMEM),
            compiler_params=params(24),
            name="join",
        )(scal, total, swap(total, "geom", bit))
    return total


def shift(value, steps):
    count = lax.axis_size("dom")
    return lax.ppermute(value, "dom", [(at, (at + steps) % count) for at in range(count)])


def neighbour(value, step):
    count = lax.axis_size("dom")
    return lax.ppermute(
        value, "dom", [(at, at + step) for at in range(count) if 0 <= at + step < count]
    )


def send_order(part_count):
    return sorted(range(1, part_count), key=lambda at: (-min(at, part_count - at), at))


def near_shape(dims, kind=BF16):
    return pltpu.VMEM(dims, kind)


def run_prep(
    fan_in,
    cell_count,
    scal,
    source,
    edges,
    cot_nodes,
    cot_edges,
    w_edge_in,
    w_edge_out,
    w_node_in,
    w_node_out,
    token,
):
    edge_count = edges.shape[0]
    padded = cell_count + 2 * HB
    cells = EDGE_BLOCK // fan_in
    near = pl.BlockSpec(memory_space=VMEM)
    return pl.pallas_call(
        functools.partial(prep_kernel, fan_in, cell_count),
        out_shape=[
            near_shape(like.shape)
            for like in (edges, cot_nodes, cot_edges, w_edge_in, w_edge_out, w_node_in, w_node_out)
        ]
        + [
            near_shape((edge_count, padded + cells)),
            near_shape((padded, edge_count)),
            near_shape(edges.shape, F32),
            near_shape((8, LANES), F32),
        ],
        in_specs=[scalars()] + [pl.BlockSpec(memory_space=pltpu.HBM)] * 8 + [near],
        out_specs=[near] * 11,
        scratch_shapes=[VMEM(source.shape, jnp.int32), pltpu.SemaphoreType.DMA((8,))],
        compiler_params=params(PREP_LIMIT),
        cost_estimate=cost(4 * edge_count * edges.shape[1] ** 2, 20 * MIB),
        name="prep",
    )(
        scal,
        *[
            pltpu.with_memory_space_constraint(value, pltpu.HBM)
            for value in (
                source,
                edges,
                cot_nodes,
                cot_edges,
                w_edge_in,
                w_edge_out,
                w_node_in,
                w_node_out,
            )
        ],
        token,
    )


def run_main(fan_in, scale, scal, nodes, before, after, prepared):
    edge_count, width = prepared[0].shape
    cell_count = nodes.shape[0]
    cells = EDGE_BLOCK // fan_in
    padded = cell_count + 2 * HB
    far = pl.BlockSpec(memory_space=pltpu.HBM)
    near = pl.BlockSpec(memory_space=VMEM)
    by_edge = (edge_count, width)
    by_cell = (cell_count, width)
    weights = (7 * width, width // 2)
    return pl.pallas_call(
        functools.partial(main_kernel, fan_in, scale),
        out_shape=[
            shape(by_edge),
            shape(by_cell),
            near_shape(by_edge),
            near_shape((2 * cell_count, width)),
            near_shape((HB, width)),
            near_shape((HB, width)),
            near_shape(by_cell, F32),
            near_shape(weights),
            near_shape(weights),
        ],
        in_specs=[scalars()] + [near] * 13,
        out_specs=[far, far] + [near] * 7,
        scratch_shapes=[
            VMEM(by_cell, BF16),
            VMEM((padded, width), BF16),
            VMEM((padded + cells, width), BF16),
            VMEM(by_cell, BF16),
            VMEM(by_edge, BF16),
            VMEM(by_edge, BF16),
            VMEM(by_edge, BF16),
            VMEM((edge_count, 1), F32),
            VMEM(by_cell, BF16),
            VMEM(by_edge, BF16),
            VMEM(by_cell, BF16),
            pltpu.SemaphoreType.DMA((2,)),
        ],
        compiler_params=params(MAIN_LIMIT),
        cost_estimate=cost(28 * edge_count * width * width, 16 * MIB),
        name="main",
    )(scal, nodes, before, after, *prepared)


def run_edges(fan_in, cot, summed_grad, pre_grad, w_edge_in, token):
    edge_count, width = cot.shape
    steps = edge_count // EDGE_BLOCK
    return pl.pallas_call(
        functools.partial(edge_kernel, fan_in),
        out_shape=[shape((edge_count, width)), near_shape((8, LANES), F32)],
        in_specs=whole(5),
        out_specs=[pl.BlockSpec(memory_space=pltpu.HBM), pl.BlockSpec(memory_space=VMEM)],
        scratch_shapes=[VMEM((edge_count, width), BF16), pltpu.SemaphoreType.DMA((steps,))],
        compiler_params=params(24),
        cost_estimate=cost(4 * edge_count * width * width, 7 * MIB),
        name="edges",
    )(cot, summed_grad, pre_grad, w_edge_in, token)


def local(
    h_in,
    edge_in,
    new_index,
    source,
    w_edge_in,
    w_edge_out,
    w_node_in,
    w_node_out,
    cot_nodes,
    cot_edges,
):
    _, cell_count, width = h_in.shape
    edge_count = source.shape[1]
    fan_in = edge_count // cell_count
    part_count = lax.axis_size("dom")
    geom_count = lax.axis_size("geom")
    capacity = cell_count // part_count + cell_count // part_count // 2
    chunks = width // LANES
    block_rows = chunks * capacity
    scale = 1.0 / math.sqrt(geom_count * part_count * cell_count * fan_in)
    part = lax.axis_index("dom")
    geom = lax.axis_index("geom")
    scal = [part, geom % 2, part % 2, part // 2]
    geom = geom // 2
    for _ in range(1, geom_count.bit_length() - 1):
        scal.append(geom % 2)
        geom = geom // 2
    scal = jnp.stack(scal).astype(jnp.int32)
    edges = edge_in[0]
    cot = cot_edges[0]

    sends = pl.pallas_call(
        functools.partial(pack_kernel, part_count, capacity),
        out_shape=[shape((block_rows + 16, LANES))] * part_count + [near_shape((8, LANES), F32)],
        in_specs=[scalars()] + whole(2),
        out_specs=whole(part_count + 1),
        compiler_params=params(24),
        name="pack",
    )(scal, h_in[0], new_index)
    prepared = run_prep(
        fan_in,
        cell_count,
        scal,
        source,
        edges,
        cot_nodes[0],
        cot,
        w_edge_in,
        w_edge_out,
        w_node_in,
        w_node_out,
        sends[part_count],
    )
    got = {0: sends[0]}
    for step in send_order(part_count):
        got[step] = shift(sends[step], step)
    nodes, head, tail, ids = pl.pallas_call(
        functools.partial(unpack_kernel, part_count, capacity),
        out_shape=[
            shape((cell_count, width)),
            shape((HB, width)),
            shape((HB, width)),
            shape((part_count * 16, LANES)),
        ],
        in_specs=whole(part_count + 1),
        out_specs=whole(4),
        scratch_shapes=[
            VMEM((part_count * LANES, width), BF16),
            VMEM((cell_count, part_count * LANES), BF16),
        ],
        compiler_params=params(24),
        name="unpack",
    )(*[got[step] for step in range(part_count)], prepared[-1])
    before = neighbour(tail, 1)
    after = neighbour(head, -1)

    (
        edge_new,
        node_new,
        pre_grad,
        summed_grad,
        to_prev,
        to_next,
        node_grad,
        keep,
        send,
    ) = run_main(fan_in, scale, scal, nodes, before, after, prepared[:-1])
    from_next = neighbour(to_prev, -1)
    from_prev = neighbour(to_next, 1)

    returning, token = pl.pallas_call(
        functools.partial(return_kernel, part_count, capacity),
        out_shape=[near_shape((part_count * block_rows, LANES)), near_shape((8, LANES), F32)],
        in_specs=[scalars()] + whole(4),
        out_specs=whole(2),
        compiler_params=params(24),
        name="returning",
    )(scal, node_grad, from_prev, from_next, ids)
    back = lax.all_to_all(
        returning.reshape(part_count, block_rows, LANES), "dom", 0, 0, tiled=True
    ).reshape(part_count * block_rows, LANES)
    grad_edge, edge_token = run_edges(
        fan_in, prepared[2], summed_grad, pre_grad, prepared[3], token
    )
    grad_in, late = pl.pallas_call(
        functools.partial(finish_kernel, part_count, capacity),
        out_shape=[shape((cell_count, width)), near_shape((8, LANES), F32)],
        in_specs=[scalars()] + whole(2),
        out_specs=whole(2),
        scratch_shapes=[
            VMEM((part_count * LANES, width), BF16),
            VMEM((part_count * LANES, cell_count), BF16),
        ],
        compiler_params=params(24),
        name="finish",
    )(scal, new_index, back)
    weight_grads = reduce_weights(
        scal, keep, swap(send, "geom", 1), geom_count, part_count, (token, edge_token), late
    )
    return (node_new[None], edge_new[None], grad_in[None], grad_edge[None], weight_grads)


def solution(mesh):
    return jax.shard_map(
        local,
        mesh=mesh,
        in_specs=(
            P("geom", "dom", None),
            P("geom", "dom", None),
            P("geom", "dom"),
            P("geom", "dom"),
            P(),
            P(),
            P(),
            P(),
            P("geom", "dom", None),
            P("geom", "dom", None),
        ),
        out_specs=(
            P("geom", "dom", None),
            P("geom", "dom", None),
            P("geom", "dom", None),
            P("geom", "dom", None),
            P("dom", None),
        ),
        check_vma=False,
    )
```

profile of v0, /device:TPU:0, one launch (start us, length us, event | category | flops | bytes accessed | tf_op | source)
XLA Modules:
  0.0 129.6 jit_solution(11856671930097238300)
XLA Ops:
  0.8 1.0 copy-done
  1.8 0.7 copy-done.1
  2.5 1.7 %pack.1 = (bf16[400,128]{1,0:T(8,128)(2,1)S(1)}, bf16[400,128]{1,0:T(8,128)(2,1)S(1)}, bf16[400,128]{1,0:T(8,128)(2,1)S(1)}, bf16[400,128]{1,0:T(8,128)(2,1)S(1)...) custom-call(s32[5]{0:T(128)S(1)} %stack.23.scal, ...), custom_call_target="tpu_custom_call" | custom-call | tf_op jit(solution)/shard_map/pack/pallas_call | solution.py:807
  4.2 3.0 %collective-permute-start = (bf16[400,128]{1,0:T(8,128)(2,1)S(1)}, bf16[400,128]{1,0:T(8,128)(2,1)S(1)}, u32[]{:S(2)}, u32[]{:S(2)}) collective-permute-start(bf16[400,128]{1,0:T(8,128)(2,1)S(1)} %get-tuple-element.56), channel_id=1, source_target_pairs={{0,1},{1,2},{2,3},{3,4},{4,5},{5,6},{6,7},{7,0},{8,9},{9,10},{10,1... | collective-permute-start | bytes 307208 | tf_op jit(solution)/shard_map/ppermute | solution.py:642
  7.3 1.6 %collective-permute-start.1 = (bf16[400,128]{1,0:T(8,128)(2,1)S(1)}, bf16[400,128]{1,0:T(8,128)(2,1)S(1)}, u32[]{:S(2)}, u32[]{:S(2)}) collective-permute-start(bf16[400,128]{1,0:T(8,128)(2,1)S(1)} %get-tuple-element.57), channel_id=1, source_target_pairs={{0,2},{1,3},{2,4},{3,5},{4,6},{5,7},{6,0},{7,1},{8,10},{9,11},{10,... | collective-permute-start | bytes 307208 | tf_op jit(solution)/shard_map/ppermute | solution.py:642
  8.8 2.5 %collective-permute-start.2 = (bf16[400,128]{1,0:T(8,128)(2,1)S(1)}, bf16[400,128]{1,0:T(8,128)(2,1)S(1)}, u32[]{:S(2)}, u32[]{:S(2)}) collective-permute-start(bf16[400,128]{1,0:T(8,128)(2,1)S(1)} %get-tuple-element.58), channel_id=1, source_target_pairs={{0,3},{1,4},{2,5},{3,6},{4,7},{5,0},{6,1},{7,2},{8,11},{9,12},{10,... | collective-permute-start | bytes 307208 | tf_op jit(solution)/shard_map/ppermute | solution.py:642
  11.4 1.2 collective-permute-start.3
  12.6 2.6 %collective-permute-start.4 = (bf16[400,128]{1,0:T(8,128)(2,1)S(1)}, bf16[400,128]{1,0:T(8,128)(2,1)S(1)}, u32[]{:S(2)}, u32[]{:S(2)}) collective-permute-start(bf16[400,128]{1,0:T(8,128)(2,1)S(1)} %get-tuple-element.60), channel_id=1, source_target_pairs={{0,5},{1,6},{2,7},{3,0},{4,1},{5,2},{6,3},{7,4},{8,13},{9,14},{10,... | collective-permute-start | bytes 307208 | tf_op jit(solution)/shard_map/ppermute | solution.py:642
  15.2 1.3 %collective-permute-start.5 = (bf16[400,128]{1,0:T(8,128)(2,1)S(1)}, bf16[400,128]{1,0:T(8,128)(2,1)S(1)}, u32[]{:S(2)}, u32[]{:S(2)}) collective-permute-start(bf16[400,128]{1,0:T(8,128)(2,1)S(1)} %get-tuple-element.61), channel_id=1, source_target_pairs={{0,6},{1,7},{2,0},{3,1},{4,2},{5,3},{6,4},{7,5},{8,14},{9,15},{10,... | collective-permute-start | bytes 307208 | tf_op jit(solution)/shard_map/ppermute | solution.py:642
  16.6 1.4 %collective-permute-start.6 = (bf16[400,128]{1,0:T(8,128)(2,1)S(1)}, bf16[400,128]{1,0:T(8,128)(2,1)S(1)}, u32[]{:S(2)}, u32[]{:S(2)}) collective-permute-start(bf16[400,128]{1,0:T(8,128)(2,1)S(1)} %get-tuple-element.62), channel_id=1, source_target_pairs={{0,7},{1,0},{2,1},{3,2},{4,3},{5,4},{6,5},{7,6},{8,15},{9,8},{10,9... | collective-permute-start | bytes 307208 | tf_op jit(solution)/shard_map/ppermute | solution.py:642
  18.0 5.0 %prep.1 = (bf16[2048,512]{1,0:T(8,128)(2,1)S(1)}, bf16[512,512]{1,0:T(8,128)(2,1)S(1)}, bf16[2048,512]{1,0:T(8,128)(2,1)S(1)}, bf16[1536,512]{1,0:T(8,128)(2,1)S...) custom-call(s32[5]{0:T(128)S(1)} %stack.23.scal, ...), custom_call_target="tpu_custom_call" | custom-call | flops 2147483648 | bytes 20971520 | tf_op jit(solution)/shard_map/prep/pallas_call | solution.py:678
  23.1 0.8 unpack.1
  23.9 5.8 %collective-permute-start.7 = (bf16[64,512]{1,0:T(8,128)(2,1)S(1)}, bf16[64,512]{1,0:T(8,128)(2,1)S(1)}, u32[]{:S(2)}, u32[]{:S(2)}) collective-permute-start(bf16[64,512]{1,0:T(8,128)(2,1)S(1)} %get-tuple-element.66), channel_id=1, source_target_pairs={{0,1},{1,2},{2,3},{3,4},{4,5},{5,6},{6,7},{8,9},{9,10},{10,11},{11... | collective-permute-start | bytes 196616 | tf_op jit(solution)/shard_map/ppermute | solution.py:647
  29.7 1.5 %collective-permute-start.8 = (bf16[64,512]{1,0:T(8,128)(2,1)S(1)}, bf16[64,512]{1,0:T(8,128)(2,1)S(1)}, u32[]{:S(2)}, u32[]{:S(2)}) collective-permute-start(bf16[64,512]{1,0:T(8,128)(2,1)S(1)} %get-tuple-element.67), channel_id=1, source_target_pairs={{1,0},{2,1},{3,2},{4,3},{5,4},{6,5},{7,6},{9,8},{10,9},{11,10},{12... | collective-permute-start | bytes 196616 | tf_op jit(solution)/shard_map/ppermute | solution.py:647
  31.6 4.7 %collective-permute-done.8.next_ref = bf16[64,512]{1,0:T(8,128)(2,1)S(1)} collective-permute-done((bf16[64,512]{1,0:T(8,128)(2,1)S(1)}, bf16[64,512]{1,0:T(8,128)(2,1)S(1)}, u32[]{:S(2)}, u32[]{:S(2)}) %collective-permute-start.8) | collective-permute-done | bytes 65568 | tf_op jit(solution)/shard_map/ppermute | solution.py:647
  36.4 21.9 %main.1 = (bf16[2048,512]{1,0:T(8,128)(2,1)}, bf16[512,512]{1,0:T(8,128)(2,1)}, bf16[2048,512]{1,0:T(8,128)(2,1)S(1)}, bf16[1024,512]{1,0:T(8,128)(2,1)S(1)}, bf...) custom-call(s32[5]{0:T(128)S(1)} %stack.23.scal, ...), custom_call_target="tpu_custom_call" | custom-call | flops 15032385536 | bytes 16777216 | tf_op jit(solution)/shard_map/main/pallas_call | solution.py:725
  58.3 1.3 %copy-done.7 = bf16[2048,512]{1,0:T(8,128)(2,1)} copy-done((bf16[2048,512]{1,0:T(8,128)(2,1)}, bf16[2048,512]{1,0:T(8,128)(2,1)S(1)}, u32[]{:S(2)}) %copy-start.7) | copy-done | bytes 2097176
  59.6 5.0 %collective-permute-start.9 = (bf16[64,512]{1,0:T(8,128)(2,1)S(1)}, bf16[64,512]{1,0:T(8,128)(2,1)S(1)}, u32[]{:S(2)}, u32[]{:S(2)}) collective-permute-start(bf16[64,512]{1,0:T(8,128)(2,1)S(1)} %get-tuple-element.81), channel_id=1, source_target_pairs={{0,1},{1,2},{2,3},{3,4},{4,5},{5,6},{6,7},{8,9},{9,10},{10,11},{11... | collective-permute-start | bytes 196616 | tf_op jit(solution)/shard_map/ppermute | solution.py:647
  64.6 1.3 collective-permute-start.10
  65.9 0.7 collective-permute-done.9.from_prev_ref
  66.6 4.4 %collective-permute-done.10.from_next_ref = bf16[64,512]{1,0:T(8,128)(2,1)S(1)} collective-permute-done((bf16[64,512]{1,0:T(8,128)(2,1)S(1)}, bf16[64,512]{1,0:T(8,128)(2,1)S(1)}, u32[]{:S(2)}, u32[]{:S(2)}) %collective-permute-start.10) | collective-permute-done | bytes 65568 | tf_op jit(solution)/shard_map/ppermute | solution.py:647
  71.0 2.2 %returning.1 = (bf16[3072,128]{1,0:T(8,128)(2,1)}, f32[8,128]{1,0:T(8,128)S(1)}) custom-call(s32[5]{0:T(128)S(1)} %stack.23.scal, f32[512,512]{1,0:T(8,128)S(1)} %get-tuple-element.80.node_grad_ref, bf16[64,512]{1,0:T(8,128)(2,1)S(1)} %collective-permute-done.9.from_prev_ref, bf16[64,512]{1,0:T(8,128)(2,1)S(1)} %collective-permute-done.10.from_next_ref, ...), custom_call_target="tpu_custom_call" | custom-call | tf_op jit(solution)/shard_map/returning/pallas_call | solution.py:866
  73.2 6.3 %all-to-all-start = ((bf16[8,384,128]{2,1,0:T(8,128)(2,1)}), bf16[8,384,128]{2,1,0:T(8,128)(2,1)S(1)}, u32[]{:S(2)}, u32[]{:S(2)}) async-start(bf16[8,384,128]{2,1,0:T(8,128)(2,1)} %bitcast.11), calls=%async_computation | async-start | bytes 1572864 | tf_op jit(solution)/shard_map/all_to_all | solution.py:874
  79.5 2.3 %core.1 = (bf16[8,448,256]{2,1,0:T(8,128)(2,1)S(1)}, bf16[8,224,128]{2,1,0:T(8,128)(2,1)S(1)}, bf16[4,224,256]{2,1,0:T(8,128)(2,1)S(1)}) custom-call(s32[5]{0:T(128)S(1)} %stack.23.scal, bf16[3584,256]{1,0:T(8,128)(2,1)S(1)} %get-tuple-element.90.keep_ref, bf16[3584,256]{1,0:T(8,128)(2,1)} %collective-permute-done.11.got_ref), custom_call_target="tpu_custom_call" | custom-call | tf_op jit(solution)/shard_map/core/pallas_call | solution.py:541
  81.8 1.6 %collective-permute-start.12 = (bf16[8,224,128]{2,1,0:T(8,128)(2,1)S(1)}, bf16[8,224,128]{2,1,0:T(8,128)(2,1)S(1)}, u32[]{:S(2)}, u32[]{:S(2)}) collective-permute-start(bf16[8,224,128]{2,1,0:T(8,128)(2,1)S(1)} %get-tuple-element.93), channel_id=1, source_target_pairs={{0,16},{8,24},{16,0},{24,8},{1,17},{9,25},{17,1},{25,9},{2,18},{10... | collective-permute-start | bytes 1376264 | tf_op jit(solution)/shard_map/ppermute | solution.py:471
  83.4 2.0 %collective-permute-start.14 = (bf16[4,224,256]{2,1,0:T(8,128)(2,1)S(1)}, bf16[4,224,256]{2,1,0:T(8,128)(2,1)S(1)}, u32[]{:S(2)}, u32[]{:S(2)}) collective-permute-start(bf16[4,224,256]{2,1,0:T(8,128)(2,1)S(1)} %get-tuple-element.97), channel_id=1, source_target_pairs={{0,1},{1,0},{2,3},{3,2},{4,5},{5,4},{6,7},{7,6},{8,9},{9,8},{10,11... | collective-permute-start | bytes 1376264 | tf_op jit(solution)/shard_map/ppermute | solution.py:471
  85.4 1.6 %copy-done.8 = bf16[2048,512]{1,0:T(8,128)(2,1)S(1)} copy-done((bf16[2048,512]{1,0:T(8,128)(2,1)S(1)}, bf16[2048,512]{1,0:T(8,128)(2,1)}, u32[]{:S(2)}) %copy-start.8) | copy-done | bytes 2097176
  87.0 1.2 copy-done.10
  88.2 2.6 %edges.1 = (bf16[2048,512]{1,0:T(8,128)(2,1)}, f32[8,128]{1,0:T(8,128)S(1)}) custom-call(bf16[2048,512]{1,0:T(8,128)(2,1)S(1)} %copy-done.4, bf16[1024,512]{1,0:T(8,128)(2,1)S(1)} %copy-done.10, bf16[2048,512]{1,0:T(8,128)(2,1)S(1)} %copy-done.8, bf16[1536,512]{1,0:T(8,128)(2,1)S(1)} %copy-done.6, f32[8,128]{1,0:T(8,128)S(1)} %get-tuple-element.88._.refs_0_), custom_call_target="tpu_custom_call" | custom-call | flops 2147483648 | bytes 7340032 | tf_op jit(solution)/shard_map/edges/pallas_call | solution.py:763
  90.8 2.9 %collective-permute-done.12.got_ref = bf16[8,224,128]{2,1,0:T(8,128)(2,1)S(1)} collective-permute-done((bf16[8,224,128]{2,1,0:T(8,128)(2,1)S(1)}, bf16[8,224,128]{2,1,0:T(8,128)(2,1)S(1)}, u32[]{:S(2)}, u32[]{:S(2)}) %collective-permute-start.12) | collective-permute-done | bytes 458784 | tf_op jit(solution)/shard_map/ppermute | solution.py:471
  93.7 0.7 stage.2
  94.5 1.8 %collective-permute-start.13 = (bf16[4,224,128]{2,1,0:T(8,128)(2,1)S(1)}, bf16[4,224,128]{2,1,0:T(8,128)(2,1)S(1)}, u32[]{:S(2)}, u32[]{:S(2)}) collective-permute-start(bf16[4,224,128]{2,1,0:T(8,128)(2,1)S(1)} %get-tuple-element.96), channel_id=1, source_target_pairs={{0,1},{1,0},{2,3},{3,2},{4,5},{5,4},{6,7},{7,6},{8,9},{9,8},{10,11... | collective-permute-start | bytes 688136 | tf_op jit(solution)/shard_map/ppermute | solution.py:471
  96.3 4.6 %collective-permute-done.14.got_ref = bf16[4,224,256]{2,1,0:T(8,128)(2,1)S(1)} collective-permute-done((bf16[4,224,256]{2,1,0:T(8,128)(2,1)S(1)}, bf16[4,224,256]{2,1,0:T(8,128)(2,1)S(1)}, u32[]{:S(2)}, u32[]{:S(2)}) %collective-permute-start.14) | collective-permute-done | bytes 458784 | tf_op jit(solution)/shard_map/ppermute | solution.py:471
  100.8 0.7 stage.3
  101.6 1.8 %collective-permute-start.15 = (bf16[4,224,128]{2,1,0:T(8,128)(2,1)S(1)}, bf16[4,224,128]{2,1,0:T(8,128)(2,1)S(1)}, u32[]{:S(2)}, u32[]{:S(2)}) collective-permute-start(bf16[4,224,128]{2,1,0:T(8,128)(2,1)S(1)} %get-tuple-element.99), channel_id=1, source_target_pairs={{0,16},{8,24},{16,0},{24,8},{1,17},{9,25},{17,1},{25,9},{2,18},{10... | collective-permute-start | bytes 688136 | tf_op jit(solution)/shard_map/ppermute | solution.py:471
  103.4 2.0 %collective-permute-done.13.refs_1_ = bf16[4,224,128]{2,1,0:T(8,128)(2,1)S(1)} collective-permute-done((bf16[4,224,128]{2,1,0:T(8,128)(2,1)S(1)}, bf16[4,224,128]{2,1,0:T(8,128)(2,1)S(1)}, u32[]{:S(2)}, u32[]{:S(2)}) %collective-permute-start.13) | collective-permute-done | bytes 229408 | tf_op jit(solution)/shard_map/ppermute | solution.py:471
  105.4 3.1 %collective-permute-done.15.refs_3_ = bf16[4,224,128]{2,1,0:T(8,128)(2,1)S(1)} collective-permute-done((bf16[4,224,128]{2,1,0:T(8,128)(2,1)S(1)}, bf16[4,224,128]{2,1,0:T(8,128)(2,1)S(1)}, u32[]{:S(2)}, u32[]{:S(2)}) %collective-permute-start.15) | collective-permute-done | bytes 229408 | tf_op jit(solution)/shard_map/ppermute | solution.py:471
  108.5 0.9 split.1
  109.5 3.1 %collective-permute-start.16 = (bf16[448,128]{1,0:T(8,128)(2,1)S(1)}, bf16[448,128]{1,0:T(8,128)(2,1)S(1)}, u32[]{:S(2)}, u32[]{:S(2)}) collective-permute-start(bf16[448,128]{1,0:T(8,128)(2,1)S(1)} %get-tuple-element.101), channel_id=1, source_target_pairs={{0,6},{1,7},{2,4},{3,5},{4,2},{5,3},{6,0},{7,1},{8,14},{9,15},{10,... | collective-permute-start | bytes 344072 | tf_op jit(solution)/shard_map/ppermute | solution.py:471
  112.6 1.3 %collective-permute-start.18 = (bf16[448,128]{1,0:T(8,128)(2,1)S(1)}, bf16[448,128]{1,0:T(8,128)(2,1)S(1)}, u32[]{:S(2)}, u32[]{:S(2)}) collective-permute-start(bf16[448,128]{1,0:T(8,128)(2,1)S(1)} %get-tuple-element.103), channel_id=1, source_target_pairs={{0,2},{1,3},{2,0},{3,1},{4,6},{5,7},{6,4},{7,5},{8,10},{9,11},{10,... | collective-permute-start | bytes 344072 | tf_op jit(solution)/shard_map/ppermute | solution.py:471
  113.9 2.3 %finish.1 = (bf16[512,512]{1,0:T(8,128)(2,1)}, f32[8,128]{1,0:T(8,128)S(1)}) custom-call(s32[5]{0:T(128)S(1)} %stack.23.scal, s32[1,512]{1,0:T(1,128)S(1)} %copy-done.2, bf16[3072,128]{1,0:T(8,128)(2,1)S(1)} %bitcast.15), custom_call_target="tpu_custom_call" | custom-call | tf_op jit(solution)/shard_map/finish/pallas_call | solution.py:880
  116.3 1.1 collective-permute-done.16.refs_1_
  117.4 3.6 %collective-permute-done.17.refs_2_ = bf16[448,128]{1,0:T(8,128)(2,1)S(1)} collective-permute-done((bf16[448,128]{1,0:T(8,128)(2,1)S(1)}, bf16[448,128]{1,0:T(8,128)(2,1)S(1)}, u32[]{:S(2)}, u32[]{:S(2)}) %collective-permute-start.17) | collective-permute-done | bytes 114720 | tf_op jit(solution)/shard_map/ppermute | solution.py:471
  121.1 1.1 collective-permute-start.19
  122.2 3.7 %collective-permute-done.19.theirs_ref = bf16[448,128]{1,0:T(8,128)(2,1)S(1)} collective-permute-done((bf16[448,128]{1,0:T(8,128)(2,1)S(1)}, bf16[448,128]{1,0:T(8,128)(2,1)S(1)}, u32[]{:S(2)}, u32[]{:S(2)}) %collective-permute-start.19) | collective-permute-done | bytes 114720 | tf_op jit(solution)/shard_map/ppermute | solution.py:471
  125.9 0.6 join.2.mine_ref
  126.6 1.5 %collective-permute-done.20.theirs_ref = bf16[448,256]{1,0:T(8,128)(2,1)S(1)} collective-permute-done((bf16[448,256]{1,0:T(8,128)(2,1)S(1)}, bf16[448,256]{1,0:T(8,128)(2,1)S(1)}, u32[]{:S(2)}, u32[]{:S(2)}) %collective-permute-start.20) | collective-permute-done | bytes 229408 | tf_op jit(solution)/shard_map/ppermute | solution.py:471
  128.1 1.6 %join.3 = f32[448,512]{1,0:T(8,128)} custom-call(s32[5]{0:T(128)S(1)} %stack.23.scal, bf16[448,256]{1,0:T(8,128)(2,1)S(1)} %join.2.mine_ref, bf16[448,256]{1,0:T(8,128)(2,1)S(1)} %collective-permute-done.20.theirs_ref), custom_call_target="tpu_custom_call" | custom-call | tf_op jit(solution)/shard_map/join/pallas_call | solution.py:629
  (33 shorter events, 0.7 us)
Async XLA Ops:
  0.8 1.0 copy-start
  1.8 0.7 copy-start.1
  4.2 11.0 %collective-permute-start = (bf16[400,128]{1,0:T(8,128)(2,1)S(1)}, bf16[400,128]{1,0:T(8,128)(2,1)S(1)}, u32[]{:S(2)}, u32[]{:S(2)}) collective-permute-start(bf16[400,128]{1,0:T(8,128)(2,1)S(1)} %get-tuple-element.56), channel_id=1, source_target_pairs={{0,1},{1,2},{2,3},{3,4},{4,5},{5,6},{6,7},{7,0},{8,9},{9,10},{10,1... | collective-permute-start | bytes 307208 | tf_op jit(solution)/shard_map/ppermute | solution.py:642
  7.3 9.3 %collective-permute-start.1 = (bf16[400,128]{1,0:T(8,128)(2,1)S(1)}, bf16[400,128]{1,0:T(8,128)(2,1)S(1)}, u32[]{:S(2)}, u32[]{:S(2)}) collective-permute-start(bf16[400,128]{1,0:T(8,128)(2,1)S(1)} %get-tuple-element.57), channel_id=1, source_target_pairs={{0,2},{1,3},{2,4},{3,5},{4,6},{5,7},{6,0},{7,1},{8,10},{9,11},{10,... | collective-permute-start | bytes 307208 | tf_op jit(solution)/shard_map/ppermute | solution.py:642
  8.8 14.2 %collective-permute-start.2 = (bf16[400,128]{1,0:T(8,128)(2,1)S(1)}, bf16[400,128]{1,0:T(8,128)(2,1)S(1)}, u32[]{:S(2)}, u32[]{:S(2)}) collective-permute-start(bf16[400,128]{1,0:T(8,128)(2,1)S(1)} %get-tuple-element.58), channel_id=1, source_target_pairs={{0,3},{1,4},{2,5},{3,6},{4,7},{5,0},{6,1},{7,2},{8,11},{9,12},{10,... | collective-permute-start | bytes 307208 | tf_op jit(solution)/shard_map/ppermute | solution.py:642
  11.4 11.7 %collective-permute-start.3 = (bf16[400,128]{1,0:T(8,128)(2,1)S(1)}, bf16[400,128]{1,0:T(8,128)(2,1)S(1)}, u32[]{:S(2)}, u32[]{:S(2)}) collective-permute-start(bf16[400,128]{1,0:T(8,128)(2,1)S(1)} %get-tuple-element.59), channel_id=1, source_target_pairs={{0,4},{1,5},{2,6},{3,7},{4,0},{5,1},{6,2},{7,3},{8,12},{9,13},{10,... | collective-permute-start | bytes 307208 | tf_op jit(solution)/shard_map/ppermute | solution.py:642
  12.6 10.5 %collective-permute-start.4 = (bf16[400,128]{1,0:T(8,128)(2,1)S(1)}, bf16[400,128]{1,0:T(8,128)(2,1)S(1)}, u32[]{:S(2)}, u32[]{:S(2)}) collective-permute-start(bf16[400,128]{1,0:T(8,128)(2,1)S(1)} %get-tuple-element.60), channel_id=1, source_target_pairs={{0,5},{1,6},{2,7},{3,0},{4,1},{5,2},{6,3},{7,4},{8,13},{9,14},{10,... | collective-permute-start | bytes 307208 | tf_op jit(solution)/shard_map/ppermute | solution.py:642
  15.2 7.8 %collective-permute-start.5 = (bf16[400,128]{1,0:T(8,128)(2,1)S(1)}, bf16[400,128]{1,0:T(8,128)(2,1)S(1)}, u32[]{:S(2)}, u32[]{:S(2)}) collective-permute-start(bf16[400,128]{1,0:T(8,128)(2,1)S(1)} %get-tuple-element.61), channel_id=1, source_target_pairs={{0,6},{1,7},{2,0},{3,1},{4,2},{5,3},{6,4},{7,5},{8,14},{9,15},{10,... | collective-permute-start | bytes 307208 | tf_op jit(solution)/shard_map/ppermute | solution.py:642
  16.6 6.5 %collective-permute-start.6 = (bf16[400,128]{1,0:T(8,128)(2,1)S(1)}, bf16[400,128]{1,0:T(8,128)(2,1)S(1)}, u32[]{:S(2)}, u32[]{:S(2)}) collective-permute-start(bf16[400,128]{1,0:T(8,128)(2,1)S(1)} %get-tuple-element.62), channel_id=1, source_target_pairs={{0,7},{1,0},{2,1},{3,2},{4,3},{5,4},{6,5},{7,6},{8,15},{9,8},{10,9... | collective-permute-start | bytes 307208 | tf_op jit(solution)/shard_map/ppermute | solution.py:642
  23.0 35.2 %copy-start.3 = (bf16[2048,512]{1,0:T(8,128)(2,1)}, bf16[2048,512]{1,0:T(8,128)(2,1)S(1)}, u32[]{:S(2)}) copy-start(bf16[2048,512]{1,0:T(8,128)(2,1)S(1)} %get-tuple-element.70.cot_edges_ref.cot_ref) | copy-start | bytes 6291460
  23.0 35.2 %copy-start.5 = (bf16[1536,512]{1,0:T(8,128)(2,1)}, bf16[1536,512]{1,0:T(8,128)(2,1)S(1)}, u32[]{:S(2)}) copy-start(bf16[1536,512]{1,0:T(8,128)(2,1)S(1)} %get-tuple-element.71.w_edge_in_ref) | copy-start | bytes 4718596
  23.9 7.7 %collective-permute-start.7 = (bf16[64,512]{1,0:T(8,128)(2,1)S(1)}, bf16[64,512]{1,0:T(8,128)(2,1)S(1)}, u32[]{:S(2)}, u32[]{:S(2)}) collective-permute-start(bf16[64,512]{1,0:T(8,128)(2,1)S(1)} %get-tuple-element.66), channel_id=1, source_target_pairs={{0,1},{1,2},{2,3},{3,4},{4,5},{5,6},{6,7},{8,9},{9,10},{10,11},{11... | collective-permute-start | bytes 196616 | tf_op jit(solution)/shard_map/ppermute | solution.py:647
  29.7 6.6 %collective-permute-start.8 = (bf16[64,512]{1,0:T(8,128)(2,1)S(1)}, bf16[64,512]{1,0:T(8,128)(2,1)S(1)}, u32[]{:S(2)}, u32[]{:S(2)}) collective-permute-start(bf16[64,512]{1,0:T(8,128)(2,1)S(1)} %get-tuple-element.67), channel_id=1, source_target_pairs={{1,0},{2,1},{3,2},{4,3},{5,4},{6,5},{7,6},{9,8},{10,9},{11,10},{12... | collective-permute-start | bytes 196616 | tf_op jit(solution)/shard_map/ppermute | solution.py:647
  58.3 1.4 %copy-start.7 = (bf16[2048,512]{1,0:T(8,128)(2,1)}, bf16[2048,512]{1,0:T(8,128)(2,1)S(1)}, u32[]{:S(2)}) copy-start(bf16[2048,512]{1,0:T(8,128)(2,1)S(1)} %get-tuple-element.87.pre_grad_ref) | copy-start | bytes 6291460
  59.6 13.6 %copy-start.9 = (bf16[1024,512]{1,0:T(8,128)(2,1)}, bf16[1024,512]{1,0:T(8,128)(2,1)S(1)}, u32[]{:S(2)}) copy-start(bf16[1024,512]{1,0:T(8,128)(2,1)S(1)} %get-tuple-element.86.summed_grad_ref) | copy-start | bytes 3145732
  59.6 19.9 %collective-permute-start.11 = (bf16[3584,256]{1,0:T(8,128)(2,1)}, bf16[3584,256]{1,0:T(8,128)(2,1)}, u32[]{:S(2)}, u32[]{:S(2)}) collective-permute-start(bf16[3584,256]{1,0:T(8,128)(2,1)} %get-tuple-element.91), channel_id=1, source_target_pairs={{0,8},{8,0},{16,24},{24,16},{1,9},{9,1},{17,25},{25,17},{2,10},{10... | collective-permute-start | bytes 5505032 | tf_op jit(solution)/shard_map/ppermute | solution.py:471
  59.6 7.0 %collective-permute-start.9 = (bf16[64,512]{1,0:T(8,128)(2,1)S(1)}, bf16[64,512]{1,0:T(8,128)(2,1)S(1)}, u32[]{:S(2)}, u32[]{:S(2)}) collective-permute-start(bf16[64,512]{1,0:T(8,128)(2,1)S(1)} %get-tuple-element.81), channel_id=1, source_target_pairs={{0,1},{1,2},{2,3},{3,4},{4,5},{5,6},{6,7},{8,9},{9,10},{10,11},{11... | collective-permute-start | bytes 196616 | tf_op jit(solution)/shard_map/ppermute | solution.py:647
  64.6 6.4 %collective-permute-start.10 = (bf16[64,512]{1,0:T(8,128)(2,1)S(1)}, bf16[64,512]{1,0:T(8,128)(2,1)S(1)}, u32[]{:S(2)}, u32[]{:S(2)}) collective-permute-start(bf16[64,512]{1,0:T(8,128)(2,1)S(1)} %get-tuple-element.82), channel_id=1, source_target_pairs={{1,0},{2,1},{3,2},{4,3},{5,4},{6,5},{7,6},{9,8},{10,9},{11,10},{12... | collective-permute-start | bytes 196616 | tf_op jit(solution)/shard_map/ppermute | solution.py:647
  73.2 40.7 %all-to-all-start = ((bf16[8,384,128]{2,1,0:T(8,128)(2,1)}), bf16[8,384,128]{2,1,0:T(8,128)(2,1)S(1)}, u32[]{:S(2)}, u32[]{:S(2)}) async-start(bf16[8,384,128]{2,1,0:T(8,128)(2,1)} %bitcast.11), calls=%async_computation | async-start | bytes 1572864 | tf_op jit(solution)/shard_map/all_to_all | solution.py:874
  79.5 5.8 %copy-start.4 = (bf16[2048,512]{1,0:T(8,128)(2,1)S(1)}, bf16[2048,512]{1,0:T(8,128)(2,1)}, u32[]{:S(2)}) copy-start(bf16[2048,512]{1,0:T(8,128)(2,1)} %copy-done.3) | copy-start | bytes 6291460
  79.5 5.8 %copy-start.6 = (bf16[1536,512]{1,0:T(8,128)(2,1)S(1)}, bf16[1536,512]{1,0:T(8,128)(2,1)}, u32[]{:S(2)}) copy-start(bf16[1536,512]{1,0:T(8,128)(2,1)} %copy-done.5) | copy-start | bytes 4718596
  81.8 11.9 %collective-permute-start.12 = (bf16[8,224,128]{2,1,0:T(8,128)(2,1)S(1)}, bf16[8,224,128]{2,1,0:T(8,128)(2,1)S(1)}, u32[]{:S(2)}, u32[]{:S(2)}) collective-permute-start(bf16[8,224,128]{2,1,0:T(8,128)(2,1)S(1)} %get-tuple-element.93), channel_id=1, source_target_pairs={{0,16},{8,24},{16,0},{24,8},{1,17},{9,25},{17,1},{25,9},{2,18},{10... | collective-permute-start | bytes 1376264 | tf_op jit(solution)/shard_map/ppermute | solution.py:471
  83.4 17.5 %collective-permute-start.14 = (bf16[4,224,256]{2,1,0:T(8,128)(2,1)S(1)}, bf16[4,224,256]{2,1,0:T(8,128)(2,1)S(1)}, u32[]{:S(2)}, u32[]{:S(2)}) collective-permute-start(bf16[4,224,256]{2,1,0:T(8,128)(2,1)S(1)} %get-tuple-element.97), channel_id=1, source_target_pairs={{0,1},{1,0},{2,3},{3,2},{4,5},{5,4},{6,7},{7,6},{8,9},{9,8},{10,11... | collective-permute-start | bytes 1376264 | tf_op jit(solution)/shard_map/ppermute | solution.py:471
  85.4 1.6 %copy-start.8 = (bf16[2048,512]{1,0:T(8,128)(2,1)S(1)}, bf16[2048,512]{1,0:T(8,128)(2,1)}, u32[]{:S(2)}) copy-start(bf16[2048,512]{1,0:T(8,128)(2,1)} %copy-done.7) | copy-start | bytes 6291460
  87.0 1.2 copy-start.10
  94.5 19.4 %copy-start.2 = (s32[1,512]{1,0:T(1,128)S(1)}, s32[1,512]{1,0:T(1,128)}, u32[]{:S(2)}) copy-start(s32[1,512]{1,0:T(1,128)} %index_ref.3) | copy-start | bytes 6148
  94.5 10.9 %collective-permute-start.13 = (bf16[4,224,128]{2,1,0:T(8,128)(2,1)S(1)}, bf16[4,224,128]{2,1,0:T(8,128)(2,1)S(1)}, u32[]{:S(2)}, u32[]{:S(2)}) collective-permute-start(bf16[4,224,128]{2,1,0:T(8,128)(2,1)S(1)} %get-tuple-element.96), channel_id=1, source_target_pairs={{0,1},{1,0},{2,3},{3,2},{4,5},{5,4},{6,7},{7,6},{8,9},{9,8},{10,11... | collective-permute-start | bytes 688136 | tf_op jit(solution)/shard_map/ppermute | solution.py:471
  101.6 7.0 %collective-permute-start.15 = (bf16[4,224,128]{2,1,0:T(8,128)(2,1)S(1)}, bf16[4,224,128]{2,1,0:T(8,128)(2,1)S(1)}, u32[]{:S(2)}, u32[]{:S(2)}) collective-permute-start(bf16[4,224,128]{2,1,0:T(8,128)(2,1)S(1)} %get-tuple-element.99), channel_id=1, source_target_pairs={{0,16},{8,24},{16,0},{24,8},{1,17},{9,25},{17,1},{25,9},{2,18},{10... | collective-permute-start | bytes 688136 | tf_op jit(solution)/shard_map/ppermute | solution.py:471
  109.5 7.9 %collective-permute-start.16 = (bf16[448,128]{1,0:T(8,128)(2,1)S(1)}, bf16[448,128]{1,0:T(8,128)(2,1)S(1)}, u32[]{:S(2)}, u32[]{:S(2)}) collective-permute-start(bf16[448,128]{1,0:T(8,128)(2,1)S(1)} %get-tuple-element.101), channel_id=1, source_target_pairs={{0,6},{1,7},{2,4},{3,5},{4,2},{5,3},{6,0},{7,1},{8,14},{9,15},{10,... | collective-permute-start | bytes 344072 | tf_op jit(solution)/shard_map/ppermute | solution.py:471
  112.6 8.4 %collective-permute-start.17 = (bf16[448,128]{1,0:T(8,128)(2,1)S(1)}, bf16[448,128]{1,0:T(8,128)(2,1)S(1)}, u32[]{:S(2)}, u32[]{:S(2)}) collective-permute-start(bf16[448,128]{1,0:T(8,128)(2,1)S(1)} %get-tuple-element.102), channel_id=1, source_target_pairs={{0,4},{1,5},{2,6},{3,7},{4,0},{5,1},{6,2},{7,3},{8,12},{9,13},{10,... | collective-permute-start | bytes 344072 | tf_op jit(solution)/shard_map/ppermute | solution.py:471
  112.6 8.4 %collective-permute-start.18 = (bf16[448,128]{1,0:T(8,128)(2,1)S(1)}, bf16[448,128]{1,0:T(8,128)(2,1)S(1)}, u32[]{:S(2)}, u32[]{:S(2)}) collective-permute-start(bf16[448,128]{1,0:T(8,128)(2,1)S(1)} %get-tuple-element.103), channel_id=1, source_target_pairs={{0,2},{1,3},{2,0},{3,1},{4,6},{5,7},{6,4},{7,5},{8,10},{9,11},{10,... | collective-permute-start | bytes 344072 | tf_op jit(solution)/shard_map/ppermute | solution.py:471
  121.1 4.9 %collective-permute-start.19 = (bf16[448,128]{1,0:T(8,128)(2,1)S(1)}, bf16[448,128]{1,0:T(8,128)(2,1)S(1)}, u32[]{:S(2)}, u32[]{:S(2)}) collective-permute-start(bf16[448,128]{1,0:T(8,128)(2,1)S(1)} %sum.1.mine_ref), channel_id=1, source_target_pairs={{0,16},{8,24},{16,0},{24,8},{1,17},{9,25},{17,1},{25,9},{2,18},{10... | collective-permute-start | bytes 344072 | tf_op jit(solution)/shard_map/ppermute | solution.py:471
  126.5 1.6 %collective-permute-start.20 = (bf16[448,256]{1,0:T(8,128)(2,1)S(1)}, bf16[448,256]{1,0:T(8,128)(2,1)S(1)}, u32[]{:S(2)}, u32[]{:S(2)}) collective-permute-start(bf16[448,256]{1,0:T(8,128)(2,1)S(1)} %join.2.mine_ref), channel_id=1, source_target_pairs={{0,8},{8,0},{16,24},{24,16},{1,9},{9,1},{17,25},{25,17},{2,10},{10... | collective-permute-start | bytes 688136 | tf_op jit(solution)/shard_map/ppermute | solution.py:471
where the time goes:
time: 130 us
  starting transfers between devices  46.5 us (36%)
  Pallas kernels  43.4 us (33%)
  waiting for transfers between devices  32.8 us (25%)
  local copies, waits for them, and re-layouts  6 us (5%)
    ppermute x10, waiting for transfers between devices, swap(): return lax.ppermute(value, axis, [(at, at ^ bit) for at in range(count)])  22.5 us
    pallas_call x1, Pallas kernels, run_main(): pl.pallas_call(functools.partial(main_kernel, fan_in, scale), out_shape=[...  21.9 us
    ppermute x7, starting transfers between devices, shift(): lax.ppermute(value, 'dom', [(at, (at + steps) % count) for at in range(co...  13.8 us
    ppermute x4, starting transfers between devices, neighbour(): lax.ppermute(value, 'dom', [(at, at + step) for at in range(count) if 0 <...  13.6 us
    ppermute x10, starting transfers between devices, swap(): return lax.ppermute(value, axis, [(at, at ^ bit) for at in range(count)])  12.9 us
    ppermute x4, waiting for transfers between devices, neighbour(): lax.ppermute(value, 'dom', [(at, at + step) for at in range(count) if 0 <...  10.2 us
    all_to_all x1, starting transfers between devices, local(): lax.all_to_all(returning.reshape(part_count, block_rows, LANES), 'dom', 0...  6.3 us
    unnamed x22, local copies, waits for them, and re-layouts  5.92 us
  transfers between devices with their start and end apart: 22, of which 12 were waited for; matrix products, arithmetic and copies ran while one was open for 0% of the time, Pallas kernels for 13%

commit v1 on v0

--- a/solution.py
+++ b/solution.py
@@ -13,6 +13,7 @@
 EDGE_BLOCK = 512
 MIB = 1024 * 1024
 MAIN_LIMIT = 25
+FIRST, SECOND = 3, 7
 PREP_LIMIT = 20
 PART, CORE, DOM_BIT, OWNER, GEOM_BITS = range(5)
 F32 = jnp.float32
@@ -102,7 +103,7 @@
 
 def unpack_kernel(part_count, capacity, *refs):
     blocks = refs[:part_count]
-    _, nodes_ref, head_ref, tail_ref, ids_ref, rows_ref, hot_ref = refs[part_count:]
+    scal, _, nodes_ref, low_ref, high_ref, ids_ref, rows_ref, hot_ref = refs[part_count:]
     cell_count, width = nodes_ref.shape
     chunks = width // LANES
     for step in range(part_count):
@@ -120,8 +121,11 @@
             )
     nodes = dot_nn(hot_ref[...], rows_ref[...]).astype(BF16)
     nodes_ref[...] = nodes
-    head_ref[...] = nodes[:HB]
-    tail_ref[...] = nodes[cell_count - HB :]
+    odd = scal[DOM_BIT] == 1
+    head = nodes[:HB]
+    tail = nodes[cell_count - HB :]
+    low_ref[...] = jnp.where(odd, head, tail)
+    high_ref[...] = jnp.where(odd, tail, head)
 
 
 def prep_kernel(
@@ -208,8 +212,8 @@
     scale,
     scal,
     nodes_ref,
-    prev_ref,
-    next_ref,
+    low_ref,
+    high_ref,
     edges_ref,
     cot_nodes_ref,
     cot_edges_ref,
@@ -222,13 +226,15 @@
     pre_ref,
     edge_new_hbm,
     node_new_hbm,
+    pre_grad_hbm,
+    summed_grad_hbm,
+    sent_ref,
+    received_ref,
+    base_ref,
+    keep_ref,
+    send_ref,
     pre_grad_ref,
     summed_grad_ref,
-    to_prev_ref,
-    to_next_ref,
-    node_grad_ref,
-    keep_ref,
-    send_ref,
     node_new_ref,
     cells_ref,
     table_ref,
@@ -239,7 +245,6 @@
     inverse_ref,
     summed_ref,
     post_grad_ref,
-    received_ref,
     out_sems,
 ):
     cell_count, width = nodes_ref.shape
@@ -250,9 +255,12 @@
     half = width // 2
     inner = slice(HB, HB + cell_count)
 
-    cells_ref[:HB, :] = prev_ref[...]
+    odd = scal[DOM_BIT] == 1
+    low = low_ref[...]
+    high = high_ref[...]
+    cells_ref[:HB, :] = jnp.where(odd, low, high)
     cells_ref[inner, :] = nodes_ref[...]
-    cells_ref[HB + cell_count :, :] = next_ref[...]
+    cells_ref[HB + cell_count :, :] = jnp.where(odd, high, low)
     table_ref[:padded, :] = dot_nn(cells_ref[...], w_edge_in_ref[width : 2 * width, :]).astype(BF16)
     recv_ref[...] = dot_nn(nodes_ref[...], w_edge_in_ref[2 * width :, :]).astype(BF16)
     collect = hot(iota((cells, EDGE_BLOCK), 0) == iota((cells, EDGE_BLOCK), 1) // fan_in)
@@ -275,7 +283,7 @@
         summed_ref[spot, :] = dot_nn(collect, edge_new).astype(BF16)
         return carry
 
-    lax.fori_loop(0, steps, forward, 0)
+    lax.fori_loop(0, steps, forward, 0, unroll=True)
     edge_store = pltpu.make_async_copy(post_grad_ref, edge_new_hbm, out_sems.at[0])
     edge_store.start()
     nodes = nodes_ref[...]
@@ -298,7 +306,9 @@
         at = slice(block * cells, (block + 1) * cells)
         summed_grad_ref[2 * block * cells : (2 * block + 1) * cells, :] = high[at]
         summed_grad_ref[(2 * block + 1) * cells : 2 * (block + 1) * cells, :] = low[at]
-    node_grad_ref[...] = upstream + dot_nt(node_pre_grad, w_node_in_ref[:width, :])
+    summed_store = pltpu.make_async_copy(summed_grad_ref, summed_grad_hbm, out_sems.at[2])
+    summed_store.start()
+    base_ref[...] = upstream + dot_nt(node_pre_grad, w_node_in_ref[:width, :])
     member = iota((EDGE_BLOCK, 2 * cells), 1)
     owner = iota((EDGE_BLOCK, 2 * cells), 0) // fan_in
     spread = hot((owner == member) | (owner + cells == member))
@@ -322,7 +332,9 @@
         received_ref[spot, :] = dot_nn(collect, pre_grad).astype(BF16)
         return carry
 
-    lax.fori_loop(0, steps, backward, 0)
+    lax.fori_loop(0, steps, backward, 0, unroll=True)
+    pre_store = pltpu.make_async_copy(pre_grad_ref, pre_grad_hbm, out_sems.at[3])
+    pre_store.start()
     first = scal[CORE] == 0
 
     def put(place_at, value):
@@ -334,14 +346,7 @@
         send_ref[rows, :] = jnp.where(first, right, left)
 
     sent = dot_nn(scatter_ref[...], pre_grad_ref[...]).astype(BF16)
-    sender = dot_nt(sent, w_edge_in_ref[width : 2 * width, :])
-    to_prev_ref[...] = sender[:HB].astype(BF16)
-    to_next_ref[...] = sender[HB + cell_count :].astype(BF16)
-    node_grad_ref[...] = (
-        node_grad_ref[...]
-        + dot_nt(received_ref[...], w_edge_in_ref[2 * width :, :])
-        + sender[inner]
-    )
+    sent_ref[...] = sent
     put(0, dot_tn(edges_ref[...], pre_grad_ref[...]))
     put(1, dot_tn(cells_ref[...], sent))
     put(2, dot_tn(nodes, received_ref[...]))
@@ -350,86 +355,142 @@
     put(5, dot_tn(summed, node_pre_grad))
     put(6, dot_tn(node_hidden, node_post_grad))
     node_store.wait()
+    summed_store.wait()
+    pre_store.wait()
+
+
+def cell_kernel(
+    scal,
+    sent_ref,
+    received_ref,
+    base_ref,
+    w_edge_in_ref,
+    low_ref,
+    high_ref,
+    node_grad_ref,
+    rim_ref,
+):
+    cell_count, width = received_ref.shape
+    sender = dot_nt(sent_ref[...], w_edge_in_ref[width : 2 * width, :])
+    odd = scal[DOM_BIT] == 1
+    to_prev = sender[:HB].astype(BF16)
+    to_next = sender[HB + cell_count :].astype(BF16)
+    low_ref[...] = jnp.where(odd, to_prev, to_next)
+    high_ref[...] = jnp.where(odd, to_next, to_prev)
+    node_grad = (
+        base_ref[...]
+        + dot_nt(received_ref[...], w_edge_in_ref[2 * width :, :])
+        + sender[HB : HB + cell_count]
+    )
+    node_grad_ref[...] = node_grad.astype(BF16)
+    rim_ref[:HB, :] = node_grad[:HB]
+    rim_ref[HB:, :] = node_grad[cell_count - HB :]
 
 
 def edge_kernel(
     fan_in,
+    cot_hbm,
+    summed_grad_hbm,
+    pre_grad_hbm,
+    w_edge_in_hbm,
+    _,
+    grad_edge_hbm,
+    token_ref,
     cot_ref,
     summed_grad_ref,
     pre_grad_ref,
-    w_edge_in_ref,
-    _,
-    grad_edge_hbm,
-    token_ref,
+    w_edge_ref,
     grad_edge_ref,
-    sems,
+    in_sems,
+    out_sems,
 ):
     edge_count, width = cot_ref.shape
     steps = edge_count // EDGE_BLOCK
     cells = EDGE_BLOCK // fan_in
+    loads = [
+        pltpu.make_async_copy(w_edge_in_hbm.at[:width, :], w_edge_ref, in_sems.at[0]),
+        pltpu.make_async_copy(summed_grad_hbm, summed_grad_ref, in_sems.at[1]),
+    ]
+    for step in range(steps):
+        rows = slice(step * EDGE_BLOCK, (step + 1) * EDGE_BLOCK)
+        for at, (far, near) in enumerate(((cot_hbm, cot_ref), (pre_grad_hbm, pre_grad_ref))):
+            loads.append(
+                pltpu.make_async_copy(
+                    far.at[rows, :], near.at[rows, :], in_sems.at[2 + 2 * step + at]
+                )
+            )
+    for load in loads:
+        load.start()
+    token_ref[...] = jnp.zeros(token_ref.shape, F32)
     member = iota((EDGE_BLOCK, 2 * cells), 1)
     owner = iota((EDGE_BLOCK, 2 * cells), 0) // fan_in
     spread = hot((owner == member) | (owner + cells == member))
+    loads[0].wait()
+    loads[1].wait()
     stores = []
     for step in range(steps):
         rows = slice(step * EDGE_BLOCK, (step + 1) * EDGE_BLOCK)
         pair = slice(step * 2 * cells, (step + 1) * 2 * cells)
+        loads[2 + 2 * step].wait()
+        loads[3 + 2 * step].wait()
         upstream = cot_ref[rows, :].astype(F32) + dot_nn(spread, summed_grad_ref[pair, :])
         grad_edge_ref[rows, :] = (
-            upstream + dot_nt(pre_grad_ref[rows, :], w_edge_in_ref[:width, :])
+            upstream + dot_nt(pre_grad_ref[rows, :], w_edge_ref[...])
         ).astype(BF16)
         stores.append(
             pltpu.make_async_copy(
-                grad_edge_ref.at[rows, :], grad_edge_hbm.at[rows, :], sems.at[step]
+                grad_edge_ref.at[rows, :], grad_edge_hbm.at[rows, :], out_sems.at[step]
             )
         )
         stores[-1].start()
-    token_ref[...] = jnp.zeros(token_ref.shape, F32)
     for store in stores:
         store.wait()
 
 
 def return_kernel(
-    part_count, capacity, scal, node_grad_ref, from_prev_ref, from_next_ref, ids_ref, out_ref, token_ref
+    part_count,
+    capacity,
+    scal,
+    node_grad_ref,
+    rim_ref,
+    low_ref,
+    high_ref,
+    ids_ref,
+    *outs,
 ):
     cell_count, width = node_grad_ref.shape
     chunks = width // LANES
-    block_rows = chunks * capacity
-    token_ref[...] = jnp.zeros(token_ref.shape, F32)
-    first = node_grad_ref[:HB, :] + from_prev_ref[...].astype(F32)
-    last = node_grad_ref[cell_count - HB :, :] + from_next_ref[...].astype(F32)
+    outs[part_count][...] = jnp.zeros(outs[part_count].shape, F32)
+    odd = scal[DOM_BIT] == 1
+    low = low_ref[...].astype(F32)
+    high = high_ref[...].astype(F32)
+    first = rim_ref[:HB, :] + jnp.where(odd, low, high)
+    last = rim_ref[HB:, :] + jnp.where(odd, high, low)
     grad = jnp.concatenate(
-        [first, node_grad_ref[HB : cell_count - HB, :], last], axis=0
-    ).astype(BF16)
+        [first.astype(BF16), node_grad_ref[HB : cell_count - HB, :], last.astype(BF16)], axis=0
+    )
     for step in range(part_count):
         pick = place(ids_ref[step * 16 : (step + 1) * 16, :], cell_count)
         rows = dot_tn(pick, grad).astype(BF16)
-        owner = scal[PART] - step
-        owner = jnp.where(owner < 0, owner + part_count, owner)
         for chunk in range(chunks):
-            start = pl.multiple_of(owner * block_rows + chunk * capacity, 16)
-            out_ref[pl.ds(start, capacity), :] = rows[
+            outs[step][chunk * capacity : (chunk + 1) * capacity, :] = rows[
                 :capacity, chunk * LANES : (chunk + 1) * LANES
             ]
 
 
-def finish_kernel(
-    part_count, capacity, scal, index_ref, block_ref, out_ref, token_ref, rows_ref, pick_ref
-):
+def finish_kernel(part_count, capacity, scal, index_ref, *refs):
+    blocks = refs[:part_count]
+    out_ref, token_ref, rows_ref, pick_ref = refs[part_count:]
     cell_count, width = out_ref.shape
     chunks = width // LANES
-    block_rows = chunks * capacity
     token_ref[...] = jnp.zeros(token_ref.shape, F32)
     slot, _ = slots_of(index_ref[...], scal[PART], part_count, cell_count)
     for step in range(part_count):
         base = step * LANES
         pick_ref[base : base + LANES, :] = hot(iota((LANES, cell_count), 0) + base == slot)
-        owner = scal[PART] + step
-        owner = jnp.where(owner >= part_count, owner - part_count, owner)
         for chunk in range(chunks):
-            start = pl.multiple_of(owner * block_rows + chunk * capacity, 16)
-            rows_ref[base : base + capacity, chunk * LANES : (chunk + 1) * LANES] = block_ref[
-                pl.ds(start, capacity), :
+            rows_ref[base : base + capacity, chunk * LANES : (chunk + 1) * LANES] = blocks[step][
+                chunk * capacity : (chunk + 1) * capacity, :
             ]
         if capacity < LANES:
             rows_ref[base + capacity : base + LANES, :] = jnp.zeros(
@@ -481,8 +542,9 @@
     return jnp.where(bit == 0, parts[0], parts[1])
 
 
-def core_kernel(kinds, bits, scal, keep_ref, got_ref, *refs):
-    total_ref, left_ref, right_ref = refs[-3:]
+def core_kernel(kinds, bits, scal, keep_ref, got_ref, _, *refs):
+    total_ref, left_ref, right_ref, token_ref = refs
+    token_ref[...] = jnp.zeros(token_ref.shape, F32)
     total = (keep_ref[...].astype(F32) + got_ref[...].astype(F32)).astype(BF16)
     total = total.reshape(total_ref.shape)
     total_ref[...] = total
@@ -554,31 +616,43 @@
     return (dims[0] // 2,) + dims[1:]
 
 
-def reduce_weights(scal, keep, got, geom_count, part_count, early, late):
-    bits = []
+def chains(geom_count):
+    columns = []
     bit = 2
     while bit < geom_count:
-        bits.append(bit)
+        columns.append(("columns", "geom", bit, GEOM_BITS + len(columns)))
         bit *= 2
-    columns = [("columns", "geom", bit, GEOM_BITS + at) for at, bit in enumerate(bits)]
     owner = ("owners", "dom", 1, DOM_BIT)
-    left = columns + [owner]
-    right = [owner] + columns
+    return columns + [owner], [owner] + columns
+
+
+def begin_weights(scal, keep, got, geom_count, part_count, *tokens):
+    left, right = chains(geom_count)
     rows, width = keep.shape
     dims = (part_count, rows // part_count, width)
     piece = (part_count, rows // part_count // 2, width)
-    total, send_left, send_right = local_call(
+    return local_call(
         functools.partial(core_kernel, (left[0][0], right[0][0]), (left[0][3], right[0][3])),
-        [(dims,), (halved(piece, left[0][0]),), (halved(piece, right[0][0]),)],
+        [
+            (dims,),
+            (halved(piece, left[0][0]),),
+            (halved(piece, right[0][0]),),
+            ((8, LANES), F32),
+        ],
         "core",
         scal,
         keep,
         got,
-    )
+        *tokens,
+    )
+
+
+def pair_weights(scal, total, send_left, send_right, geom_count, part_count, early):
+    rows = total.shape[1]
     ends = []
-    for part, chain, send in ((0, left, send_left), (1, right, send_right)):
+    for part, chain, send in zip((0, 1), chains(geom_count), (send_left, send_right)):
         value = total
-        now = piece
+        now = (part_count, rows // 2, total.shape[2])
         for at in range(len(chain) - 1):
             kind, axis, bit, place_at = chain[at]
             follow = chain[at + 1]
@@ -595,13 +669,18 @@
                 scal,
                 value,
                 swap(send, axis, bit),
-                *early,
+                *early[part],
             )
         if len(chain) == 1:
-            half = rows // part_count // 2
+            half = rows // 2
             value = value[:, part * half : (part + 1) * half]
         ends.append((value, swap(send, chain[-1][1], chain[-1][2])))
         end = halved(now, chain[-1][0])
+    return ends, end
+
+
+def reduce_weights(scal, ends, end, geom_count, part_count, early, late):
+    left, right = chains(geom_count)
     out = (2 * end[1], end[2])
     owners = part_count // 2
     pieces = local_call(
@@ -611,6 +690,7 @@
         scal,
         *ends[0],
         *ends[1],
+        early,
     )
     got = [swap(pieces[other], "dom", 2 * other) for other in range(owners - 1, 0, -1)]
     total = pl.pallas_call(
@@ -621,9 +701,7 @@
         compiler_params=params(24),
         name="sum",
     )(pieces[0], *got, late)
-    for place_at, bit in [(GEOM_BITS + at, bit) for at, bit in enumerate(bits)][::-1] + [
-        (CORE, 1)
-    ]:
+    for place_at, bit in [(link[3], link[2]) for link in left[-2::-1]] + [(CORE, 1)]:
         out = (out[0], 2 * out[1])
         last = bit == 1
         total = pl.pallas_call(
@@ -642,15 +720,18 @@
     return lax.ppermute(value, "dom", [(at, (at + steps) % count) for at in range(count)])
 
 
-def neighbour(value, step):
+def neighbour(value, first):
     count = lax.axis_size("dom")
-    return lax.ppermute(
-        value, "dom", [(at, at + step) for at in range(count) if 0 <= at + step < count]
-    )
+    pairs = [(at, at + 1) for at in range(first, count - 1, 2)]
+    return lax.ppermute(value, "dom", pairs + [(right, left) for left, right in pairs])
 
 
 def send_order(part_count):
     return sorted(range(1, part_count), key=lambda at: (-min(at, part_count - at), at))
+
+
+def pinned(value):
+    return pltpu.with_memory_space_constraint(value, pltpu.HBM)
 
 
 def near_shape(dims, kind=BF16):
@@ -696,7 +777,7 @@
     )(
         scal,
         *[
-            pltpu.with_memory_space_constraint(value, pltpu.HBM)
+            pinned(value)
             for value in (
                 source,
                 edges,
@@ -712,7 +793,7 @@
     )
 
 
-def run_main(fan_in, scale, scal, nodes, before, after, prepared):
+def run_main(fan_in, scale, scal, nodes, low, high, prepared):
     edge_count, width = prepared[0].shape
     cell_count = nodes.shape[0]
     cells = EDGE_BLOCK // fan_in
@@ -727,17 +808,19 @@
         out_shape=[
             shape(by_edge),
             shape(by_cell),
-            near_shape(by_edge),
-            near_shape((2 * cell_count, width)),
-            near_shape((HB, width)),
-            near_shape((HB, width)),
+            shape(by_edge),
+            shape((2 * cell_count, width)),
+            near_shape((padded, width)),
+            near_shape(by_cell),
             near_shape(by_cell, F32),
             near_shape(weights),
             near_shape(weights),
         ],
         in_specs=[scalars()] + [near] * 13,
-        out_specs=[far, far] + [near] * 7,
+        out_specs=[far] * 4 + [near] * 5,
         scratch_shapes=[
+            VMEM(by_edge, BF16),
+            VMEM((2 * cell_count, width), BF16),
             VMEM(by_cell, BF16),
             VMEM((padded, width), BF16),
             VMEM((padded + cells, width), BF16),
@@ -748,28 +831,36 @@
             VMEM((edge_count, 1), F32),
             VMEM(by_cell, BF16),
             VMEM(by_edge, BF16),
-            VMEM(by_cell, BF16),
-            pltpu.SemaphoreType.DMA((2,)),
+            pltpu.SemaphoreType.DMA((4,)),
         ],
         compiler_params=params(MAIN_LIMIT),
         cost_estimate=cost(28 * edge_count * width * width, 16 * MIB),
         name="main",
-    )(scal, nodes, before, after, *prepared)
-
-
-def run_edges(fan_in, cot, summed_grad, pre_grad, w_edge_in, token):
+    )(scal, nodes, low, high, *prepared)
+
+
+def run_edges(fan_in, cot, summed_grad, pre_grad, w_edge_in, *tokens):
     edge_count, width = cot.shape
     steps = edge_count // EDGE_BLOCK
+    far = pl.BlockSpec(memory_space=pltpu.HBM)
     return pl.pallas_call(
         functools.partial(edge_kernel, fan_in),
         out_shape=[shape((edge_count, width)), near_shape((8, LANES), F32)],
-        in_specs=whole(5),
-        out_specs=[pl.BlockSpec(memory_space=pltpu.HBM), pl.BlockSpec(memory_space=VMEM)],
-        scratch_shapes=[VMEM((edge_count, width), BF16), pltpu.SemaphoreType.DMA((steps,))],
+        in_specs=[far] * 4 + whole(len(tokens)),
+        out_specs=[far, pl.BlockSpec(memory_space=VMEM)],
+        scratch_shapes=[
+            VMEM((edge_count, width), BF16),
+            VMEM(summed_grad.shape, BF16),
+            VMEM((edge_count, width), BF16),
+            VMEM((width, width), BF16),
+            VMEM((edge_count, width), BF16),
+            pltpu.SemaphoreType.DMA((2 + 2 * steps,)),
+            pltpu.SemaphoreType.DMA((steps,)),
+        ],
         compiler_params=params(24),
-        cost_estimate=cost(4 * edge_count * width * width, 7 * MIB),
+        cost_estimate=cost(1, 1),
         name="edges",
-    )(cot, summed_grad, pre_grad, w_edge_in, token)
+    )(*[pinned(value) for value in (cot, summed_grad, pre_grad, w_edge_in)], *tokens)
 
 
 def local(
@@ -829,7 +920,7 @@
     got = {0: sends[0]}
     for step in send_order(part_count):
         got[step] = shift(sends[step], step)
-    nodes, head, tail, ids = pl.pallas_call(
+    nodes, low, high, ids = pl.pallas_call(
         functools.partial(unpack_kernel, part_count, capacity),
         out_shape=[
             shape((cell_count, width)),
@@ -837,7 +928,7 @@
             shape((HB, width)),
             shape((part_count * 16, LANES)),
         ],
-        in_specs=whole(part_count + 1),
+        in_specs=whole(part_count) + [scalars()] + whole(1),
         out_specs=whole(4),
         scratch_shapes=[
             VMEM((part_count * LANES, width), BF16),
@@ -845,42 +936,64 @@
         ],
         compiler_params=params(24),
         name="unpack",
-    )(*[got[step] for step in range(part_count)], prepared[-1])
-    before = neighbour(tail, 1)
-    after = neighbour(head, -1)
+    )(*[got[step] for step in range(part_count)], scal, prepared[-1])
+    low = neighbour(low, 0)
+    high = neighbour(high, 1)
 
     (
         edge_new,
         node_new,
         pre_grad,
         summed_grad,
-        to_prev,
-        to_next,
-        node_grad,
+        sent,
+        received,
+        base,
         keep,
         send,
-    ) = run_main(fan_in, scale, scal, nodes, before, after, prepared[:-1])
-    from_next = neighbour(to_prev, -1)
-    from_prev = neighbour(to_next, 1)
-
-    returning, token = pl.pallas_call(
+    ) = run_main(fan_in, scale, scal, nodes, low, high, prepared[:-1])
+    low, high, node_grad, rim = pl.pallas_call(
+        cell_kernel,
+        out_shape=[
+            near_shape((HB, width)),
+            near_shape((HB, width)),
+            near_shape((cell_count, width)),
+            near_shape((2 * HB, width), F32),
+        ],
+        in_specs=[scalars()] + whole(4),
+        out_specs=whole(4),
+        compiler_params=params(24),
+        cost_estimate=cost(3 * cell_count * width * width, 3 * MIB),
+        name="cells",
+    )(scal, sent, received, base, prepared[3])
+    low = neighbour(low, 0)
+    high = neighbour(high, 1)
+    *returning, token = pl.pallas_call(
         functools.partial(return_kernel, part_count, capacity),
-        out_shape=[near_shape((part_count * block_rows, LANES)), near_shape((8, LANES), F32)],
-        in_specs=[scalars()] + whole(4),
-        out_specs=whole(2),
+        out_shape=[near_shape((block_rows, LANES))] * part_count + [near_shape((8, LANES), F32)],
+        in_specs=[scalars()] + whole(5),
+        out_specs=whole(part_count + 1),
         compiler_params=params(24),
+        cost_estimate=cost(1, 1),
         name="returning",
-    )(scal, node_grad, from_prev, from_next, ids)
-    back = lax.all_to_all(
-        returning.reshape(part_count, block_rows, LANES), "dom", 0, 0, tiled=True
-    ).reshape(part_count * block_rows, LANES)
+    )(scal, node_grad, rim, low, high, ids)
+    *begun, token = begin_weights(
+        scal, keep, swap(send, "geom", 1), geom_count, part_count, token
+    )
+
     grad_edge, edge_token = run_edges(
-        fan_in, prepared[2], summed_grad, pre_grad, prepared[3], token
+        fan_in, cot, summed_grad, pre_grad, w_edge_in, token
+    )
+    back = {0: returning[0]}
+    for step in send_order(part_count):
+        back[step] = shift(returning[step], -step)
+    early = [back[step] for step in send_order(part_count)]
+    ends, end = pair_weights(
+        scal, *begun, geom_count, part_count, (early[:FIRST], early[:SECOND])
     )
     grad_in, late = pl.pallas_call(
         functools.partial(finish_kernel, part_count, capacity),
         out_shape=[shape((cell_count, width)), near_shape((8, LANES), F32)],
-        in_specs=[scalars()] + whole(2),
+        in_specs=[scalars()] + whole(1 + part_count),
         out_specs=whole(2),
         scratch_shapes=[
             VMEM((part_count * LANES, width), BF16),
@@ -888,10 +1001,8 @@
         ],
         compiler_params=params(24),
         name="finish",
-    )(scal, new_index, back)
-    weight_grads = reduce_weights(
-        scal, keep, swap(send, "geom", 1), geom_count, part_count, (token, edge_token), late
-    )
+    )(scal, new_index, *[back[step] for step in range(part_count)])
+    weight_grads = reduce_weights(scal, ends, end, geom_count, part_count, edge_token, late)
     return (node_new[None], edge_new[None], grad_in[None], grad_edge[None], weight_grads)
 
 

time: 130 us -> 124 us (0.954)
  waiting for transfers between devices: 32.8 us -> 20.8 us
  starting transfers between devices: 46.5 us -> 56.1 us
  local copies, waits for them, and re-layouts: 6 us -> 2.79 us
    ppermute x7 -> x14, starting transfers between devices: 13.8 us -> 28.7 us  [shift(): lax.ppermute(value, 'dom', [(at, (at + steps) % count) for at in range(co...]
    ppermute x10, waiting for transfers between devices: 22.5 us -> 10.5 us  [swap(): return lax.ppermute(value, axis, [(at, at ^ bit) for at in range(count)])]
    ppermute x7 -> x14, waiting for transfers between devices: 0.02 us -> 6.64 us  [shift(): lax.ppermute(value, 'dom', [(at, (at + steps) % count) for at in range(co...]
    ppermute x4, waiting for transfers between devices: 10.2 us -> 3.69 us  [neighbour(): lax.ppermute(value, 'dom', pairs + [(right, left) for left, right in pairs])]
    all_to_all x1 -> x0, starting transfers between devices: 6.3 us -> none  [local(): lax.all_to_all(returning.reshape(part_count, block_rows, LANES), 'dom', 0...]
    unnamed x22 -> x10, local copies, waits for them, and re-layouts: 5.92 us -> 2.71 us
    pallas_call x1, Pallas kernels: 21.9 us -> 19.1 us  [run_main(): pl.pallas_call(functools.partial(main_kernel, fan_in, scale), out_shape=[...]
    pallas_call x1, Pallas kernels: 2.63 us -> 4.91 us  [run_edges(): pl.pallas_call(functools.partial(edge_kernel, fan_in), out_shape=[shape((...]
  transfers between devices with their start and end apart: 22 -> 28, of which waited for: 12 -> 13; matrix products, arithmetic and copies ran while one was open for 0% -> 0% of each run, Pallas kernels for 13% -> 13%
where the time goes in v1:
time: 124 us; the launch traced here: 123 us
  starting transfers between devices  56.1 us (45%)
  Pallas kernels  42.8 us (35%)
  waiting for transfers between devices  20.8 us (17%)
  local copies, waits for them, and re-layouts  2.79 us (2%)
    ppermute x14, starting transfers between devices, shift(): lax.ppermute(value, 'dom', [(at, (at + steps) % count) for at in range(co...  28.7 us
    pallas_call x1, Pallas kernels, run_main(): pl.pallas_call(functools.partial(main_kernel, fan_in, scale), out_shape=[...  19.1 us
    ppermute x10, starting transfers between devices, swap(): return lax.ppermute(value, axis, [(at, at ^ bit) for at in range(count)])  14.6 us
    ppermute x4, starting transfers between devices, neighbour(): lax.ppermute(value, 'dom', pairs + [(right, left) for left, right in pairs])  12.8 us
    ppermute x10, waiting for transfers between devices, swap(): return lax.ppermute(value, axis, [(at, at ^ bit) for at in range(count)])  10.5 us
    ppermute x14, waiting for transfers between devices, shift(): lax.ppermute(value, 'dom', [(at, (at + steps) % count) for at in range(co...  6.64 us
    pallas_call x1, Pallas kernels, run_prep(): pl.pallas_call(functools.partial(prep_kernel, fan_in, cell_count), out_sh...  5.01 us
    pallas_call x1, Pallas kernels, run_edges(): pl.pallas_call(functools.partial(edge_kernel, fan_in), out_shape=[shape((...  4.91 us
  transfers between devices with their start and end apart: 28, of which 13 were waited for; matrix products, arithmetic and copies ran while one was open for 0% of the time, Pallas kernels for 13%

profile of v1, /device:TPU:0, one launch (start us, length us, event | category | flops | bytes accessed | tf_op | source)
XLA Modules:
  0.0 123.5 jit_solution(2660258321211410720)
XLA Ops:
  0.8 1.0 copy-done.2
  1.8 0.7 copy-done.3
  2.5 1.7 %pack.1 = (bf16[400,128]{1,0:T(8,128)(2,1)S(1)}, bf16[400,128]{1,0:T(8,128)(2,1)S(1)}, bf16[400,128]{1,0:T(8,128)(2,1)S(1)}, bf16[400,128]{1,0:T(8,128)(2,1)S(1)...) custom-call(s32[5]{0:T(128)S(1)} %stack.23.scal.refs_8_, ...), custom_call_target="tpu_custom_call" | custom-call | tf_op jit(solution)/shard_map/pack/pallas_call | solution.py:898
  4.2 3.0 %collective-permute-start = (bf16[400,128]{1,0:T(8,128)(2,1)S(1)}, bf16[400,128]{1,0:T(8,128)(2,1)S(1)}, u32[]{:S(2)}, u32[]{:S(2)}) collective-permute-start(bf16[400,128]{1,0:T(8,128)(2,1)S(1)} %get-tuple-element.68), channel_id=1, source_target_pairs={{0,1},{1,2},{2,3},{3,4},{4,5},{5,6},{6,7},{7,0},{8,9},{9,10},{10,1... | collective-permute-start | bytes 307208 | tf_op jit(solution)/shard_map/ppermute | solution.py:720
  7.3 1.6 %collective-permute-start.1 = (bf16[400,128]{1,0:T(8,128)(2,1)S(1)}, bf16[400,128]{1,0:T(8,128)(2,1)S(1)}, u32[]{:S(2)}, u32[]{:S(2)}) collective-permute-start(bf16[400,128]{1,0:T(8,128)(2,1)S(1)} %get-tuple-element.69), channel_id=1, source_target_pairs={{0,2},{1,3},{2,4},{3,5},{4,6},{5,7},{6,0},{7,1},{8,10},{9,11},{10,... | collective-permute-start | bytes 307208 | tf_op jit(solution)/shard_map/ppermute | solution.py:720
  8.8 2.5 %collective-permute-start.2 = (bf16[400,128]{1,0:T(8,128)(2,1)S(1)}, bf16[400,128]{1,0:T(8,128)(2,1)S(1)}, u32[]{:S(2)}, u32[]{:S(2)}) collective-permute-start(bf16[400,128]{1,0:T(8,128)(2,1)S(1)} %get-tuple-element.70), channel_id=1, source_target_pairs={{0,3},{1,4},{2,5},{3,6},{4,7},{5,0},{6,1},{7,2},{8,11},{9,12},{10,... | collective-permute-start | bytes 307208 | tf_op jit(solution)/shard_map/ppermute | solution.py:720
  11.4 1.2 collective-permute-start.3
  12.6 2.6 %collective-permute-start.4 = (bf16[400,128]{1,0:T(8,128)(2,1)S(1)}, bf16[400,128]{1,0:T(8,128)(2,1)S(1)}, u32[]{:S(2)}, u32[]{:S(2)}) collective-permute-start(bf16[400,128]{1,0:T(8,128)(2,1)S(1)} %get-tuple-element.72), channel_id=1, source_target_pairs={{0,5},{1,6},{2,7},{3,0},{4,1},{5,2},{6,3},{7,4},{8,13},{9,14},{10,... | collective-permute-start | bytes 307208 | tf_op jit(solution)/shard_map/ppermute | solution.py:720
  15.2 1.3 %collective-permute-start.5 = (bf16[400,128]{1,0:T(8,128)(2,1)S(1)}, bf16[400,128]{1,0:T(8,128)(2,1)S(1)}, u32[]{:S(2)}, u32[]{:S(2)}) collective-permute-start(bf16[400,128]{1,0:T(8,128)(2,1)S(1)} %get-tuple-element.73), channel_id=1, source_target_pairs={{0,6},{1,7},{2,0},{3,1},{4,2},{5,3},{6,4},{7,5},{8,14},{9,15},{10,... | collective-permute-start | bytes 307208 | tf_op jit(solution)/shard_map/ppermute | solution.py:720
  16.6 1.4 %collective-permute-start.6 = (bf16[400,128]{1,0:T(8,128)(2,1)S(1)}, bf16[400,128]{1,0:T(8,128)(2,1)S(1)}, u32[]{:S(2)}, u32[]{:S(2)}) collective-permute-start(bf16[400,128]{1,0:T(8,128)(2,1)S(1)} %get-tuple-element.74), channel_id=1, source_target_pairs={{0,7},{1,0},{2,1},{3,2},{4,3},{5,4},{6,5},{7,6},{8,15},{9,8},{10,9... | collective-permute-start | bytes 307208 | tf_op jit(solution)/shard_map/ppermute | solution.py:720
  18.0 5.0 %prep.1 = (bf16[2048,512]{1,0:T(8,128)(2,1)S(1)}, bf16[512,512]{1,0:T(8,128)(2,1)S(1)}, bf16[2048,512]{1,0:T(8,128)(2,1)S(1)}, bf16[1536,512]{1,0:T(8,128)(2,1)S...) custom-call(s32[5]{0:T(128)S(1)} %stack.23.scal.refs_8_, ...), custom_call_target="tpu_custom_call" | custom-call | flops 2147483648 | bytes 20971520 | tf_op jit(solution)/shard_map/prep/pallas_call | solution.py:759
  23.1 1.3 %unpack.1 = (bf16[512,512]{1,0:T(8,128)(2,1)S(1)}, bf16[64,512]{1,0:T(8,128)(2,1)S(1)}, bf16[64,512]{1,0:T(8,128)(2,1)S(1)}, bf16[128,128]{1,0:T(8,128)(2,1)S(1)}) custom-call(bf16[400,128]{1,0:T(8,128)(2,1)S(1)} %get-tuple-element.67.refs_0_, bf16[400,128]{1,0:T(8,128)(2,1)S(1)} %collective-permute-done.refs_1_, ...), custom_call_target="tpu_custom_call" | custom-call | tf_op jit(solution)/shard_map/unpack/pallas_call | solution.py:923
  24.4 4.0 %collective-permute-start.7 = (bf16[64,512]{1,0:T(8,128)(2,1)S(1)}, bf16[64,512]{1,0:T(8,128)(2,1)S(1)}, u32[]{:S(2)}, u32[]{:S(2)}) collective-permute-start(bf16[64,512]{1,0:T(8,128)(2,1)S(1)} %get-tuple-element.78), channel_id=1, source_target_pairs={{0,1},{2,3},{4,5},{6,7},{1,0},{3,2},{5,4},{7,6},{8,9},{10,11},{12,... | collective-permute-start | bytes 196616 | tf_op jit(solution)/shard_map/ppermute | solution.py:726
  28.4 0.7 collective-permute-start.8
  29.1 1.6 %collective-permute-done.7.low_ref = bf16[64,512]{1,0:T(8,128)(2,1)S(1)} collective-permute-done((bf16[64,512]{1,0:T(8,128)(2,1)S(1)}, bf16[64,512]{1,0:T(8,128)(2,1)S(1)}, u32[]{:S(2)}, u32[]{:S(2)}) %collective-permute-start.7) | collective-permute-done | bytes 65568 | tf_op jit(solution)/shard_map/ppermute | solution.py:726
  30.7 19.1 %main.1 = (bf16[2048,512]{1,0:T(8,128)(2,1)}, bf16[512,512]{1,0:T(8,128)(2,1)}, bf16[2048,512]{1,0:T(8,128)(2,1)S(1)}, bf16[1024,512]{1,0:T(8,128)(2,1)S(1)}, bf...) custom-call(s32[5]{0:T(128)S(1)} %stack.23.scal.refs_8_, ...), custom_call_target="tpu_custom_call" | custom-call | flops 15032385536 | bytes 16777216 | tf_op jit(solution)/shard_map/main/pallas_call | solution.py:806
  49.9 1.0 copy-done.1
  50.8 1.3 %cells.1 = (bf16[64,512]{1,0:T(8,128)(2,1)S(1)}, bf16[64,512]{1,0:T(8,128)(2,1)S(1)}, bf16[512,512]{1,0:T(8,128)(2,1)S(1)}, f32[128,512]{1,0:T(8,128)S(1)}) custom-call(s32[5]{0:T(128)S(1)} %stack.23.scal.refs_8_, bf16[640,512]{1,0:T(8,128)(2,1)S(1)} %get-tuple-element.92.sent_ref, bf16[512,512]{1,0:T(8,128)(2,1)S(1)} %get-tuple-element.93.received_ref, ...), custom_call_target="tpu_custom_call" | custom-call | flops 402653184 | bytes 3145728 | tf_op jit(solution)/shard_map/cells/pallas_call | solution.py:954
  52.2 7.5 %collective-permute-start.9 = (bf16[64,512]{1,0:T(8,128)(2,1)S(1)}, bf16[64,512]{1,0:T(8,128)(2,1)S(1)}, u32[]{:S(2)}, u32[]{:S(2)}) collective-permute-start(bf16[64,512]{1,0:T(8,128)(2,1)S(1)} %get-tuple-element.97), channel_id=1, source_target_pairs={{0,1},{2,3},{4,5},{6,7},{1,0},{3,2},{5,4},{7,6},{8,9},{10,11},{12,... | collective-permute-start | bytes 196616 | tf_op jit(solution)/shard_map/ppermute | solution.py:726
  59.7 0.7 collective-permute-start.10
  60.4 2.1 %collective-permute-done.9.low_ref = bf16[64,512]{1,0:T(8,128)(2,1)S(1)} collective-permute-done((bf16[64,512]{1,0:T(8,128)(2,1)S(1)}, bf16[64,512]{1,0:T(8,128)(2,1)S(1)}, u32[]{:S(2)}, u32[]{:S(2)}) %collective-permute-start.9) | collective-permute-done | bytes 65568 | tf_op jit(solution)/shard_map/ppermute | solution.py:726
  62.5 1.3 %returning.1 = (bf16[384,128]{1,0:T(8,128)(2,1)S(1)}, bf16[384,128]{1,0:T(8,128)(2,1)S(1)}, bf16[384,128]{1,0:T(8,128)(2,1)S(1)}, bf16[384,128]{1,0:T(8,128)(2,1...) custom-call(s32[5]{0:T(128)S(1)} %stack.23.scal.refs_8_, ...), custom_call_target="tpu_custom_call" | custom-call | flops 1 | bytes 1 | tf_op jit(solution)/shard_map/returning/pallas_call | solution.py:970
  63.8 1.1 core.1
  64.9 1.6 %collective-permute-start.19 = (bf16[8,224,128]{2,1,0:T(8,128)(2,1)S(1)}, bf16[8,224,128]{2,1,0:T(8,128)(2,1)S(1)}, u32[]{:S(2)}, u32[]{:S(2)}) collective-permute-start(bf16[8,224,128]{2,1,0:T(8,128)(2,1)S(1)} %get-tuple-element.117), channel_id=1, source_target_pairs={{0,16},{8,24},{16,0},{24,8},{1,17},{9,25},{17,1},{25,9},{2,18},{10... | collective-permute-start | bytes 1376264 | tf_op jit(solution)/shard_map/ppermute | solution.py:532
  66.5 4.8 %collective-permute-start.21 = (bf16[4,224,256]{2,1,0:T(8,128)(2,1)S(1)}, bf16[4,224,256]{2,1,0:T(8,128)(2,1)S(1)}, u32[]{:S(2)}, u32[]{:S(2)}) collective-permute-start(bf16[4,224,256]{2,1,0:T(8,128)(2,1)S(1)} %get-tuple-element.120), channel_id=1, source_target_pairs={{0,1},{1,0},{2,3},{3,2},{4,5},{5,4},{6,7},{7,6},{8,9},{9,8},{10,11... | collective-permute-start | bytes 1376264 | tf_op jit(solution)/shard_map/ppermute | solution.py:532
  71.3 3.6 %collective-permute-start.13 = (bf16[384,128]{1,0:T(8,128)(2,1)S(1)}, bf16[384,128]{1,0:T(8,128)(2,1)S(1)}, u32[]{:S(2)}, u32[]{:S(2)}) collective-permute-start(bf16[384,128]{1,0:T(8,128)(2,1)S(1)} %get-tuple-element.103), channel_id=1, source_target_pairs={{0,5},{1,6},{2,7},{3,0},{4,1},{5,2},{6,3},{7,4},{8,13},{9,14},{10,... | collective-permute-start | bytes 294920 | tf_op jit(solution)/shard_map/ppermute | solution.py:720
  75.0 2.9 %collective-permute-start.15 = (bf16[384,128]{1,0:T(8,128)(2,1)S(1)}, bf16[384,128]{1,0:T(8,128)(2,1)S(1)}, u32[]{:S(2)}, u32[]{:S(2)}) collective-permute-start(bf16[384,128]{1,0:T(8,128)(2,1)S(1)} %get-tuple-element.105), channel_id=1, source_target_pairs={{0,3},{1,4},{2,5},{3,6},{4,7},{5,0},{6,1},{7,2},{8,11},{9,12},{10,... | collective-permute-start | bytes 294920 | tf_op jit(solution)/shard_map/ppermute | solution.py:720
  78.1 7.1 %collective-permute-start.11 = (bf16[384,128]{1,0:T(8,128)(2,1)S(1)}, bf16[384,128]{1,0:T(8,128)(2,1)S(1)}, u32[]{:S(2)}, u32[]{:S(2)}) collective-permute-start(bf16[384,128]{1,0:T(8,128)(2,1)S(1)} %get-tuple-element.101), channel_id=1, source_target_pairs={{0,7},{1,0},{2,1},{3,2},{4,3},{5,4},{6,5},{7,6},{8,15},{9,8},{10,9... | collective-permute-start | bytes 294920 | tf_op jit(solution)/shard_map/ppermute | solution.py:720
  85.2 1.4 %collective-permute-done.14.refs_4_.refs_0_ = bf16[384,128]{1,0:T(8,128)(2,1)S(1)} collective-permute-done((bf16[384,128]{1,0:T(8,128)(2,1)S(1)}, bf16[384,128]{1,0:T(8,128)(2,1)S(1)}, u32[]{:S(2)}, u32[]{:S(2)}) %collective-permute-start.14) | collective-permute-done | bytes 98336 | tf_op jit(solution)/shard_map/ppermute | solution.py:720
  86.6 0.8 collective-permute-done.15.refs_5_.refs_2_
  87.4 1.3 %collective-permute-start.16 = (bf16[384,128]{1,0:T(8,128)(2,1)S(1)}, bf16[384,128]{1,0:T(8,128)(2,1)S(1)}, u32[]{:S(2)}, u32[]{:S(2)}) collective-permute-start(bf16[384,128]{1,0:T(8,128)(2,1)S(1)} %get-tuple-element.106), channel_id=1, source_target_pairs={{0,2},{1,3},{2,4},{3,5},{4,6},{5,7},{6,0},{7,1},{8,10},{9,11},{10,... | collective-permute-start | bytes 294920 | tf_op jit(solution)/shard_map/ppermute | solution.py:720
  88.7 0.8 stage.2
  89.4 2.4 %collective-permute-start.20 = (bf16[4,224,128]{2,1,0:T(8,128)(2,1)S(1)}, bf16[4,224,128]{2,1,0:T(8,128)(2,1)S(1)}, u32[]{:S(2)}, u32[]{:S(2)}) collective-permute-start(bf16[4,224,128]{2,1,0:T(8,128)(2,1)S(1)} %get-tuple-element.119), channel_id=1, source_target_pairs={{0,1},{1,0},{2,3},{3,2},{4,5},{5,4},{6,7},{7,6},{8,9},{9,8},{10,11... | collective-permute-start | bytes 688136 | tf_op jit(solution)/shard_map/ppermute | solution.py:532
  92.3 1.5 %collective-permute-done.16.refs_6_.refs_4_ = bf16[384,128]{1,0:T(8,128)(2,1)S(1)} collective-permute-done((bf16[384,128]{1,0:T(8,128)(2,1)S(1)}, bf16[384,128]{1,0:T(8,128)(2,1)S(1)}, u32[]{:S(2)}, u32[]{:S(2)}) %collective-permute-start.16) | collective-permute-done | bytes 98336 | tf_op jit(solution)/shard_map/ppermute | solution.py:720
  93.8 2.3 %collective-permute-done.17.refs_7_.refs_6_ = bf16[384,128]{1,0:T(8,128)(2,1)S(1)} collective-permute-done((bf16[384,128]{1,0:T(8,128)(2,1)S(1)}, bf16[384,128]{1,0:T(8,128)(2,1)S(1)}, u32[]{:S(2)}, u32[]{:S(2)}) %collective-permute-start.17) | collective-permute-done | bytes 98336 | tf_op jit(solution)/shard_map/ppermute | solution.py:720
  96.1 0.7 stage.3
  96.8 0.6 collective-permute-start.22
  97.4 4.9 %edges.1 = (bf16[2048,512]{1,0:T(8,128)(2,1)}, f32[8,128]{1,0:T(8,128)S(1)}) custom-call(bf16[2048,512]{1,0:T(8,128)(2,1)} %bitcast.15, bf16[1024,512]{1,0:T(8,128)(2,1)} %copy-done.1, bf16[2048,512]{1,0:T(8,128)(2,1)} %copy-done, bf16[1536,512]{1,0:T(8,128)(2,1)} %w_edge_in_hbm.3, f32[8,128]{1,0:T(8,128)S(1)} %get-tuple-element.114._), custom_call_target="tpu_custom_call" | custom-call | flops 1 | bytes 1 | tf_op jit(solution)/shard_map/edges/pallas_call | solution.py:846
  102.9 0.9 split.1
  103.8 1.7 %collective-permute-start.23 = (bf16[448,128]{1,0:T(8,128)(2,1)S(1)}, bf16[448,128]{1,0:T(8,128)(2,1)S(1)}, u32[]{:S(2)}, u32[]{:S(2)}) collective-permute-start(bf16[448,128]{1,0:T(8,128)(2,1)S(1)} %get-tuple-element.125), channel_id=1, source_target_pairs={{0,6},{1,7},{2,4},{3,5},{4,2},{5,3},{6,0},{7,1},{8,14},{9,15},{10,... | collective-permute-start | bytes 344072 | tf_op jit(solution)/shard_map/ppermute | solution.py:532
  105.7 2.6 %collective-permute-start.25 = (bf16[448,128]{1,0:T(8,128)(2,1)S(1)}, bf16[448,128]{1,0:T(8,128)(2,1)S(1)}, u32[]{:S(2)}, u32[]{:S(2)}) collective-permute-start(bf16[448,128]{1,0:T(8,128)(2,1)S(1)} %get-tuple-element.127), channel_id=1, source_target_pairs={{0,2},{1,3},{2,0},{3,1},{4,6},{5,7},{6,4},{7,5},{8,10},{9,11},{10,... | collective-permute-start | bytes 344072 | tf_op jit(solution)/shard_map/ppermute | solution.py:532
  108.3 2.4 %finish.1 = (bf16[512,512]{1,0:T(8,128)(2,1)}, f32[8,128]{1,0:T(8,128)S(1)}) custom-call(s32[5]{0:T(128)S(1)} %stack.23.scal.refs_8_, s32[1,512]{1,0:T(1,128)S(1)} %copy-done.4, bf16[384,128]{1,0:T(8,128)(2,1)S(1)} %get-tuple-element.100.refs_0_, bf16[384,128]{1,0:T(8,128)(2,1)S(1)} %collective-permute-done.11.refs_1_.refs_5_, ...), custom_call_target="tpu_custom_call" | custom-call | tf_op jit(solution)/shard_map/finish/pallas_call | solution.py:993
  110.6 0.6 collective-permute-done.23.refs_1_
  111.3 3.6 %collective-permute-done.24.refs_2_ = bf16[448,128]{1,0:T(8,128)(2,1)S(1)} collective-permute-done((bf16[448,128]{1,0:T(8,128)(2,1)S(1)}, bf16[448,128]{1,0:T(8,128)(2,1)S(1)}, u32[]{:S(2)}, u32[]{:S(2)}) %collective-permute-start.24) | collective-permute-done | bytes 114720 | tf_op jit(solution)/shard_map/ppermute | solution.py:532
  114.9 0.7 collective-permute-start.26
  115.6 4.2 %collective-permute-done.26.theirs_ref = bf16[448,128]{1,0:T(8,128)(2,1)S(1)} collective-permute-done((bf16[448,128]{1,0:T(8,128)(2,1)S(1)}, bf16[448,128]{1,0:T(8,128)(2,1)S(1)}, u32[]{:S(2)}, u32[]{:S(2)}) %collective-permute-start.26) | collective-permute-done | bytes 114720 | tf_op jit(solution)/shard_map/ppermute | solution.py:532
  120.4 1.5 %collective-permute-done.27.theirs_ref = bf16[448,256]{1,0:T(8,128)(2,1)S(1)} collective-permute-done((bf16[448,256]{1,0:T(8,128)(2,1)S(1)}, bf16[448,256]{1,0:T(8,128)(2,1)S(1)}, u32[]{:S(2)}, u32[]{:S(2)}) %collective-permute-start.27) | collective-permute-done | bytes 229408 | tf_op jit(solution)/shard_map/ppermute | solution.py:532
  121.9 1.6 %join.3 = f32[448,512]{1,0:T(8,128)} custom-call(s32[5]{0:T(128)S(1)} %stack.23.scal.refs_8_, bf16[448,256]{1,0:T(8,128)(2,1)S(1)} %join.2.mine_ref, bf16[448,256]{1,0:T(8,128)(2,1)S(1)} %collective-permute-done.27.theirs_ref), custom_call_target="tpu_custom_call" | custom-call | tf_op jit(solution)/shard_map/join/pallas_call | solution.py:707
  (34 shorter events, 2.3 us)
Async XLA Ops:
  0.8 1.0 copy-start.2
  1.8 0.7 copy-start.3
  4.2 11.0 %collective-permute-start = (bf16[400,128]{1,0:T(8,128)(2,1)S(1)}, bf16[400,128]{1,0:T(8,128)(2,1)S(1)}, u32[]{:S(2)}, u32[]{:S(2)}) collective-permute-start(bf16[400,128]{1,0:T(8,128)(2,1)S(1)} %get-tuple-element.68), channel_id=1, source_target_pairs={{0,1},{1,2},{2,3},{3,4},{4,5},{5,6},{6,7},{7,0},{8,9},{9,10},{10,1... | collective-permute-start | bytes 307208 | tf_op jit(solution)/shard_map/ppermute | solution.py:720
  7.3 9.3 %collective-permute-start.1 = (bf16[400,128]{1,0:T(8,128)(2,1)S(1)}, bf16[400,128]{1,0:T(8,128)(2,1)S(1)}, u32[]{:S(2)}, u32[]{:S(2)}) collective-permute-start(bf16[400,128]{1,0:T(8,128)(2,1)S(1)} %get-tuple-element.69), channel_id=1, source_target_pairs={{0,2},{1,3},{2,4},{3,5},{4,6},{5,7},{6,0},{7,1},{8,10},{9,11},{10,... | collective-permute-start | bytes 307208 | tf_op jit(solution)/shard_map/ppermute | solution.py:720
  8.8 14.2 %collective-permute-start.2 = (bf16[400,128]{1,0:T(8,128)(2,1)S(1)}, bf16[400,128]{1,0:T(8,128)(2,1)S(1)}, u32[]{:S(2)}, u32[]{:S(2)}) collective-permute-start(bf16[400,128]{1,0:T(8,128)(2,1)S(1)} %get-tuple-element.70), channel_id=1, source_target_pairs={{0,3},{1,4},{2,5},{3,6},{4,7},{5,0},{6,1},{7,2},{8,11},{9,12},{10,... | collective-permute-start | bytes 307208 | tf_op jit(solution)/shard_map/ppermute | solution.py:720
  11.4 11.7 %collective-permute-start.3 = (bf16[400,128]{1,0:T(8,128)(2,1)S(1)}, bf16[400,128]{1,0:T(8,128)(2,1)S(1)}, u32[]{:S(2)}, u32[]{:S(2)}) collective-permute-start(bf16[400,128]{1,0:T(8,128)(2,1)S(1)} %get-tuple-element.71), channel_id=1, source_target_pairs={{0,4},{1,5},{2,6},{3,7},{4,0},{5,1},{6,2},{7,3},{8,12},{9,13},{10,... | collective-permute-start | bytes 307208 | tf_op jit(solution)/shard_map/ppermute | solution.py:720
  12.6 10.5 %collective-permute-start.4 = (bf16[400,128]{1,0:T(8,128)(2,1)S(1)}, bf16[400,128]{1,0:T(8,128)(2,1)S(1)}, u32[]{:S(2)}, u32[]{:S(2)}) collective-permute-start(bf16[400,128]{1,0:T(8,128)(2,1)S(1)} %get-tuple-element.72), channel_id=1, source_target_pairs={{0,5},{1,6},{2,7},{3,0},{4,1},{5,2},{6,3},{7,4},{8,13},{9,14},{10,... | collective-permute-start | bytes 307208 | tf_op jit(solution)/shard_map/ppermute | solution.py:720
  15.2 7.8 %collective-permute-start.5 = (bf16[400,128]{1,0:T(8,128)(2,1)S(1)}, bf16[400,128]{1,0:T(8,128)(2,1)S(1)}, u32[]{:S(2)}, u32[]{:S(2)}) collective-permute-start(bf16[400,128]{1,0:T(8,128)(2,1)S(1)} %get-tuple-element.73), channel_id=1, source_target_pairs={{0,6},{1,7},{2,0},{3,1},{4,2},{5,3},{6,4},{7,5},{8,14},{9,15},{10,... | collective-permute-start | bytes 307208 | tf_op jit(solution)/shard_map/ppermute | solution.py:720
  16.6 6.5 %collective-permute-start.6 = (bf16[400,128]{1,0:T(8,128)(2,1)S(1)}, bf16[400,128]{1,0:T(8,128)(2,1)S(1)}, u32[]{:S(2)}, u32[]{:S(2)}) collective-permute-start(bf16[400,128]{1,0:T(8,128)(2,1)S(1)} %get-tuple-element.74), channel_id=1, source_target_pairs={{0,7},{1,0},{2,1},{3,2},{4,3},{5,4},{6,5},{7,6},{8,15},{9,8},{10,9... | collective-permute-start | bytes 307208 | tf_op jit(solution)/shard_map/ppermute | solution.py:720
  24.4 6.3 %collective-permute-start.7 = (bf16[64,512]{1,0:T(8,128)(2,1)S(1)}, bf16[64,512]{1,0:T(8,128)(2,1)S(1)}, u32[]{:S(2)}, u32[]{:S(2)}) collective-permute-start(bf16[64,512]{1,0:T(8,128)(2,1)S(1)} %get-tuple-element.78), channel_id=1, source_target_pairs={{0,1},{2,3},{4,5},{6,7},{1,0},{3,2},{5,4},{7,6},{8,9},{10,11},{12,... | collective-permute-start | bytes 196616 | tf_op jit(solution)/shard_map/ppermute | solution.py:726
  28.4 2.2 %collective-permute-start.8 = (bf16[64,512]{1,0:T(8,128)(2,1)S(1)}, bf16[64,512]{1,0:T(8,128)(2,1)S(1)}, u32[]{:S(2)}, u32[]{:S(2)}) collective-permute-start(bf16[64,512]{1,0:T(8,128)(2,1)S(1)} %get-tuple-element.79), channel_id=1, source_target_pairs={{1,2},{3,4},{5,6},{2,1},{4,3},{6,5},{9,10},{11,12},{13,14},{10,9},... | collective-permute-start | bytes 196616 | tf_op jit(solution)/shard_map/ppermute | solution.py:726
  49.8 1.0 copy-start.1
  50.8 12.9 %copy-start = (bf16[2048,512]{1,0:T(8,128)(2,1)}, bf16[2048,512]{1,0:T(8,128)(2,1)S(1)}, u32[]{:S(2)}) copy-start(bf16[2048,512]{1,0:T(8,128)(2,1)S(1)} %get-tuple-element.110.pre_grad_hbm) | copy-start | bytes 6291460
  50.8 12.9 %collective-permute-start.18 = (bf16[3584,256]{1,0:T(8,128)(2,1)S(1)}, bf16[3584,256]{1,0:T(8,128)(2,1)S(1)}, u32[]{:S(2)}, u32[]{:S(2)}) collective-permute-start(bf16[3584,256]{1,0:T(8,128)(2,1)S(1)} %get-tuple-element.112), channel_id=1, source_target_pairs={{0,8},{8,0},{16,24},{24,16},{1,9},{9,1},{17,25},{25,17},{2,10},{10... | collective-permute-start | bytes 5505032 | tf_op jit(solution)/shard_map/ppermute | solution.py:532
  52.2 10.3 %collective-permute-start.9 = (bf16[64,512]{1,0:T(8,128)(2,1)S(1)}, bf16[64,512]{1,0:T(8,128)(2,1)S(1)}, u32[]{:S(2)}, u32[]{:S(2)}) collective-permute-start(bf16[64,512]{1,0:T(8,128)(2,1)S(1)} %get-tuple-element.97), channel_id=1, source_target_pairs={{0,1},{2,3},{4,5},{6,7},{1,0},{3,2},{5,4},{7,6},{8,9},{10,11},{12,... | collective-permute-start | bytes 196616 | tf_op jit(solution)/shard_map/ppermute | solution.py:726
  59.7 2.8 %collective-permute-start.10 = (bf16[64,512]{1,0:T(8,128)(2,1)S(1)}, bf16[64,512]{1,0:T(8,128)(2,1)S(1)}, u32[]{:S(2)}, u32[]{:S(2)}) collective-permute-start(bf16[64,512]{1,0:T(8,128)(2,1)S(1)} %get-tuple-element.98), channel_id=1, source_target_pairs={{1,2},{3,4},{5,6},{2,1},{4,3},{6,5},{9,10},{11,12},{13,14},{10,9},... | collective-permute-start | bytes 196616 | tf_op jit(solution)/shard_map/ppermute | solution.py:726
  64.9 23.7 %collective-permute-start.19 = (bf16[8,224,128]{2,1,0:T(8,128)(2,1)S(1)}, bf16[8,224,128]{2,1,0:T(8,128)(2,1)S(1)}, u32[]{:S(2)}, u32[]{:S(2)}) collective-permute-start(bf16[8,224,128]{2,1,0:T(8,128)(2,1)S(1)} %get-tuple-element.117), channel_id=1, source_target_pairs={{0,16},{8,24},{16,0},{24,8},{1,17},{9,25},{17,1},{25,9},{2,18},{10... | collective-permute-start | bytes 1376264 | tf_op jit(solution)/shard_map/ppermute | solution.py:532
  66.5 29.6 %collective-permute-start.21 = (bf16[4,224,256]{2,1,0:T(8,128)(2,1)S(1)}, bf16[4,224,256]{2,1,0:T(8,128)(2,1)S(1)}, u32[]{:S(2)}, u32[]{:S(2)}) collective-permute-start(bf16[4,224,256]{2,1,0:T(8,128)(2,1)S(1)} %get-tuple-element.120), channel_id=1, source_target_pairs={{0,1},{1,0},{2,3},{3,2},{4,5},{5,4},{6,7},{7,6},{8,9},{9,8},{10,11... | collective-permute-start | bytes 1376264 | tf_op jit(solution)/shard_map/ppermute | solution.py:532
  71.3 6.8 %collective-permute-start.13 = (bf16[384,128]{1,0:T(8,128)(2,1)S(1)}, bf16[384,128]{1,0:T(8,128)(2,1)S(1)}, u32[]{:S(2)}, u32[]{:S(2)}) collective-permute-start(bf16[384,128]{1,0:T(8,128)(2,1)S(1)} %get-tuple-element.103), channel_id=1, source_target_pairs={{0,5},{1,6},{2,7},{3,0},{4,1},{5,2},{6,3},{7,4},{8,13},{9,14},{10,... | collective-permute-start | bytes 294920 | tf_op jit(solution)/shard_map/ppermute | solution.py:720
  75.0 11.6 %collective-permute-start.14 = (bf16[384,128]{1,0:T(8,128)(2,1)S(1)}, bf16[384,128]{1,0:T(8,128)(2,1)S(1)}, u32[]{:S(2)}, u32[]{:S(2)}) collective-permute-start(bf16[384,128]{1,0:T(8,128)(2,1)S(1)} %get-tuple-element.104), channel_id=1, source_target_pairs={{0,4},{1,5},{2,6},{3,7},{4,0},{5,1},{6,2},{7,3},{8,12},{9,13},{10,... | collective-permute-start | bytes 294920 | tf_op jit(solution)/shard_map/ppermute | solution.py:720
  75.0 12.4 %collective-permute-start.15 = (bf16[384,128]{1,0:T(8,128)(2,1)S(1)}, bf16[384,128]{1,0:T(8,128)(2,1)S(1)}, u32[]{:S(2)}, u32[]{:S(2)}) collective-permute-start(bf16[384,128]{1,0:T(8,128)(2,1)S(1)} %get-tuple-element.105), channel_id=1, source_target_pairs={{0,3},{1,4},{2,5},{3,6},{4,7},{5,0},{6,1},{7,2},{8,11},{9,12},{10,... | collective-permute-start | bytes 294920 | tf_op jit(solution)/shard_map/ppermute | solution.py:720
  78.1 11.3 %collective-permute-start.11 = (bf16[384,128]{1,0:T(8,128)(2,1)S(1)}, bf16[384,128]{1,0:T(8,128)(2,1)S(1)}, u32[]{:S(2)}, u32[]{:S(2)}) collective-permute-start(bf16[384,128]{1,0:T(8,128)(2,1)S(1)} %get-tuple-element.101), channel_id=1, source_target_pairs={{0,7},{1,0},{2,1},{3,2},{4,3},{5,4},{6,5},{7,6},{8,15},{9,8},{10,9... | collective-permute-start | bytes 294920 | tf_op jit(solution)/shard_map/ppermute | solution.py:720
  86.6 5.7 %collective-permute-start.12 = (bf16[384,128]{1,0:T(8,128)(2,1)S(1)}, bf16[384,128]{1,0:T(8,128)(2,1)S(1)}, u32[]{:S(2)}, u32[]{:S(2)}) collective-permute-start(bf16[384,128]{1,0:T(8,128)(2,1)S(1)} %get-tuple-element.102), channel_id=1, source_target_pairs={{0,6},{1,7},{2,0},{3,1},{4,2},{5,3},{6,4},{7,5},{8,14},{9,15},{10,... | collective-permute-start | bytes 294920 | tf_op jit(solution)/shard_map/ppermute | solution.py:720
  87.4 6.4 %collective-permute-start.16 = (bf16[384,128]{1,0:T(8,128)(2,1)S(1)}, bf16[384,128]{1,0:T(8,128)(2,1)S(1)}, u32[]{:S(2)}, u32[]{:S(2)}) collective-permute-start(bf16[384,128]{1,0:T(8,128)(2,1)S(1)} %get-tuple-element.106), channel_id=1, source_target_pairs={{0,2},{1,3},{2,4},{3,5},{4,6},{5,7},{6,0},{7,1},{8,10},{9,11},{10,... | collective-permute-start | bytes 294920 | tf_op jit(solution)/shard_map/ppermute | solution.py:720
  88.6 7.4 %collective-permute-start.17 = (bf16[384,128]{1,0:T(8,128)(2,1)S(1)}, bf16[384,128]{1,0:T(8,128)(2,1)S(1)}, u32[]{:S(2)}, u32[]{:S(2)}) collective-permute-start(bf16[384,128]{1,0:T(8,128)(2,1)S(1)} %get-tuple-element.107), channel_id=1, source_target_pairs={{0,1},{1,2},{2,3},{3,4},{4,5},{5,6},{6,7},{7,0},{8,9},{9,10},{10,1... | collective-permute-start | bytes 294920 | tf_op jit(solution)/shard_map/ppermute | solution.py:720
  89.4 12.9 %collective-permute-start.20 = (bf16[4,224,128]{2,1,0:T(8,128)(2,1)S(1)}, bf16[4,224,128]{2,1,0:T(8,128)(2,1)S(1)}, u32[]{:S(2)}, u32[]{:S(2)}) collective-permute-start(bf16[4,224,128]{2,1,0:T(8,128)(2,1)S(1)} %get-tuple-element.119), channel_id=1, source_target_pairs={{0,1},{1,0},{2,3},{3,2},{4,5},{5,4},{6,7},{7,6},{8,9},{9,8},{10,11... | collective-permute-start | bytes 688136 | tf_op jit(solution)/shard_map/ppermute | solution.py:532
  96.8 6.1 %collective-permute-start.22 = (bf16[4,224,128]{2,1,0:T(8,128)(2,1)S(1)}, bf16[4,224,128]{2,1,0:T(8,128)(2,1)S(1)}, u32[]{:S(2)}, u32[]{:S(2)}) collective-permute-start(bf16[4,224,128]{2,1,0:T(8,128)(2,1)S(1)} %get-tuple-element.122), channel_id=1, source_target_pairs={{0,16},{8,24},{16,0},{24,8},{1,17},{9,25},{17,1},{25,9},{2,18},{10... | collective-permute-start | bytes 688136 | tf_op jit(solution)/shard_map/ppermute | solution.py:532
  97.4 10.9 %copy-start.4 = (s32[1,512]{1,0:T(1,128)S(1)}, s32[1,512]{1,0:T(1,128)}, u32[]{:S(2)}) copy-start(s32[1,512]{1,0:T(1,128)} %index_ref.3) | copy-start | bytes 6148
  103.8 7.4 %collective-permute-start.23 = (bf16[448,128]{1,0:T(8,128)(2,1)S(1)}, bf16[448,128]{1,0:T(8,128)(2,1)S(1)}, u32[]{:S(2)}, u32[]{:S(2)}) collective-permute-start(bf16[448,128]{1,0:T(8,128)(2,1)S(1)} %get-tuple-element.125), channel_id=1, source_target_pairs={{0,6},{1,7},{2,4},{3,5},{4,2},{5,3},{6,0},{7,1},{8,14},{9,15},{10,... | collective-permute-start | bytes 344072 | tf_op jit(solution)/shard_map/ppermute | solution.py:532
  105.5 9.3 %collective-permute-start.24 = (bf16[448,128]{1,0:T(8,128)(2,1)S(1)}, bf16[448,128]{1,0:T(8,128)(2,1)S(1)}, u32[]{:S(2)}, u32[]{:S(2)}) collective-permute-start(bf16[448,128]{1,0:T(8,128)(2,1)S(1)} %get-tuple-element.126), channel_id=1, source_target_pairs={{0,4},{1,5},{2,6},{3,7},{4,0},{5,1},{6,2},{7,3},{8,12},{9,13},{10,... | collective-permute-start | bytes 344072 | tf_op jit(solution)/shard_map/ppermute | solution.py:532
  105.7 9.2 %collective-permute-start.25 = (bf16[448,128]{1,0:T(8,128)(2,1)S(1)}, bf16[448,128]{1,0:T(8,128)(2,1)S(1)}, u32[]{:S(2)}, u32[]{:S(2)}) collective-permute-start(bf16[448,128]{1,0:T(8,128)(2,1)S(1)} %get-tuple-element.127), channel_id=1, source_target_pairs={{0,2},{1,3},{2,0},{3,1},{4,6},{5,7},{6,4},{7,5},{8,10},{9,11},{10,... | collective-permute-start | bytes 344072 | tf_op jit(solution)/shard_map/ppermute | solution.py:532
  114.9 4.9 %collective-permute-start.26 = (bf16[448,128]{1,0:T(8,128)(2,1)S(1)}, bf16[448,128]{1,0:T(8,128)(2,1)S(1)}, u32[]{:S(2)}, u32[]{:S(2)}) collective-permute-start(bf16[448,128]{1,0:T(8,128)(2,1)S(1)} %sum.1.mine_ref), channel_id=1, source_target_pairs={{0,16},{8,24},{16,0},{24,8},{1,17},{9,25},{17,1},{25,9},{2,18},{10... | collective-permute-start | bytes 344072 | tf_op jit(solution)/shard_map/ppermute | solution.py:532
  120.3 1.6 %collective-permute-start.27 = (bf16[448,256]{1,0:T(8,128)(2,1)S(1)}, bf16[448,256]{1,0:T(8,128)(2,1)S(1)}, u32[]{:S(2)}, u32[]{:S(2)}) collective-permute-start(bf16[448,256]{1,0:T(8,128)(2,1)S(1)} %join.2.mine_ref), channel_id=1, source_target_pairs={{0,8},{8,0},{16,24},{24,16},{1,9},{9,1},{17,25},{25,17},{2,10},{10... | collective-permute-start | bytes 688136 | tf_op jit(solution)/shard_map/ppermute | solution.py:532

commit v2 on v1

--- a/solution.py
+++ b/solution.py
@@ -74,8 +74,17 @@
     return ahead * LANES + rank.astype(jnp.int32), row
 
 
-def pack_kernel(part_count, capacity, scal, h_ref, index_ref, *outs):
+def pack_kernel(part_count, capacity, scal, h_hbm, index_hbm, *refs):
+    outs = refs[:-3]
+    h_ref, index_ref, sems = refs[-3:]
     cell_count, width = h_ref.shape
+    loads = [
+        pltpu.make_async_copy(index_hbm, index_ref, sems.at[0]),
+        pltpu.make_async_copy(h_hbm, h_ref, sems.at[1]),
+    ]
+    for load in loads:
+        load.start()
+    loads[0].wait()
     chunks = width // LANES
     slot, row = slots_of(index_ref[...], scal[PART], part_count, cell_count)
     kind = iota((16, cell_count), 0)
@@ -83,6 +92,7 @@
         kind == 0, row >> 8, jnp.where(kind == 1, row & 255, jnp.where(kind == 2, 1, 0))
     )
     coded = coded.astype(F32).astype(BF16)
+    loads[1].wait()
     cells = h_ref[...]
     for step in range(part_count):
         pick = hot(iota((LANES, cell_count), 0) + step * LANES == slot)
@@ -126,6 +136,29 @@
     tail = nodes[cell_count - HB :]
     low_ref[...] = jnp.where(odd, head, tail)
     high_ref[...] = jnp.where(odd, tail, head)
+
+
+def spread_rows(wide, base, rows, fan_in):
+    count, width = rows.shape
+    chunks = width // LANES
+    for chunk in range(chunks):
+        for at in range(fan_in):
+            wide[base + chunk, pl.ds(at, count, stride=fan_in), :] = rows[
+                :, chunk * LANES : (chunk + 1) * LANES
+            ]
+    return jnp.concatenate([wide[base + chunk] for chunk in range(chunks)], axis=1)
+
+
+def collect_rows(wide, base, values, fan_in):
+    count = values.shape[0] // fan_in
+    sums = []
+    for chunk in range(values.shape[1] // LANES):
+        wide[base + chunk] = values[:, chunk * LANES : (chunk + 1) * LANES]
+        total = wide[base + chunk, pl.ds(0, count, stride=fan_in), :]
+        for at in range(1, fan_in):
+            total = total + wide[base + chunk, pl.ds(at, count, stride=fan_in), :]
+        sums.append(total)
+    return jnp.concatenate(sums, axis=1)
 
 
 def prep_kernel(
@@ -245,6 +278,7 @@
     inverse_ref,
     summed_ref,
     post_grad_ref,
+    wide_ref,
     out_sems,
 ):
     cell_count, width = nodes_ref.shape
@@ -263,11 +297,10 @@
     cells_ref[HB + cell_count :, :] = jnp.where(odd, high, low)
     table_ref[:padded, :] = dot_nn(cells_ref[...], w_edge_in_ref[width : 2 * width, :]).astype(BF16)
     recv_ref[...] = dot_nn(nodes_ref[...], w_edge_in_ref[2 * width :, :]).astype(BF16)
-    collect = hot(iota((cells, EDGE_BLOCK), 0) == iota((cells, EDGE_BLOCK), 1) // fan_in)
-
-    def forward(step, carry):
-        spot = pl.ds(pl.multiple_of(step * cells, cells), cells)
-        rows = pl.ds(pl.multiple_of(step * EDGE_BLOCK, EDGE_BLOCK), EDGE_BLOCK)
+
+    for step in range(steps):
+        spot = slice(step * cells, (step + 1) * cells)
+        rows = slice(step * EDGE_BLOCK, (step + 1) * EDGE_BLOCK)
         table_ref[padded : padded + cells, :] = recv_ref[spot, :]
         edges = edges_ref[rows, :]
         pre = pre_ref[rows, :] + dot_nn(gather_ref[rows, :], table_ref[...])
@@ -280,10 +313,8 @@
         inverse_ref[rows, :] = inverse
         edge_new = (edges.astype(F32) + normed).astype(BF16)
         post_grad_ref[rows, :] = edge_new
-        summed_ref[spot, :] = dot_nn(collect, edge_new).astype(BF16)
-        return carry
-
-    lax.fori_loop(0, steps, forward, 0, unroll=True)
+        summed_ref[spot, :] = collect_rows(wide_ref, 0, edge_new.astype(F32), fan_in).astype(BF16)
+
     edge_store = pltpu.make_async_copy(post_grad_ref, edge_new_hbm, out_sems.at[0])
     edge_store.start()
     nodes = nodes_ref[...]
@@ -300,39 +331,30 @@
     node_slope = node_gate * (1.0 + node_pre * (1.0 - node_gate))
     node_pre_grad = (dot_nt(node_post_grad, w_node_out_ref[...]) * node_slope).astype(BF16)
     summed_grad = dot_nt(node_pre_grad, w_node_in_ref[width:, :])
-    high = summed_grad.astype(BF16)
-    low = (summed_grad - high.astype(F32)).astype(BF16)
-    for block in range(steps):
-        at = slice(block * cells, (block + 1) * cells)
-        summed_grad_ref[2 * block * cells : (2 * block + 1) * cells, :] = high[at]
-        summed_grad_ref[(2 * block + 1) * cells : 2 * (block + 1) * cells, :] = low[at]
+    summed_grad_ref[...] = summed_grad
     summed_store = pltpu.make_async_copy(summed_grad_ref, summed_grad_hbm, out_sems.at[2])
     summed_store.start()
     base_ref[...] = upstream + dot_nt(node_pre_grad, w_node_in_ref[:width, :])
-    member = iota((EDGE_BLOCK, 2 * cells), 1)
-    owner = iota((EDGE_BLOCK, 2 * cells), 0) // fan_in
-    spread = hot((owner == member) | (owner + cells == member))
-
     edge_store.wait()
-
-    def backward(step, carry):
-        spot = pl.ds(pl.multiple_of(step * cells, cells), cells)
-        pair = pl.ds(pl.multiple_of(step * 2 * cells, 2 * cells), 2 * cells)
-        rows = pl.ds(pl.multiple_of(step * EDGE_BLOCK, EDGE_BLOCK), EDGE_BLOCK)
-        upstream = cot_edges_ref[rows, :].astype(F32) + dot_nn(spread, summed_grad_ref[pair, :])
+    for step in range(steps):
+        spot = slice(step * cells, (step + 1) * cells)
+        rows = slice(step * EDGE_BLOCK, (step + 1) * EDGE_BLOCK)
+        base = (step % 2) * (width // LANES)
+        upstream = cot_edges_ref[rows, :].astype(F32) + spread_rows(
+            wide_ref, base, summed_grad_ref[spot, :], fan_in
+        )
         post_grad = normalize_back(
             normed_ref[rows, :].astype(F32), inverse_ref[rows, :], upstream
         )
         post_grad = post_grad.astype(BF16)
         post_grad_ref[rows, :] = post_grad
-        pre_grad = (dot_nt(post_grad, w_edge_out_ref[...]) * slope_ref[rows, :].astype(F32)).astype(
-            BF16
-        )
+        pre_grad = dot_nt(post_grad, w_edge_out_ref[...]) * slope_ref[rows, :].astype(F32)
+        pre_grad = pre_grad.astype(BF16)
         pre_grad_ref[rows, :] = pre_grad
-        received_ref[spot, :] = dot_nn(collect, pre_grad).astype(BF16)
-        return carry
-
-    lax.fori_loop(0, steps, backward, 0, unroll=True)
+        received_ref[spot, :] = collect_rows(
+            wide_ref, base, pre_grad.astype(F32), fan_in
+        ).astype(BF16)
+
     pre_store = pltpu.make_async_copy(pre_grad_ref, pre_grad_hbm, out_sems.at[3])
     pre_store.start()
     first = scal[CORE] == 0
@@ -401,6 +423,7 @@
     pre_grad_ref,
     w_edge_ref,
     grad_edge_ref,
+    wide_ref,
     in_sems,
     out_sems,
 ):
@@ -422,18 +445,16 @@
     for load in loads:
         load.start()
     token_ref[...] = jnp.zeros(token_ref.shape, F32)
-    member = iota((EDGE_BLOCK, 2 * cells), 1)
-    owner = iota((EDGE_BLOCK, 2 * cells), 0) // fan_in
-    spread = hot((owner == member) | (owner + cells == member))
     loads[0].wait()
     loads[1].wait()
     stores = []
     for step in range(steps):
         rows = slice(step * EDGE_BLOCK, (step + 1) * EDGE_BLOCK)
-        pair = slice(step * 2 * cells, (step + 1) * 2 * cells)
         loads[2 + 2 * step].wait()
         loads[3 + 2 * step].wait()
-        upstream = cot_ref[rows, :].astype(F32) + dot_nn(spread, summed_grad_ref[pair, :])
+        upstream = cot_ref[rows, :].astype(F32) + spread_rows(
+            wide_ref, 0, summed_grad_ref[step * cells : (step + 1) * cells, :], fan_in
+        )
         grad_edge_ref[rows, :] = (
             upstream + dot_nt(pre_grad_ref[rows, :], w_edge_ref[...])
         ).astype(BF16)
@@ -808,8 +829,8 @@
         out_shape=[
             shape(by_edge),
             shape(by_cell),
-            shape(by_edge),
-            shape((2 * cell_count, width)),
+            pltpu.HBM(by_edge, BF16),
+            pltpu.HBM(by_cell, F32),
             near_shape((padded, width)),
             near_shape(by_cell),
             near_shape(by_cell, F32),
@@ -820,7 +841,7 @@
         out_specs=[far] * 4 + [near] * 5,
         scratch_shapes=[
             VMEM(by_edge, BF16),
-            VMEM((2 * cell_count, width), BF16),
+            VMEM(by_cell, F32),
             VMEM(by_cell, BF16),
             VMEM((padded, width), BF16),
             VMEM((padded + cells, width), BF16),
@@ -831,6 +852,7 @@
             VMEM((edge_count, 1), F32),
             VMEM(by_cell, BF16),
             VMEM(by_edge, BF16),
+            VMEM((2 * width // LANES, EDGE_BLOCK, LANES), F32),
             pltpu.SemaphoreType.DMA((4,)),
         ],
         compiler_params=params(MAIN_LIMIT),
@@ -850,10 +872,11 @@
         out_specs=[far, pl.BlockSpec(memory_space=VMEM)],
         scratch_shapes=[
             VMEM((edge_count, width), BF16),
-            VMEM(summed_grad.shape, BF16),
+            VMEM(summed_grad.shape, F32),
             VMEM((edge_count, width), BF16),
             VMEM((width, width), BF16),
             VMEM((edge_count, width), BF16),
+            VMEM((width // LANES, EDGE_BLOCK, LANES), F32),
             pltpu.SemaphoreType.DMA((2 + 2 * steps,)),
             pltpu.SemaphoreType.DMA((steps,)),
         ],
@@ -898,11 +921,16 @@
     sends = pl.pallas_call(
         functools.partial(pack_kernel, part_count, capacity),
         out_shape=[shape((block_rows + 16, LANES))] * part_count + [near_shape((8, LANES), F32)],
-        in_specs=[scalars()] + whole(2),
+        in_specs=[scalars()] + [pl.BlockSpec(memory_space=pltpu.HBM)] * 2,
         out_specs=whole(part_count + 1),
+        scratch_shapes=[
+            VMEM((cell_count, width), BF16),
+            VMEM((1, cell_count), jnp.int32),
+            pltpu.SemaphoreType.DMA((2,)),
+        ],
         compiler_params=params(24),
         name="pack",
-    )(scal, h_in[0], new_index)
+    )(scal, pinned(h_in[0]), pinned(new_index))
     prepared = run_prep(
         fan_in,
         cell_count,

time: 124 us -> 119 us (0.960)
  local copies, waits for them, and re-layouts: 2.79 us -> 0.09 us
  Pallas kernels: 42.8 us -> 41 us
    unnamed x10 -> x2, local copies, waits for them, and re-layouts: 2.71 us -> 0.01 us
    pallas_call x1, Pallas kernels: 19.1 us -> 16.8 us  [run_main(): pl.pallas_call(functools.partial(main_kernel, fan_in, scale), out_shape=[...]
where the time goes in v2:
time: 119 us
  starting transfers between devices  56.7 us (48%)
  Pallas kernels  41 us (34%)
  waiting for transfers between devices  20.4 us (17%)
    ppermute x14, starting transfers between devices, shift(): lax.ppermute(value, 'dom', [(at, (at + steps) % count) for at in range(co...  28.7 us
    pallas_call x1, Pallas kernels, run_main(): pl.pallas_call(functools.partial(main_kernel, fan_in, scale), out_shape=[...  16.8 us
    ppermute x10, starting transfers between devices, swap(): return lax.ppermute(value, axis, [(at, at ^ bit) for at in range(count)])  14.9 us
    ppermute x4, starting transfers between devices, neighbour(): lax.ppermute(value, 'dom', pairs + [(right, left) for left, right in pairs])  13 us
    ppermute x10, waiting for transfers between devices, swap(): return lax.ppermute(value, axis, [(at, at ^ bit) for at in range(count)])  10.3 us
    ppermute x14, waiting for transfers between devices, shift(): lax.ppermute(value, 'dom', [(at, (at + steps) % count) for at in range(co...  6.61 us
    pallas_call x1, Pallas kernels, run_prep(): pl.pallas_call(functools.partial(prep_kernel, fan_in, cell_count), out_sh...  5.01 us
    pallas_call x1, Pallas kernels, run_edges(): pl.pallas_call(functools.partial(edge_kernel, fan_in), out_shape=[shape((...  4.5 us
  transfers between devices with their start and end apart: 28, of which 13 were waited for; matrix products, arithmetic and copies ran while one was open for 0% of the time, Pallas kernels for 13%

profile of v2, /device:TPU:0, one launch (start us, length us, event | category | flops | bytes accessed | tf_op | source)
XLA Modules:
  0.0 119.0 jit_solution(16670172656279929776)
XLA Ops:
  0.8 2.6 %pack.1 = (bf16[400,128]{1,0:T(8,128)(2,1)S(1)}, bf16[400,128]{1,0:T(8,128)(2,1)S(1)}, bf16[400,128]{1,0:T(8,128)(2,1)S(1)}, bf16[400,128]{1,0:T(8,128)(2,1)S(1)...) custom-call(s32[5]{0:T(128)S(1)} %stack.23.scal.refs_8_, ...), custom_call_target="tpu_custom_call" | custom-call | tf_op jit(solution)/shard_map/pack/pallas_call | solution.py:921
  3.4 3.0 %collective-permute-start = (bf16[400,128]{1,0:T(8,128)(2,1)S(1)}, bf16[400,128]{1,0:T(8,128)(2,1)S(1)}, u32[]{:S(2)}, u32[]{:S(2)}) collective-permute-start(bf16[400,128]{1,0:T(8,128)(2,1)S(1)} %get-tuple-element.68), channel_id=1, source_target_pairs={{0,1},{1,2},{2,3},{3,4},{4,5},{5,6},{6,7},{7,0},{8,9},{9,10},{10,1... | collective-permute-start | bytes 307208 | tf_op jit(solution)/shard_map/ppermute | solution.py:741
  6.4 1.6 %collective-permute-start.1 = (bf16[400,128]{1,0:T(8,128)(2,1)S(1)}, bf16[400,128]{1,0:T(8,128)(2,1)S(1)}, u32[]{:S(2)}, u32[]{:S(2)}) collective-permute-start(bf16[400,128]{1,0:T(8,128)(2,1)S(1)} %get-tuple-element.69), channel_id=1, source_target_pairs={{0,2},{1,3},{2,4},{3,5},{4,6},{5,7},{6,0},{7,1},{8,10},{9,11},{10,... | collective-permute-start | bytes 307208 | tf_op jit(solution)/shard_map/ppermute | solution.py:741
  8.0 2.5 %collective-permute-start.2 = (bf16[400,128]{1,0:T(8,128)(2,1)S(1)}, bf16[400,128]{1,0:T(8,128)(2,1)S(1)}, u32[]{:S(2)}, u32[]{:S(2)}) collective-permute-start(bf16[400,128]{1,0:T(8,128)(2,1)S(1)} %get-tuple-element.70), channel_id=1, source_target_pairs={{0,3},{1,4},{2,5},{3,6},{4,7},{5,0},{6,1},{7,2},{8,11},{9,12},{10,... | collective-permute-start | bytes 307208 | tf_op jit(solution)/shard_map/ppermute | solution.py:741
  10.5 1.2 %collective-permute-start.3 = (bf16[400,128]{1,0:T(8,128)(2,1)S(1)}, bf16[400,128]{1,0:T(8,128)(2,1)S(1)}, u32[]{:S(2)}, u32[]{:S(2)}) collective-permute-start(bf16[400,128]{1,0:T(8,128)(2,1)S(1)} %get-tuple-element.71), channel_id=1, source_target_pairs={{0,4},{1,5},{2,6},{3,7},{4,0},{5,1},{6,2},{7,3},{8,12},{9,13},{10,... | collective-permute-start | bytes 307208 | tf_op jit(solution)/shard_map/ppermute | solution.py:741
  11.8 2.7 %collective-permute-start.4 = (bf16[400,128]{1,0:T(8,128)(2,1)S(1)}, bf16[400,128]{1,0:T(8,128)(2,1)S(1)}, u32[]{:S(2)}, u32[]{:S(2)}) collective-permute-start(bf16[400,128]{1,0:T(8,128)(2,1)S(1)} %get-tuple-element.72), channel_id=1, source_target_pairs={{0,5},{1,6},{2,7},{3,0},{4,1},{5,2},{6,3},{7,4},{8,13},{9,14},{10,... | collective-permute-start | bytes 307208 | tf_op jit(solution)/shard_map/ppermute | solution.py:741
  14.4 1.3 %collective-permute-start.5 = (bf16[400,128]{1,0:T(8,128)(2,1)S(1)}, bf16[400,128]{1,0:T(8,128)(2,1)S(1)}, u32[]{:S(2)}, u32[]{:S(2)}) collective-permute-start(bf16[400,128]{1,0:T(8,128)(2,1)S(1)} %get-tuple-element.73), channel_id=1, source_target_pairs={{0,6},{1,7},{2,0},{3,1},{4,2},{5,3},{6,4},{7,5},{8,14},{9,15},{10,... | collective-permute-start | bytes 307208 | tf_op jit(solution)/shard_map/ppermute | solution.py:741
  15.8 1.4 %collective-permute-start.6 = (bf16[400,128]{1,0:T(8,128)(2,1)S(1)}, bf16[400,128]{1,0:T(8,128)(2,1)S(1)}, u32[]{:S(2)}, u32[]{:S(2)}) collective-permute-start(bf16[400,128]{1,0:T(8,128)(2,1)S(1)} %get-tuple-element.74), channel_id=1, source_target_pairs={{0,7},{1,0},{2,1},{3,2},{4,3},{5,4},{6,5},{7,6},{8,15},{9,8},{10,9... | collective-permute-start | bytes 307208 | tf_op jit(solution)/shard_map/ppermute | solution.py:741
  17.2 5.0 %prep.1 = (bf16[2048,512]{1,0:T(8,128)(2,1)S(1)}, bf16[512,512]{1,0:T(8,128)(2,1)S(1)}, bf16[2048,512]{1,0:T(8,128)(2,1)S(1)}, bf16[1536,512]{1,0:T(8,128)(2,1)S...) custom-call(s32[5]{0:T(128)S(1)} %stack.23.scal.refs_8_, ...), custom_call_target="tpu_custom_call" | custom-call | flops 2147483648 | bytes 20971520 | tf_op jit(solution)/shard_map/prep/pallas_call | solution.py:780
  22.3 1.3 %unpack.1 = (bf16[512,512]{1,0:T(8,128)(2,1)S(1)}, bf16[64,512]{1,0:T(8,128)(2,1)S(1)}, bf16[64,512]{1,0:T(8,128)(2,1)S(1)}, bf16[128,128]{1,0:T(8,128)(2,1)S(1)}) custom-call(bf16[400,128]{1,0:T(8,128)(2,1)S(1)} %get-tuple-element.67.refs_0_, bf16[400,128]{1,0:T(8,128)(2,1)S(1)} %collective-permute-done.refs_1_, ...), custom_call_target="tpu_custom_call" | custom-call | tf_op jit(solution)/shard_map/unpack/pallas_call | solution.py:951
  23.6 4.0 %collective-permute-start.7 = (bf16[64,512]{1,0:T(8,128)(2,1)S(1)}, bf16[64,512]{1,0:T(8,128)(2,1)S(1)}, u32[]{:S(2)}, u32[]{:S(2)}) collective-permute-start(bf16[64,512]{1,0:T(8,128)(2,1)S(1)} %get-tuple-element.78), channel_id=1, source_target_pairs={{0,1},{2,3},{4,5},{6,7},{1,0},{3,2},{5,4},{7,6},{8,9},{10,11},{12,... | collective-permute-start | bytes 196616 | tf_op jit(solution)/shard_map/ppermute | solution.py:747
  27.6 0.8 collective-permute-start.8
  28.5 1.4 %collective-permute-done.7.low_ref = bf16[64,512]{1,0:T(8,128)(2,1)S(1)} collective-permute-done((bf16[64,512]{1,0:T(8,128)(2,1)S(1)}, bf16[64,512]{1,0:T(8,128)(2,1)S(1)}, u32[]{:S(2)}, u32[]{:S(2)}) %collective-permute-start.7) | collective-permute-done | bytes 65568 | tf_op jit(solution)/shard_map/ppermute | solution.py:747
  29.9 16.8 %main.1 = (bf16[2048,512]{1,0:T(8,128)(2,1)}, bf16[512,512]{1,0:T(8,128)(2,1)}, bf16[2048,512]{1,0:T(8,128)(2,1)}, f32[512,512]{1,0:T(8,128)}, bf16[640,512]{1,0...) custom-call(s32[5]{0:T(128)S(1)} %stack.23.scal.refs_8_, ...), custom_call_target="tpu_custom_call" | custom-call | flops 15032385536 | bytes 16777216 | tf_op jit(solution)/shard_map/main/pallas_call | solution.py:827
  46.7 1.3 %cells.1 = (bf16[64,512]{1,0:T(8,128)(2,1)S(1)}, bf16[64,512]{1,0:T(8,128)(2,1)S(1)}, bf16[512,512]{1,0:T(8,128)(2,1)S(1)}, f32[128,512]{1,0:T(8,128)S(1)}) custom-call(s32[5]{0:T(128)S(1)} %stack.23.scal.refs_8_, bf16[640,512]{1,0:T(8,128)(2,1)S(1)} %get-tuple-element.92.sent_ref, bf16[512,512]{1,0:T(8,128)(2,1)S(1)} %get-tuple-element.93.received_ref, ...), custom_call_target="tpu_custom_call" | custom-call | flops 402653184 | bytes 3145728 | tf_op jit(solution)/shard_map/cells/pallas_call | solution.py:982
  48.1 7.5 %collective-permute-start.9 = (bf16[64,512]{1,0:T(8,128)(2,1)S(1)}, bf16[64,512]{1,0:T(8,128)(2,1)S(1)}, u32[]{:S(2)}, u32[]{:S(2)}) collective-permute-start(bf16[64,512]{1,0:T(8,128)(2,1)S(1)} %get-tuple-element.97), channel_id=1, source_target_pairs={{0,1},{2,3},{4,5},{6,7},{1,0},{3,2},{5,4},{7,6},{8,9},{10,11},{12,... | collective-permute-start | bytes 196616 | tf_op jit(solution)/shard_map/ppermute | solution.py:747
  55.6 0.7 collective-permute-start.10
  56.3 2.1 %collective-permute-done.9.low_ref = bf16[64,512]{1,0:T(8,128)(2,1)S(1)} collective-permute-done((bf16[64,512]{1,0:T(8,128)(2,1)S(1)}, bf16[64,512]{1,0:T(8,128)(2,1)S(1)}, u32[]{:S(2)}, u32[]{:S(2)}) %collective-permute-start.9) | collective-permute-done | bytes 65568 | tf_op jit(solution)/shard_map/ppermute | solution.py:747
  58.4 1.3 %returning.1 = (bf16[384,128]{1,0:T(8,128)(2,1)S(1)}, bf16[384,128]{1,0:T(8,128)(2,1)S(1)}, bf16[384,128]{1,0:T(8,128)(2,1)S(1)}, bf16[384,128]{1,0:T(8,128)(2,1...) custom-call(s32[5]{0:T(128)S(1)} %stack.23.scal.refs_8_, ...), custom_call_target="tpu_custom_call" | custom-call | flops 1 | bytes 1 | tf_op jit(solution)/shard_map/returning/pallas_call | solution.py:998
  59.7 1.1 core.1
  60.8 1.6 %collective-permute-start.19 = (bf16[8,224,128]{2,1,0:T(8,128)(2,1)S(1)}, bf16[8,224,128]{2,1,0:T(8,128)(2,1)S(1)}, u32[]{:S(2)}, u32[]{:S(2)}) collective-permute-start(bf16[8,224,128]{2,1,0:T(8,128)(2,1)S(1)} %get-tuple-element.117), channel_id=1, source_target_pairs={{0,16},{8,24},{16,0},{24,8},{1,17},{9,25},{17,1},{25,9},{2,18},{10... | collective-permute-start | bytes 1376264 | tf_op jit(solution)/shard_map/ppermute | solution.py:553
  62.4 4.8 %collective-permute-start.21 = (bf16[4,224,256]{2,1,0:T(8,128)(2,1)S(1)}, bf16[4,224,256]{2,1,0:T(8,128)(2,1)S(1)}, u32[]{:S(2)}, u32[]{:S(2)}) collective-permute-start(bf16[4,224,256]{2,1,0:T(8,128)(2,1)S(1)} %get-tuple-element.120), channel_id=1, source_target_pairs={{0,1},{1,0},{2,3},{3,2},{4,5},{5,4},{6,7},{7,6},{8,9},{9,8},{10,11... | collective-permute-start | bytes 1376264 | tf_op jit(solution)/shard_map/ppermute | solution.py:553
  67.2 3.7 %collective-permute-start.13 = (bf16[384,128]{1,0:T(8,128)(2,1)S(1)}, bf16[384,128]{1,0:T(8,128)(2,1)S(1)}, u32[]{:S(2)}, u32[]{:S(2)}) collective-permute-start(bf16[384,128]{1,0:T(8,128)(2,1)S(1)} %get-tuple-element.103), channel_id=1, source_target_pairs={{0,5},{1,6},{2,7},{3,0},{4,1},{5,2},{6,3},{7,4},{8,13},{9,14},{10,... | collective-permute-start | bytes 294920 | tf_op jit(solution)/shard_map/ppermute | solution.py:741
  70.9 2.9 %collective-permute-start.15 = (bf16[384,128]{1,0:T(8,128)(2,1)S(1)}, bf16[384,128]{1,0:T(8,128)(2,1)S(1)}, u32[]{:S(2)}, u32[]{:S(2)}) collective-permute-start(bf16[384,128]{1,0:T(8,128)(2,1)S(1)} %get-tuple-element.105), channel_id=1, source_target_pairs={{0,3},{1,4},{2,5},{3,6},{4,7},{5,0},{6,1},{7,2},{8,11},{9,12},{10,... | collective-permute-start | bytes 294920 | tf_op jit(solution)/shard_map/ppermute | solution.py:741
  74.0 7.1 %collective-permute-start.11 = (bf16[384,128]{1,0:T(8,128)(2,1)S(1)}, bf16[384,128]{1,0:T(8,128)(2,1)S(1)}, u32[]{:S(2)}, u32[]{:S(2)}) collective-permute-start(bf16[384,128]{1,0:T(8,128)(2,1)S(1)} %get-tuple-element.101), channel_id=1, source_target_pairs={{0,7},{1,0},{2,1},{3,2},{4,3},{5,4},{6,5},{7,6},{8,15},{9,8},{10,9... | collective-permute-start | bytes 294920 | tf_op jit(solution)/shard_map/ppermute | solution.py:741
  81.1 1.4 %collective-permute-done.14.refs_4_.refs_0_ = bf16[384,128]{1,0:T(8,128)(2,1)S(1)} collective-permute-done((bf16[384,128]{1,0:T(8,128)(2,1)S(1)}, bf16[384,128]{1,0:T(8,128)(2,1)S(1)}, u32[]{:S(2)}, u32[]{:S(2)}) %collective-permute-start.14) | collective-permute-done | bytes 98336 | tf_op jit(solution)/shard_map/ppermute | solution.py:741
  82.5 0.8 collective-permute-done.15.refs_5_.refs_2_
  83.3 1.2 %collective-permute-start.16 = (bf16[384,128]{1,0:T(8,128)(2,1)S(1)}, bf16[384,128]{1,0:T(8,128)(2,1)S(1)}, u32[]{:S(2)}, u32[]{:S(2)}) collective-permute-start(bf16[384,128]{1,0:T(8,128)(2,1)S(1)} %get-tuple-element.106), channel_id=1, source_target_pairs={{0,2},{1,3},{2,4},{3,5},{4,6},{5,7},{6,0},{7,1},{8,10},{9,11},{10,... | collective-permute-start | bytes 294920 | tf_op jit(solution)/shard_map/ppermute | solution.py:741
  84.5 0.8 stage.2
  85.3 2.4 %collective-permute-start.20 = (bf16[4,224,128]{2,1,0:T(8,128)(2,1)S(1)}, bf16[4,224,128]{2,1,0:T(8,128)(2,1)S(1)}, u32[]{:S(2)}, u32[]{:S(2)}) collective-permute-start(bf16[4,224,128]{2,1,0:T(8,128)(2,1)S(1)} %get-tuple-element.119), channel_id=1, source_target_pairs={{0,1},{1,0},{2,3},{3,2},{4,5},{5,4},{6,7},{7,6},{8,9},{9,8},{10,11... | collective-permute-start | bytes 688136 | tf_op jit(solution)/shard_map/ppermute | solution.py:553
  87.7 0.5 collective-permute-done.12.refs_2_.refs_3_
  88.1 1.5 %collective-permute-done.16.refs_6_.refs_4_ = bf16[384,128]{1,0:T(8,128)(2,1)S(1)} collective-permute-done((bf16[384,128]{1,0:T(8,128)(2,1)S(1)}, bf16[384,128]{1,0:T(8,128)(2,1)S(1)}, u32[]{:S(2)}, u32[]{:S(2)}) %collective-permute-start.16) | collective-permute-done | bytes 98336 | tf_op jit(solution)/shard_map/ppermute | solution.py:741
  89.7 2.2 %collective-permute-done.17.refs_7_.refs_6_ = bf16[384,128]{1,0:T(8,128)(2,1)S(1)} collective-permute-done((bf16[384,128]{1,0:T(8,128)(2,1)S(1)}, bf16[384,128]{1,0:T(8,128)(2,1)S(1)}, u32[]{:S(2)}, u32[]{:S(2)}) %collective-permute-start.17) | collective-permute-done | bytes 98336 | tf_op jit(solution)/shard_map/ppermute | solution.py:741
  91.9 0.7 stage.3
  92.7 0.6 collective-permute-start.22
  93.3 4.5 %edges.1 = (bf16[2048,512]{1,0:T(8,128)(2,1)}, f32[8,128]{1,0:T(8,128)S(1)}) custom-call(bf16[2048,512]{1,0:T(8,128)(2,1)} %bitcast.14, f32[512,512]{1,0:T(8,128)} %get-tuple-element.109.summed_grad_hbm, bf16[2048,512]{1,0:T(8,128)(2,1)} %get-tuple-element.110.pre_grad_hbm, bf16[1536,512]{1,0:T(8,128)(2,1)} %w_edge_in_hbm.3, f32[8,128]{1,0:T(8,128)S(1)} %get-tuple-element.114._), custom_call_target="tpu_custom_call" | custom-call | flops 1 | bytes 1 | tf_op jit(solution)/shard_map/edges/pallas_call | solution.py:868
  97.8 1.0 collective-permute-done.22.refs_3_
  98.7 0.9 split.1
  99.7 1.7 %collective-permute-start.23 = (bf16[448,128]{1,0:T(8,128)(2,1)S(1)}, bf16[448,128]{1,0:T(8,128)(2,1)S(1)}, u32[]{:S(2)}, u32[]{:S(2)}) collective-permute-start(bf16[448,128]{1,0:T(8,128)(2,1)S(1)} %get-tuple-element.125), channel_id=1, source_target_pairs={{0,6},{1,7},{2,4},{3,5},{4,2},{5,3},{6,0},{7,1},{8,14},{9,15},{10,... | collective-permute-start | bytes 344072 | tf_op jit(solution)/shard_map/ppermute | solution.py:553
  101.6 2.6 %collective-permute-start.25 = (bf16[448,128]{1,0:T(8,128)(2,1)S(1)}, bf16[448,128]{1,0:T(8,128)(2,1)S(1)}, u32[]{:S(2)}, u32[]{:S(2)}) collective-permute-start(bf16[448,128]{1,0:T(8,128)(2,1)S(1)} %get-tuple-element.127), channel_id=1, source_target_pairs={{0,2},{1,3},{2,0},{3,1},{4,6},{5,7},{6,4},{7,5},{8,10},{9,11},{10,... | collective-permute-start | bytes 344072 | tf_op jit(solution)/shard_map/ppermute | solution.py:553
  104.1 2.4 %finish.1 = (bf16[512,512]{1,0:T(8,128)(2,1)}, f32[8,128]{1,0:T(8,128)S(1)}) custom-call(s32[5]{0:T(128)S(1)} %stack.23.scal.refs_8_, s32[1,512]{1,0:T(1,128)S(1)} %copy-done, bf16[384,128]{1,0:T(8,128)(2,1)S(1)} %get-tuple-element.100.refs_0_, bf16[384,128]{1,0:T(8,128)(2,1)S(1)} %collective-permute-done.11.refs_1_.refs_5_, ...), custom_call_target="tpu_custom_call" | custom-call | tf_op jit(solution)/shard_map/finish/pallas_call | solution.py:1021
  106.5 0.7 collective-permute-done.23.refs_1_
  107.2 3.2 %collective-permute-done.24.refs_2_ = bf16[448,128]{1,0:T(8,128)(2,1)S(1)} collective-permute-done((bf16[448,128]{1,0:T(8,128)(2,1)S(1)}, bf16[448,128]{1,0:T(8,128)(2,1)S(1)}, u32[]{:S(2)}, u32[]{:S(2)}) %collective-permute-start.24) | collective-permute-done | bytes 114720 | tf_op jit(solution)/shard_map/ppermute | solution.py:553
  110.5 1.0 collective-permute-start.26
  111.4 3.9 %collective-permute-done.26.theirs_ref = bf16[448,128]{1,0:T(8,128)(2,1)S(1)} collective-permute-done((bf16[448,128]{1,0:T(8,128)(2,1)S(1)}, bf16[448,128]{1,0:T(8,128)(2,1)S(1)}, u32[]{:S(2)}, u32[]{:S(2)}) %collective-permute-start.26) | collective-permute-done | bytes 114720 | tf_op jit(solution)/shard_map/ppermute | solution.py:553
  115.3 0.6 join.2.mine_ref
  116.0 1.5 %collective-permute-done.27.theirs_ref = bf16[448,256]{1,0:T(8,128)(2,1)S(1)} collective-permute-done((bf16[448,256]{1,0:T(8,128)(2,1)S(1)}, bf16[448,256]{1,0:T(8,128)(2,1)S(1)}, u32[]{:S(2)}, u32[]{:S(2)}) %collective-permute-start.27) | collective-permute-done | bytes 229408 | tf_op jit(solution)/shard_map/ppermute | solution.py:553
  117.5 1.6 %join.3 = f32[448,512]{1,0:T(8,128)} custom-call(s32[5]{0:T(128)S(1)} %stack.23.scal.refs_8_, bf16[448,256]{1,0:T(8,128)(2,1)S(1)} %join.2.mine_ref, bf16[448,256]{1,0:T(8,128)(2,1)S(1)} %collective-permute-done.27.theirs_ref), custom_call_target="tpu_custom_call" | custom-call | tf_op jit(solution)/shard_map/join/pallas_call | solution.py:728
  (26 shorter events, 0.8 us)
Async XLA Ops:
  3.4 11.0 %collective-permute-start = (bf16[400,128]{1,0:T(8,128)(2,1)S(1)}, bf16[400,128]{1,0:T(8,128)(2,1)S(1)}, u32[]{:S(2)}, u32[]{:S(2)}) collective-permute-start(bf16[400,128]{1,0:T(8,128)(2,1)S(1)} %get-tuple-element.68), channel_id=1, source_target_pairs={{0,1},{1,2},{2,3},{3,4},{4,5},{5,6},{6,7},{7,0},{8,9},{9,10},{10,1... | collective-permute-start | bytes 307208 | tf_op jit(solution)/shard_map/ppermute | solution.py:741
  6.4 9.3 %collective-permute-start.1 = (bf16[400,128]{1,0:T(8,128)(2,1)S(1)}, bf16[400,128]{1,0:T(8,128)(2,1)S(1)}, u32[]{:S(2)}, u32[]{:S(2)}) collective-permute-start(bf16[400,128]{1,0:T(8,128)(2,1)S(1)} %get-tuple-element.69), channel_id=1, source_target_pairs={{0,2},{1,3},{2,4},{3,5},{4,6},{5,7},{6,0},{7,1},{8,10},{9,11},{10,... | collective-permute-start | bytes 307208 | tf_op jit(solution)/shard_map/ppermute | solution.py:741
  8.0 14.2 %collective-permute-start.2 = (bf16[400,128]{1,0:T(8,128)(2,1)S(1)}, bf16[400,128]{1,0:T(8,128)(2,1)S(1)}, u32[]{:S(2)}, u32[]{:S(2)}) collective-permute-start(bf16[400,128]{1,0:T(8,128)(2,1)S(1)} %get-tuple-element.70), channel_id=1, source_target_pairs={{0,3},{1,4},{2,5},{3,6},{4,7},{5,0},{6,1},{7,2},{8,11},{9,12},{10,... | collective-permute-start | bytes 307208 | tf_op jit(solution)/shard_map/ppermute | solution.py:741
  10.5 11.7 %collective-permute-start.3 = (bf16[400,128]{1,0:T(8,128)(2,1)S(1)}, bf16[400,128]{1,0:T(8,128)(2,1)S(1)}, u32[]{:S(2)}, u32[]{:S(2)}) collective-permute-start(bf16[400,128]{1,0:T(8,128)(2,1)S(1)} %get-tuple-element.71), channel_id=1, source_target_pairs={{0,4},{1,5},{2,6},{3,7},{4,0},{5,1},{6,2},{7,3},{8,12},{9,13},{10,... | collective-permute-start | bytes 307208 | tf_op jit(solution)/shard_map/ppermute | solution.py:741
  11.8 10.5 %collective-permute-start.4 = (bf16[400,128]{1,0:T(8,128)(2,1)S(1)}, bf16[400,128]{1,0:T(8,128)(2,1)S(1)}, u32[]{:S(2)}, u32[]{:S(2)}) collective-permute-start(bf16[400,128]{1,0:T(8,128)(2,1)S(1)} %get-tuple-element.72), channel_id=1, source_target_pairs={{0,5},{1,6},{2,7},{3,0},{4,1},{5,2},{6,3},{7,4},{8,13},{9,14},{10,... | collective-permute-start | bytes 307208 | tf_op jit(solution)/shard_map/ppermute | solution.py:741
  14.4 7.8 %collective-permute-start.5 = (bf16[400,128]{1,0:T(8,128)(2,1)S(1)}, bf16[400,128]{1,0:T(8,128)(2,1)S(1)}, u32[]{:S(2)}, u32[]{:S(2)}) collective-permute-start(bf16[400,128]{1,0:T(8,128)(2,1)S(1)} %get-tuple-element.73), channel_id=1, source_target_pairs={{0,6},{1,7},{2,0},{3,1},{4,2},{5,3},{6,4},{7,5},{8,14},{9,15},{10,... | collective-permute-start | bytes 307208 | tf_op jit(solution)/shard_map/ppermute | solution.py:741
  15.8 6.5 %collective-permute-start.6 = (bf16[400,128]{1,0:T(8,128)(2,1)S(1)}, bf16[400,128]{1,0:T(8,128)(2,1)S(1)}, u32[]{:S(2)}, u32[]{:S(2)}) collective-permute-start(bf16[400,128]{1,0:T(8,128)(2,1)S(1)} %get-tuple-element.74), channel_id=1, source_target_pairs={{0,7},{1,0},{2,1},{3,2},{4,3},{5,4},{6,5},{7,6},{8,15},{9,8},{10,9... | collective-permute-start | bytes 307208 | tf_op jit(solution)/shard_map/ppermute | solution.py:741
  23.6 6.3 %collective-permute-start.7 = (bf16[64,512]{1,0:T(8,128)(2,1)S(1)}, bf16[64,512]{1,0:T(8,128)(2,1)S(1)}, u32[]{:S(2)}, u32[]{:S(2)}) collective-permute-start(bf16[64,512]{1,0:T(8,128)(2,1)S(1)} %get-tuple-element.78), channel_id=1, source_target_pairs={{0,1},{2,3},{4,5},{6,7},{1,0},{3,2},{5,4},{7,6},{8,9},{10,11},{12,... | collective-permute-start | bytes 196616 | tf_op jit(solution)/shard_map/ppermute | solution.py:747
  27.6 2.2 %collective-permute-start.8 = (bf16[64,512]{1,0:T(8,128)(2,1)S(1)}, bf16[64,512]{1,0:T(8,128)(2,1)S(1)}, u32[]{:S(2)}, u32[]{:S(2)}) collective-permute-start(bf16[64,512]{1,0:T(8,128)(2,1)S(1)} %get-tuple-element.79), channel_id=1, source_target_pairs={{1,2},{3,4},{5,6},{2,1},{4,3},{6,5},{9,10},{11,12},{13,14},{10,9},... | collective-permute-start | bytes 196616 | tf_op jit(solution)/shard_map/ppermute | solution.py:747
  46.7 13.0 %collective-permute-start.18 = (bf16[3584,256]{1,0:T(8,128)(2,1)S(1)}, bf16[3584,256]{1,0:T(8,128)(2,1)S(1)}, u32[]{:S(2)}, u32[]{:S(2)}) collective-permute-start(bf16[3584,256]{1,0:T(8,128)(2,1)S(1)} %get-tuple-element.112), channel_id=1, source_target_pairs={{0,8},{8,0},{16,24},{24,16},{1,9},{9,1},{17,25},{25,17},{2,10},{10... | collective-permute-start | bytes 5505032 | tf_op jit(solution)/shard_map/ppermute | solution.py:553
  48.1 10.3 %collective-permute-start.9 = (bf16[64,512]{1,0:T(8,128)(2,1)S(1)}, bf16[64,512]{1,0:T(8,128)(2,1)S(1)}, u32[]{:S(2)}, u32[]{:S(2)}) collective-permute-start(bf16[64,512]{1,0:T(8,128)(2,1)S(1)} %get-tuple-element.97), channel_id=1, source_target_pairs={{0,1},{2,3},{4,5},{6,7},{1,0},{3,2},{5,4},{7,6},{8,9},{10,11},{12,... | collective-permute-start | bytes 196616 | tf_op jit(solution)/shard_map/ppermute | solution.py:747
  55.6 2.8 %collective-permute-start.10 = (bf16[64,512]{1,0:T(8,128)(2,1)S(1)}, bf16[64,512]{1,0:T(8,128)(2,1)S(1)}, u32[]{:S(2)}, u32[]{:S(2)}) collective-permute-start(bf16[64,512]{1,0:T(8,128)(2,1)S(1)} %get-tuple-element.98), channel_id=1, source_target_pairs={{1,2},{3,4},{5,6},{2,1},{4,3},{6,5},{9,10},{11,12},{13,14},{10,9},... | collective-permute-start | bytes 196616 | tf_op jit(solution)/shard_map/ppermute | solution.py:747
  60.8 23.7 %collective-permute-start.19 = (bf16[8,224,128]{2,1,0:T(8,128)(2,1)S(1)}, bf16[8,224,128]{2,1,0:T(8,128)(2,1)S(1)}, u32[]{:S(2)}, u32[]{:S(2)}) collective-permute-start(bf16[8,224,128]{2,1,0:T(8,128)(2,1)S(1)} %get-tuple-element.117), channel_id=1, source_target_pairs={{0,16},{8,24},{16,0},{24,8},{1,17},{9,25},{17,1},{25,9},{2,18},{10... | collective-permute-start | bytes 1376264 | tf_op jit(solution)/shard_map/ppermute | solution.py:553
  62.4 29.6 %collective-permute-start.21 = (bf16[4,224,256]{2,1,0:T(8,128)(2,1)S(1)}, bf16[4,224,256]{2,1,0:T(8,128)(2,1)S(1)}, u32[]{:S(2)}, u32[]{:S(2)}) collective-permute-start(bf16[4,224,256]{2,1,0:T(8,128)(2,1)S(1)} %get-tuple-element.120), channel_id=1, source_target_pairs={{0,1},{1,0},{2,3},{3,2},{4,5},{5,4},{6,7},{7,6},{8,9},{9,8},{10,11... | collective-permute-start | bytes 1376264 | tf_op jit(solution)/shard_map/ppermute | solution.py:553
  67.2 6.8 %collective-permute-start.13 = (bf16[384,128]{1,0:T(8,128)(2,1)S(1)}, bf16[384,128]{1,0:T(8,128)(2,1)S(1)}, u32[]{:S(2)}, u32[]{:S(2)}) collective-permute-start(bf16[384,128]{1,0:T(8,128)(2,1)S(1)} %get-tuple-element.103), channel_id=1, source_target_pairs={{0,5},{1,6},{2,7},{3,0},{4,1},{5,2},{6,3},{7,4},{8,13},{9,14},{10,... | collective-permute-start | bytes 294920 | tf_op jit(solution)/shard_map/ppermute | solution.py:741
  70.9 11.6 %collective-permute-start.14 = (bf16[384,128]{1,0:T(8,128)(2,1)S(1)}, bf16[384,128]{1,0:T(8,128)(2,1)S(1)}, u32[]{:S(2)}, u32[]{:S(2)}) collective-permute-start(bf16[384,128]{1,0:T(8,128)(2,1)S(1)} %get-tuple-element.104), channel_id=1, source_target_pairs={{0,4},{1,5},{2,6},{3,7},{4,0},{5,1},{6,2},{7,3},{8,12},{9,13},{10,... | collective-permute-start | bytes 294920 | tf_op jit(solution)/shard_map/ppermute | solution.py:741
  70.9 12.4 %collective-permute-start.15 = (bf16[384,128]{1,0:T(8,128)(2,1)S(1)}, bf16[384,128]{1,0:T(8,128)(2,1)S(1)}, u32[]{:S(2)}, u32[]{:S(2)}) collective-permute-start(bf16[384,128]{1,0:T(8,128)(2,1)S(1)} %get-tuple-element.105), channel_id=1, source_target_pairs={{0,3},{1,4},{2,5},{3,6},{4,7},{5,0},{6,1},{7,2},{8,11},{9,12},{10,... | collective-permute-start | bytes 294920 | tf_op jit(solution)/shard_map/ppermute | solution.py:741
  74.0 11.3 %collective-permute-start.11 = (bf16[384,128]{1,0:T(8,128)(2,1)S(1)}, bf16[384,128]{1,0:T(8,128)(2,1)S(1)}, u32[]{:S(2)}, u32[]{:S(2)}) collective-permute-start(bf16[384,128]{1,0:T(8,128)(2,1)S(1)} %get-tuple-element.101), channel_id=1, source_target_pairs={{0,7},{1,0},{2,1},{3,2},{4,3},{5,4},{6,5},{7,6},{8,15},{9,8},{10,9... | collective-permute-start | bytes 294920 | tf_op jit(solution)/shard_map/ppermute | solution.py:741
  82.5 5.7 %collective-permute-start.12 = (bf16[384,128]{1,0:T(8,128)(2,1)S(1)}, bf16[384,128]{1,0:T(8,128)(2,1)S(1)}, u32[]{:S(2)}, u32[]{:S(2)}) collective-permute-start(bf16[384,128]{1,0:T(8,128)(2,1)S(1)} %get-tuple-element.102), channel_id=1, source_target_pairs={{0,6},{1,7},{2,0},{3,1},{4,2},{5,3},{6,4},{7,5},{8,14},{9,15},{10,... | collective-permute-start | bytes 294920 | tf_op jit(solution)/shard_map/ppermute | solution.py:741
  83.3 6.4 %collective-permute-start.16 = (bf16[384,128]{1,0:T(8,128)(2,1)S(1)}, bf16[384,128]{1,0:T(8,128)(2,1)S(1)}, u32[]{:S(2)}, u32[]{:S(2)}) collective-permute-start(bf16[384,128]{1,0:T(8,128)(2,1)S(1)} %get-tuple-element.106), channel_id=1, source_target_pairs={{0,2},{1,3},{2,4},{3,5},{4,6},{5,7},{6,0},{7,1},{8,10},{9,11},{10,... | collective-permute-start | bytes 294920 | tf_op jit(solution)/shard_map/ppermute | solution.py:741
  84.5 7.4 %collective-permute-start.17 = (bf16[384,128]{1,0:T(8,128)(2,1)S(1)}, bf16[384,128]{1,0:T(8,128)(2,1)S(1)}, u32[]{:S(2)}, u32[]{:S(2)}) collective-permute-start(bf16[384,128]{1,0:T(8,128)(2,1)S(1)} %get-tuple-element.107), channel_id=1, source_target_pairs={{0,1},{1,2},{2,3},{3,4},{4,5},{5,6},{6,7},{7,0},{8,9},{9,10},{10,1... | collective-permute-start | bytes 294920 | tf_op jit(solution)/shard_map/ppermute | solution.py:741
  85.3 12.5 %collective-permute-start.20 = (bf16[4,224,128]{2,1,0:T(8,128)(2,1)S(1)}, bf16[4,224,128]{2,1,0:T(8,128)(2,1)S(1)}, u32[]{:S(2)}, u32[]{:S(2)}) collective-permute-start(bf16[4,224,128]{2,1,0:T(8,128)(2,1)S(1)} %get-tuple-element.119), channel_id=1, source_target_pairs={{0,1},{1,0},{2,3},{3,2},{4,5},{5,4},{6,7},{7,6},{8,9},{9,8},{10,11... | collective-permute-start | bytes 688136 | tf_op jit(solution)/shard_map/ppermute | solution.py:553
  92.7 6.1 %collective-permute-start.22 = (bf16[4,224,128]{2,1,0:T(8,128)(2,1)S(1)}, bf16[4,224,128]{2,1,0:T(8,128)(2,1)S(1)}, u32[]{:S(2)}, u32[]{:S(2)}) collective-permute-start(bf16[4,224,128]{2,1,0:T(8,128)(2,1)S(1)} %get-tuple-element.122), channel_id=1, source_target_pairs={{0,16},{8,24},{16,0},{24,8},{1,17},{9,25},{17,1},{25,9},{2,18},{10... | collective-permute-start | bytes 688136 | tf_op jit(solution)/shard_map/ppermute | solution.py:553
  93.3 10.9 %copy-start = (s32[1,512]{1,0:T(1,128)S(1)}, s32[1,512]{1,0:T(1,128)}, u32[]{:S(2)}) copy-start(s32[1,512]{1,0:T(1,128)} %index_ref.1) | copy-start | bytes 6148
  99.7 7.5 %collective-permute-start.23 = (bf16[448,128]{1,0:T(8,128)(2,1)S(1)}, bf16[448,128]{1,0:T(8,128)(2,1)S(1)}, u32[]{:S(2)}, u32[]{:S(2)}) collective-permute-start(bf16[448,128]{1,0:T(8,128)(2,1)S(1)} %get-tuple-element.125), channel_id=1, source_target_pairs={{0,6},{1,7},{2,4},{3,5},{4,2},{5,3},{6,0},{7,1},{8,14},{9,15},{10,... | collective-permute-start | bytes 344072 | tf_op jit(solution)/shard_map/ppermute | solution.py:553
  101.3 9.1 %collective-permute-start.24 = (bf16[448,128]{1,0:T(8,128)(2,1)S(1)}, bf16[448,128]{1,0:T(8,128)(2,1)S(1)}, u32[]{:S(2)}, u32[]{:S(2)}) collective-permute-start(bf16[448,128]{1,0:T(8,128)(2,1)S(1)} %get-tuple-element.126), channel_id=1, source_target_pairs={{0,4},{1,5},{2,6},{3,7},{4,0},{5,1},{6,2},{7,3},{8,12},{9,13},{10,... | collective-permute-start | bytes 344072 | tf_op jit(solution)/shard_map/ppermute | solution.py:553
  101.6 8.9 %collective-permute-start.25 = (bf16[448,128]{1,0:T(8,128)(2,1)S(1)}, bf16[448,128]{1,0:T(8,128)(2,1)S(1)}, u32[]{:S(2)}, u32[]{:S(2)}) collective-permute-start(bf16[448,128]{1,0:T(8,128)(2,1)S(1)} %get-tuple-element.127), channel_id=1, source_target_pairs={{0,2},{1,3},{2,0},{3,1},{4,6},{5,7},{6,4},{7,5},{8,10},{9,11},{10,... | collective-permute-start | bytes 344072 | tf_op jit(solution)/shard_map/ppermute | solution.py:553
  110.5 4.9 %collective-permute-start.26 = (bf16[448,128]{1,0:T(8,128)(2,1)S(1)}, bf16[448,128]{1,0:T(8,128)(2,1)S(1)}, u32[]{:S(2)}, u32[]{:S(2)}) collective-permute-start(bf16[448,128]{1,0:T(8,128)(2,1)S(1)} %sum.1.mine_ref), channel_id=1, source_target_pairs={{0,16},{8,24},{16,0},{24,8},{1,17},{9,25},{17,1},{25,9},{2,18},{10... | collective-permute-start | bytes 344072 | tf_op jit(solution)/shard_map/ppermute | solution.py:553
  115.9 1.6 %collective-permute-start.27 = (bf16[448,256]{1,0:T(8,128)(2,1)S(1)}, bf16[448,256]{1,0:T(8,128)(2,1)S(1)}, u32[]{:S(2)}, u32[]{:S(2)}) collective-permute-start(bf16[448,256]{1,0:T(8,128)(2,1)S(1)} %join.2.mine_ref), channel_id=1, source_target_pairs={{0,8},{8,0},{16,24},{24,16},{1,9},{9,1},{17,25},{25,17},{2,10},{10... | collective-permute-start | bytes 688136 | tf_op jit(solution)/shard_map/ppermute | solution.py:553

commit v3 on v2

--- a/solution.py
+++ b/solution.py
@@ -19,7 +19,25 @@
 F32 = jnp.float32
 BF16 = jnp.bfloat16
 VMEM = pltpu.VMEM
-SMEM = pltpu.SMEM
+
+
+class Places:
+    def __getitem__(self, at):
+        part = lax.axis_index("dom")
+        geom = lax.axis_index("geom")
+        if at == PART:
+            return part
+        if at == CORE:
+            return geom & 1
+        if at == DOM_BIT:
+            return part & 1
+        if at == OWNER:
+            return part >> 1
+        return (geom >> (at - GEOM_BITS + 1)) & 1
+
+
+def placed(kernel, *fixed):
+    return lambda *refs: kernel(*fixed, Places(), *refs)
 
 
 def dot_nn(left, right):
@@ -111,9 +129,9 @@
     return hot(iota((cell_count, LANES), 0) == spot.astype(jnp.int32))
 
 
-def unpack_kernel(part_count, capacity, *refs):
+def unpack_kernel(part_count, capacity, scal, *refs):
     blocks = refs[:part_count]
-    scal, _, nodes_ref, low_ref, high_ref, ids_ref, rows_ref, hot_ref = refs[part_count:]
+    _, nodes_ref, low_ref, high_ref, ids_ref, rows_ref, hot_ref = refs[part_count:]
     cell_count, width = nodes_ref.shape
     chunks = width // LANES
     for step in range(part_count):
@@ -528,10 +546,6 @@
     return [pl.BlockSpec(memory_space=VMEM)] * count
 
 
-def scalars():
-    return pl.BlockSpec(memory_space=SMEM)
-
-
 def params(limit):
     return pltpu.CompilerParams(vmem_limit_bytes=limit * MIB)
 
@@ -624,7 +638,7 @@
     return pl.pallas_call(
         kernel,
         out_shape=[near_shape(*out) for out in outs],
-        in_specs=[scalars()] + whole(len(operands) - 1),
+        in_specs=whole(len(operands)),
         out_specs=whole(len(outs)),
         compiler_params=params(24),
         name=name,
@@ -647,13 +661,13 @@
     return columns + [owner], [owner] + columns
 
 
-def begin_weights(scal, keep, got, geom_count, part_count, *tokens):
+def begin_weights(keep, got, geom_count, part_count, *tokens):
     left, right = chains(geom_count)
     rows, width = keep.shape
     dims = (part_count, rows // part_count, width)
     piece = (part_count, rows // part_count // 2, width)
     return local_call(
-        functools.partial(core_kernel, (left[0][0], right[0][0]), (left[0][3], right[0][3])),
+        placed(core_kernel, (left[0][0], right[0][0]), (left[0][3], right[0][3])),
         [
             (dims,),
             (halved(piece, left[0][0]),),
@@ -661,14 +675,13 @@
             ((8, LANES), F32),
         ],
         "core",
-        scal,
         keep,
         got,
         *tokens,
     )
 
 
-def pair_weights(scal, total, send_left, send_right, geom_count, part_count, early):
+def pair_weights(total, send_left, send_right, geom_count, part_count, early):
     rows = total.shape[1]
     ends = []
     for part, chain, send in zip((0, 1), chains(geom_count), (send_left, send_right)):
@@ -679,7 +692,7 @@
             follow = chain[at + 1]
             now = halved(now, kind)
             value, send = local_call(
-                functools.partial(
+                placed(
                     stage_kernel,
                     part if at == 0 else None,
                     (kind, follow[0]),
@@ -687,7 +700,6 @@
                 ),
                 [(now,), (halved(now, follow[0]),)],
                 "stage",
-                scal,
                 value,
                 swap(send, axis, bit),
                 *early[part],
@@ -700,15 +712,14 @@
     return ends, end
 
 
-def reduce_weights(scal, ends, end, geom_count, part_count, early, late):
+def reduce_weights(ends, end, geom_count, part_count, early, late):
     left, right = chains(geom_count)
     out = (2 * end[1], end[2])
     owners = part_count // 2
     pieces = local_call(
-        functools.partial(split_kernel, (left[-1][0], right[-1][0]), (left[-1][3], right[-1][3])),
+        placed(split_kernel, (left[-1][0], right[-1][0]), (left[-1][3], right[-1][3])),
         [(out,)] * owners,
         "split",
-        scal,
         *ends[0],
         *ends[1],
         early,
@@ -726,13 +737,13 @@
         out = (out[0], 2 * out[1])
         last = bit == 1
         total = pl.pallas_call(
-            functools.partial(join_kernel, place_at),
+            placed(join_kernel, place_at),
             out_shape=shape(out, F32) if last else near_shape(out),
-            in_specs=[scalars()] + whole(2),
+            in_specs=whole(2),
             out_specs=pl.BlockSpec(memory_space=VMEM),
             compiler_params=params(24),
             name="join",
-        )(scal, total, swap(total, "geom", bit))
+        )(total, swap(total, "geom", bit))
     return total
 
 
@@ -762,7 +773,6 @@
 def run_prep(
     fan_in,
     cell_count,
-    scal,
     source,
     edges,
     cot_nodes,
@@ -778,7 +788,7 @@
     cells = EDGE_BLOCK // fan_in
     near = pl.BlockSpec(memory_space=VMEM)
     return pl.pallas_call(
-        functools.partial(prep_kernel, fan_in, cell_count),
+        placed(prep_kernel, fan_in, cell_count),
         out_shape=[
             near_shape(like.shape)
             for like in (edges, cot_nodes, cot_edges, w_edge_in, w_edge_out, w_node_in, w_node_out)
@@ -789,14 +799,13 @@
             near_shape(edges.shape, F32),
             near_shape((8, LANES), F32),
         ],
-        in_specs=[scalars()] + [pl.BlockSpec(memory_space=pltpu.HBM)] * 8 + [near],
+        in_specs=[pl.BlockSpec(memory_space=pltpu.HBM)] * 8 + [near],
         out_specs=[near] * 11,
         scratch_shapes=[VMEM(source.shape, jnp.int32), pltpu.SemaphoreType.DMA((8,))],
         compiler_params=params(PREP_LIMIT),
         cost_estimate=cost(4 * edge_count * edges.shape[1] ** 2, 20 * MIB),
         name="prep",
     )(
-        scal,
         *[
             pinned(value)
             for value in (
@@ -814,7 +823,7 @@
     )
 
 
-def run_main(fan_in, scale, scal, nodes, low, high, prepared):
+def run_main(fan_in, scale, nodes, low, high, prepared):
     edge_count, width = prepared[0].shape
     cell_count = nodes.shape[0]
     cells = EDGE_BLOCK // fan_in
@@ -825,7 +834,7 @@
     by_cell = (cell_count, width)
     weights = (7 * width, width // 2)
     return pl.pallas_call(
-        functools.partial(main_kernel, fan_in, scale),
+        placed(main_kernel, fan_in, scale),
         out_shape=[
             shape(by_edge),
             shape(by_cell),
@@ -837,7 +846,7 @@
             near_shape(weights),
             near_shape(weights),
         ],
-        in_specs=[scalars()] + [near] * 13,
+        in_specs=[near] * 13,
         out_specs=[far] * 4 + [near] * 5,
         scratch_shapes=[
             VMEM(by_edge, BF16),
@@ -858,7 +867,7 @@
         compiler_params=params(MAIN_LIMIT),
         cost_estimate=cost(28 * edge_count * width * width, 16 * MIB),
         name="main",
-    )(scal, nodes, low, high, *prepared)
+    )(nodes, low, high, *prepared)
 
 
 def run_edges(fan_in, cot, summed_grad, pre_grad, w_edge_in, *tokens):
@@ -907,21 +916,13 @@
     chunks = width // LANES
     block_rows = chunks * capacity
     scale = 1.0 / math.sqrt(geom_count * part_count * cell_count * fan_in)
-    part = lax.axis_index("dom")
-    geom = lax.axis_index("geom")
-    scal = [part, geom % 2, part % 2, part // 2]
-    geom = geom // 2
-    for _ in range(1, geom_count.bit_length() - 1):
-        scal.append(geom % 2)
-        geom = geom // 2
-    scal = jnp.stack(scal).astype(jnp.int32)
     edges = edge_in[0]
     cot = cot_edges[0]
 
     sends = pl.pallas_call(
-        functools.partial(pack_kernel, part_count, capacity),
+        placed(pack_kernel, part_count, capacity),
         out_shape=[shape((block_rows + 16, LANES))] * part_count + [near_shape((8, LANES), F32)],
-        in_specs=[scalars()] + [pl.BlockSpec(memory_space=pltpu.HBM)] * 2,
+        in_specs=[pl.BlockSpec(memory_space=pltpu.HBM)] * 2,
         out_specs=whole(part_count + 1),
         scratch_shapes=[
             VMEM((cell_count, width), BF16),
@@ -930,11 +931,10 @@
         ],
         compiler_params=params(24),
         name="pack",
-    )(scal, pinned(h_in[0]), pinned(new_index))
+    )(pinned(h_in[0]), pinned(new_index))
     prepared = run_prep(
         fan_in,
         cell_count,
-        scal,
         source,
         edges,
         cot_nodes[0],
@@ -949,14 +949,14 @@
     for step in send_order(part_count):
         got[step] = shift(sends[step], step)
     nodes, low, high, ids = pl.pallas_call(
-        functools.partial(unpack_kernel, part_count, capacity),
+        placed(unpack_kernel, part_count, capacity),
         out_shape=[
             shape((cell_count, width)),
             shape((HB, width)),
             shape((HB, width)),
             shape((part_count * 16, LANES)),
         ],
-        in_specs=whole(part_count) + [scalars()] + whole(1),
+        in_specs=whole(part_count + 1),
         out_specs=whole(4),
         scratch_shapes=[
             VMEM((part_count * LANES, width), BF16),
@@ -964,7 +964,7 @@
         ],
         compiler_params=params(24),
         name="unpack",
-    )(*[got[step] for step in range(part_count)], scal, prepared[-1])
+    )(*[got[step] for step in range(part_count)], prepared[-1])
     low = neighbour(low, 0)
     high = neighbour(high, 1)
 
@@ -978,34 +978,34 @@
         base,
         keep,
         send,
-    ) = run_main(fan_in, scale, scal, nodes, low, high, prepared[:-1])
+    ) = run_main(fan_in, scale, nodes, low, high, prepared[:-1])
     low, high, node_grad, rim = pl.pallas_call(
-        cell_kernel,
+        placed(cell_kernel),
         out_shape=[
             near_shape((HB, width)),
             near_shape((HB, width)),
             near_shape((cell_count, width)),
             near_shape((2 * HB, width), F32),
         ],
-        in_specs=[scalars()] + whole(4),
+        in_specs=whole(4),
         out_specs=whole(4),
         compiler_params=params(24),
         cost_estimate=cost(3 * cell_count * width * width, 3 * MIB),
         name="cells",
-    )(scal, sent, received, base, prepared[3])
+    )(sent, received, base, prepared[3])
     low = neighbour(low, 0)
     high = neighbour(high, 1)
     *returning, token = pl.pallas_call(
-        functools.partial(return_kernel, part_count, capacity),
+        placed(return_kernel, part_count, capacity),
         out_shape=[near_shape((block_rows, LANES))] * part_count + [near_shape((8, LANES), F32)],
-        in_specs=[scalars()] + whole(5),
+        in_specs=whole(5),
         out_specs=whole(part_count + 1),
         compiler_params=params(24),
         cost_estimate=cost(1, 1),
         name="returning",
-    )(scal, node_grad, rim, low, high, ids)
+    )(node_grad, rim, low, high, ids)
     *begun, token = begin_weights(
-        scal, keep, swap(send, "geom", 1), geom_count, part_count, token
+        keep, swap(send, "geom", 1), geom_count, part_count, token
     )
 
     grad_edge, edge_token = run_edges(
@@ -1016,12 +1016,12 @@
         back[step] = shift(returning[step], -step)
     early = [back[step] for step in send_order(part_count)]
     ends, end = pair_weights(
-        scal, *begun, geom_count, part_count, (early[:FIRST], early[:SECOND])
+        *begun, geom_count, part_count, (early[:FIRST], early[:SECOND])
     )
     grad_in, late = pl.pallas_call(
-        functools.partial(finish_kernel, part_count, capacity),
+        placed(finish_kernel, part_count, capacity),
         out_shape=[shape((cell_count, width)), near_shape((8, LANES), F32)],
-        in_specs=[scalars()] + whole(1 + part_count),
+        in_specs=whole(1 + part_count),
         out_specs=whole(2),
         scratch_shapes=[
             VMEM((part_count * LANES, width), BF16),
@@ -1029,8 +1029,8 @@
         ],
         compiler_params=params(24),
         name="finish",
-    )(scal, new_index, *[back[step] for step in range(part_count)])
-    weight_grads = reduce_weights(scal, ends, end, geom_count, part_count, edge_token, late)
+    )(new_index, *[back[step] for step in range(part_count)])
+    weight_grads = reduce_weights(ends, end, geom_count, part_count, edge_token, late)
     return (node_new[None], edge_new[None], grad_in[None], grad_edge[None], weight_grads)
 
 

time: 119 us -> 112 us (0.941)
  Pallas kernels: 41 us -> 33.5 us
  waiting for transfers between devices: 20.4 us -> 17.6 us
  starting transfers between devices: 56.7 us -> 59.4 us
    pallas_call x9, Pallas kernels: 32.9 us -> 27.6 us  [the longest x1 15.8 us: run_main(): pl.pallas_call(placed(main_kernel, fan_in, scale), out_shape=[shape(by_ed...]
    pallas_call x4, Pallas kernels: 3.52 us -> 1.31 us  [local_call(): pl.pallas_call(kernel, out_shape=[near_shape(*out) for out in outs], in_s...]
    ppermute x14, waiting for transfers between devices: 6.61 us -> 4.93 us  [shift(): lax.ppermute(value, 'dom', [(at, (at + steps) % count) for at in range(co...]
    ppermute x14, starting transfers between devices: 28.7 us -> 30.1 us  [shift(): lax.ppermute(value, 'dom', [(at, (at + steps) % count) for at in range(co...]
  transfers between devices with their start and end apart: 28 -> 28, of which waited for: 13 -> 12; matrix products, arithmetic and copies ran while one was open for 0% -> 0% of each run, Pallas kernels for 13% -> 11%
where the time goes in v3:
time: 112 us; the launch traced here: 111 us
  starting transfers between devices  59.4 us (53%)
  Pallas kernels  33.5 us (30%)
  waiting for transfers between devices  17.6 us (16%)
    ppermute x14, starting transfers between devices, shift(): lax.ppermute(value, 'dom', [(at, (at + steps) % count) for at in range(co...  30.1 us
    ppermute x10, starting transfers between devices, swap(): return lax.ppermute(value, axis, [(at, at ^ bit) for at in range(count)])  16 us
    pallas_call x1, Pallas kernels, run_main(): pl.pallas_call(placed(main_kernel, fan_in, scale), out_shape=[shape(by_ed...  15.8 us
    ppermute x4, starting transfers between devices, neighbour(): lax.ppermute(value, 'dom', pairs + [(right, left) for left, right in pairs])  13.3 us
    ppermute x10, waiting for transfers between devices, swap(): return lax.ppermute(value, axis, [(at, at ^ bit) for at in range(count)])  9.22 us
    ppermute x14, waiting for transfers between devices, shift(): lax.ppermute(value, 'dom', [(at, (at + steps) % count) for at in range(co...  4.93 us
    pallas_call x1, Pallas kernels, run_edges(): pl.pallas_call(functools.partial(edge_kernel, fan_in), out_shape=[shape((...  4.5 us
    pallas_call x1, Pallas kernels, run_prep(): pl.pallas_call(placed(prep_kernel, fan_in, cell_count), out_shape=[near_s...  4.47 us
  transfers between devices with their start and end apart: 28, of which 12 were waited for; matrix products, arithmetic and copies ran while one was open for 0% of the time, Pallas kernels for 11%

profile of v3, /device:TPU:0, one launch (start us, length us, event | category | flops | bytes accessed | tf_op | source)
XLA Modules:
  0.0 111.3 jit_solution(858098624912868624)
XLA Ops:
  0.6 2.1 %pack.1 = (bf16[400,128]{1,0:T(8,128)(2,1)S(1)}, bf16[400,128]{1,0:T(8,128)(2,1)S(1)}, bf16[400,128]{1,0:T(8,128)(2,1)S(1)}, bf16[400,128]{1,0:T(8,128)(2,1)S(1)...) custom-call(bf16[512,512]{1,0:T(8,128)(2,1)} %bitcast.12, ...), custom_call_target="tpu_custom_call" | custom-call | tf_op jit(solution)/shard_map/pack/pallas_call | solution.py:922
  2.7 3.0 %collective-permute-start = (bf16[400,128]{1,0:T(8,128)(2,1)S(1)}, bf16[400,128]{1,0:T(8,128)(2,1)S(1)}, u32[]{:S(2)}, u32[]{:S(2)}) collective-permute-start(bf16[400,128]{1,0:T(8,128)(2,1)S(1)} %get-tuple-element.68), channel_id=1, source_target_pairs={{0,1},{1,2},{2,3},{3,4},{4,5},{5,6},{6,7},{7,0},{8,9},{9,10},{10,1... | collective-permute-start | bytes 307208 | tf_op jit(solution)/shard_map/ppermute | solution.py:752
  5.8 1.6 %collective-permute-start.1 = (bf16[400,128]{1,0:T(8,128)(2,1)S(1)}, bf16[400,128]{1,0:T(8,128)(2,1)S(1)}, u32[]{:S(2)}, u32[]{:S(2)}) collective-permute-start(bf16[400,128]{1,0:T(8,128)(2,1)S(1)} %get-tuple-element.69), channel_id=1, source_target_pairs={{0,2},{1,3},{2,4},{3,5},{4,6},{5,7},{6,0},{7,1},{8,10},{9,11},{10,... | collective-permute-start | bytes 307208 | tf_op jit(solution)/shard_map/ppermute | solution.py:752
  7.3 2.5 %collective-permute-start.2 = (bf16[400,128]{1,0:T(8,128)(2,1)S(1)}, bf16[400,128]{1,0:T(8,128)(2,1)S(1)}, u32[]{:S(2)}, u32[]{:S(2)}) collective-permute-start(bf16[400,128]{1,0:T(8,128)(2,1)S(1)} %get-tuple-element.70), channel_id=1, source_target_pairs={{0,3},{1,4},{2,5},{3,6},{4,7},{5,0},{6,1},{7,2},{8,11},{9,12},{10,... | collective-permute-start | bytes 307208 | tf_op jit(solution)/shard_map/ppermute | solution.py:752
  9.9 1.2 %collective-permute-start.3 = (bf16[400,128]{1,0:T(8,128)(2,1)S(1)}, bf16[400,128]{1,0:T(8,128)(2,1)S(1)}, u32[]{:S(2)}, u32[]{:S(2)}) collective-permute-start(bf16[400,128]{1,0:T(8,128)(2,1)S(1)} %get-tuple-element.71), channel_id=1, source_target_pairs={{0,4},{1,5},{2,6},{3,7},{4,0},{5,1},{6,2},{7,3},{8,12},{9,13},{10,... | collective-permute-start | bytes 307208 | tf_op jit(solution)/shard_map/ppermute | solution.py:752
  11.1 2.6 %collective-permute-start.4 = (bf16[400,128]{1,0:T(8,128)(2,1)S(1)}, bf16[400,128]{1,0:T(8,128)(2,1)S(1)}, u32[]{:S(2)}, u32[]{:S(2)}) collective-permute-start(bf16[400,128]{1,0:T(8,128)(2,1)S(1)} %get-tuple-element.72), channel_id=1, source_target_pairs={{0,5},{1,6},{2,7},{3,0},{4,1},{5,2},{6,3},{7,4},{8,13},{9,14},{10,... | collective-permute-start | bytes 307208 | tf_op jit(solution)/shard_map/ppermute | solution.py:752
  13.7 1.3 %collective-permute-start.5 = (bf16[400,128]{1,0:T(8,128)(2,1)S(1)}, bf16[400,128]{1,0:T(8,128)(2,1)S(1)}, u32[]{:S(2)}, u32[]{:S(2)}) collective-permute-start(bf16[400,128]{1,0:T(8,128)(2,1)S(1)} %get-tuple-element.73), channel_id=1, source_target_pairs={{0,6},{1,7},{2,0},{3,1},{4,2},{5,3},{6,4},{7,5},{8,14},{9,15},{10,... | collective-permute-start | bytes 307208 | tf_op jit(solution)/shard_map/ppermute | solution.py:752
  15.1 1.4 %collective-permute-start.6 = (bf16[400,128]{1,0:T(8,128)(2,1)S(1)}, bf16[400,128]{1,0:T(8,128)(2,1)S(1)}, u32[]{:S(2)}, u32[]{:S(2)}) collective-permute-start(bf16[400,128]{1,0:T(8,128)(2,1)S(1)} %get-tuple-element.74), channel_id=1, source_target_pairs={{0,7},{1,0},{2,1},{3,2},{4,3},{5,4},{6,5},{7,6},{8,15},{9,8},{10,9... | collective-permute-start | bytes 307208 | tf_op jit(solution)/shard_map/ppermute | solution.py:752
  16.5 4.5 %prep.1 = (bf16[2048,512]{1,0:T(8,128)(2,1)S(1)}, bf16[512,512]{1,0:T(8,128)(2,1)S(1)}, bf16[2048,512]{1,0:T(8,128)(2,1)S(1)}, bf16[1536,512]{1,0:T(8,128)(2,1)S...) custom-call(s32[1,2048]{1,0:T(1,128)} %refs_0_.2, ...), custom_call_target="tpu_custom_call" | custom-call | flops 2147483648 | bytes 20971520 | tf_op jit(solution)/shard_map/prep/pallas_call | solution.py:790
  21.0 0.2 collective-permute-done.3.refs_4_
  21.3 0.8 unpack.1
  22.1 4.3 %collective-permute-start.7 = (bf16[64,512]{1,0:T(8,128)(2,1)S(1)}, bf16[64,512]{1,0:T(8,128)(2,1)S(1)}, u32[]{:S(2)}, u32[]{:S(2)}) collective-permute-start(bf16[64,512]{1,0:T(8,128)(2,1)S(1)} %get-tuple-element.78), channel_id=1, source_target_pairs={{0,1},{2,3},{4,5},{6,7},{1,0},{3,2},{5,4},{7,6},{8,9},{10,11},{12,... | collective-permute-start | bytes 196616 | tf_op jit(solution)/shard_map/ppermute | solution.py:758
  26.4 0.8 collective-permute-start.8
  27.2 1.4 %collective-permute-done.7.refs_1_ = bf16[64,512]{1,0:T(8,128)(2,1)S(1)} collective-permute-done((bf16[64,512]{1,0:T(8,128)(2,1)S(1)}, bf16[64,512]{1,0:T(8,128)(2,1)S(1)}, u32[]{:S(2)}, u32[]{:S(2)}) %collective-permute-start.7) | collective-permute-done | bytes 65568 | tf_op jit(solution)/shard_map/ppermute | solution.py:758
  28.7 15.8 %main.1 = (bf16[2048,512]{1,0:T(8,128)(2,1)}, bf16[512,512]{1,0:T(8,128)(2,1)}, bf16[2048,512]{1,0:T(8,128)(2,1)}, f32[512,512]{1,0:T(8,128)}, bf16[640,512]{1,0...) custom-call(bf16[512,512]{1,0:T(8,128)(2,1)S(1)} %get-tuple-element., ...), custom_call_target="tpu_custom_call" | custom-call | flops 15032385536 | bytes 16777216 | tf_op jit(solution)/shard_map/main/pallas_call | solution.py:836
  44.5 0.8 cells.1
  45.4 7.5 %collective-permute-start.9 = (bf16[64,512]{1,0:T(8,128)(2,1)S(1)}, bf16[64,512]{1,0:T(8,128)(2,1)S(1)}, u32[]{:S(2)}, u32[]{:S(2)}) collective-permute-start(bf16[64,512]{1,0:T(8,128)(2,1)S(1)} %get-tuple-element.97), channel_id=1, source_target_pairs={{0,1},{2,3},{4,5},{6,7},{1,0},{3,2},{5,4},{7,6},{8,9},{10,11},{12,... | collective-permute-start | bytes 196616 | tf_op jit(solution)/shard_map/ppermute | solution.py:758
  52.8 0.7 collective-permute-start.10
  53.5 2.1 %collective-permute-done.9.refs_2_ = bf16[64,512]{1,0:T(8,128)(2,1)S(1)} collective-permute-done((bf16[64,512]{1,0:T(8,128)(2,1)S(1)}, bf16[64,512]{1,0:T(8,128)(2,1)S(1)}, u32[]{:S(2)}, u32[]{:S(2)}) %collective-permute-start.9) | collective-permute-done | bytes 65568 | tf_op jit(solution)/shard_map/ppermute | solution.py:758
  55.6 0.8 returning.1
  56.4 0.6 core.1
  57.0 1.6 %collective-permute-start.19 = (bf16[8,224,128]{2,1,0:T(8,128)(2,1)S(1)}, bf16[8,224,128]{2,1,0:T(8,128)(2,1)S(1)}, u32[]{:S(2)}, u32[]{:S(2)}) collective-permute-start(bf16[8,224,128]{2,1,0:T(8,128)(2,1)S(1)} %get-tuple-element.117), channel_id=1, source_target_pairs={{0,16},{8,24},{16,0},{24,8},{1,17},{9,25},{17,1},{25,9},{2,18},{10... | collective-permute-start | bytes 1376264 | tf_op jit(solution)/shard_map/ppermute | solution.py:567
  58.6 4.8 %collective-permute-start.21 = (bf16[4,224,256]{2,1,0:T(8,128)(2,1)S(1)}, bf16[4,224,256]{2,1,0:T(8,128)(2,1)S(1)}, u32[]{:S(2)}, u32[]{:S(2)}) collective-permute-start(bf16[4,224,256]{2,1,0:T(8,128)(2,1)S(1)} %get-tuple-element.120), channel_id=1, source_target_pairs={{0,1},{1,0},{2,3},{3,2},{4,5},{5,4},{6,7},{7,6},{8,9},{9,8},{10,11... | collective-permute-start | bytes 1376264 | tf_op jit(solution)/shard_map/ppermute | solution.py:567
  63.4 3.4 %collective-permute-start.13 = (bf16[384,128]{1,0:T(8,128)(2,1)S(1)}, bf16[384,128]{1,0:T(8,128)(2,1)S(1)}, u32[]{:S(2)}, u32[]{:S(2)}) collective-permute-start(bf16[384,128]{1,0:T(8,128)(2,1)S(1)} %get-tuple-element.103), channel_id=1, source_target_pairs={{0,5},{1,6},{2,7},{3,0},{4,1},{5,2},{6,3},{7,4},{8,13},{9,14},{10,... | collective-permute-start | bytes 294920 | tf_op jit(solution)/shard_map/ppermute | solution.py:752
  66.8 0.3 collective-permute-start.14
  67.1 2.9 %collective-permute-start.15 = (bf16[384,128]{1,0:T(8,128)(2,1)S(1)}, bf16[384,128]{1,0:T(8,128)(2,1)S(1)}, u32[]{:S(2)}, u32[]{:S(2)}) collective-permute-start(bf16[384,128]{1,0:T(8,128)(2,1)S(1)} %get-tuple-element.105), channel_id=1, source_target_pairs={{0,3},{1,4},{2,5},{3,6},{4,7},{5,0},{6,1},{7,2},{8,11},{9,12},{10,... | collective-permute-start | bytes 294920 | tf_op jit(solution)/shard_map/ppermute | solution.py:752
  70.0 7.7 %collective-permute-start.11 = (bf16[384,128]{1,0:T(8,128)(2,1)S(1)}, bf16[384,128]{1,0:T(8,128)(2,1)S(1)}, u32[]{:S(2)}, u32[]{:S(2)}) collective-permute-start(bf16[384,128]{1,0:T(8,128)(2,1)S(1)} %get-tuple-element.101), channel_id=1, source_target_pairs={{0,7},{1,0},{2,1},{3,2},{4,3},{5,4},{6,5},{7,6},{8,15},{9,8},{10,9... | collective-permute-start | bytes 294920 | tf_op jit(solution)/shard_map/ppermute | solution.py:752
  77.7 0.9 collective-permute-done.14.refs_5_.refs_2_
  78.6 1.4 %collective-permute-start.12 = (bf16[384,128]{1,0:T(8,128)(2,1)S(1)}, bf16[384,128]{1,0:T(8,128)(2,1)S(1)}, u32[]{:S(2)}, u32[]{:S(2)}) collective-permute-start(bf16[384,128]{1,0:T(8,128)(2,1)S(1)} %get-tuple-element.102), channel_id=1, source_target_pairs={{0,6},{1,7},{2,0},{3,1},{4,2},{5,3},{6,4},{7,5},{8,14},{9,15},{10,... | collective-permute-start | bytes 294920 | tf_op jit(solution)/shard_map/ppermute | solution.py:752
  80.0 0.6 collective-permute-start.16
  80.6 0.2 stage.2
  80.8 3.5 %collective-permute-start.20 = (bf16[4,224,128]{2,1,0:T(8,128)(2,1)S(1)}, bf16[4,224,128]{2,1,0:T(8,128)(2,1)S(1)}, u32[]{:S(2)}, u32[]{:S(2)}) collective-permute-start(bf16[4,224,128]{2,1,0:T(8,128)(2,1)S(1)} %get-tuple-element.119), channel_id=1, source_target_pairs={{0,1},{1,0},{2,3},{3,2},{4,5},{5,4},{6,7},{7,6},{8,9},{9,8},{10,11... | collective-permute-start | bytes 688136 | tf_op jit(solution)/shard_map/ppermute | solution.py:567
  84.3 2.1 %collective-permute-done.16.refs_7_.refs_6_ = bf16[384,128]{1,0:T(8,128)(2,1)S(1)} collective-permute-done((bf16[384,128]{1,0:T(8,128)(2,1)S(1)}, bf16[384,128]{1,0:T(8,128)(2,1)S(1)}, u32[]{:S(2)}, u32[]{:S(2)}) %collective-permute-start.16) | collective-permute-done | bytes 98336 | tf_op jit(solution)/shard_map/ppermute | solution.py:752
  86.4 1.7 %collective-permute-done.17.refs_8_ = bf16[384,128]{1,0:T(8,128)(2,1)S(1)} collective-permute-done((bf16[384,128]{1,0:T(8,128)(2,1)S(1)}, bf16[384,128]{1,0:T(8,128)(2,1)S(1)}, u32[]{:S(2)}, u32[]{:S(2)}) %collective-permute-start.17) | collective-permute-done | bytes 98336 | tf_op jit(solution)/shard_map/ppermute | solution.py:752
  88.0 0.2 stage.3
  88.2 0.6 collective-permute-start.22
  88.8 4.5 %edges.1 = (bf16[2048,512]{1,0:T(8,128)(2,1)}, f32[8,128]{1,0:T(8,128)S(1)}) custom-call(bf16[2048,512]{1,0:T(8,128)(2,1)} %bitcast.9, f32[512,512]{1,0:T(8,128)} %get-tuple-element.109.summed_grad_hbm, bf16[2048,512]{1,0:T(8,128)(2,1)} %get-tuple-element.110.pre_grad_hbm, bf16[1536,512]{1,0:T(8,128)(2,1)} %w_edge_in_hbm.1, f32[8,128]{1,0:T(8,128)S(1)} %get-tuple-element.114._), custom_call_target="tpu_custom_call" | custom-call | flops 1 | bytes 1 | tf_op jit(solution)/shard_map/edges/pallas_call | solution.py:877
  93.3 1.0 collective-permute-done.22.refs_3_
  94.3 0.3 split.1
  94.6 1.4 %collective-permute-start.23 = (bf16[448,128]{1,0:T(8,128)(2,1)S(1)}, bf16[448,128]{1,0:T(8,128)(2,1)S(1)}, u32[]{:S(2)}, u32[]{:S(2)}) collective-permute-start(bf16[448,128]{1,0:T(8,128)(2,1)S(1)} %get-tuple-element.125), channel_id=1, source_target_pairs={{0,6},{1,7},{2,4},{3,5},{4,2},{5,3},{6,0},{7,1},{8,14},{9,15},{10,... | collective-permute-start | bytes 344072 | tf_op jit(solution)/shard_map/ppermute | solution.py:567
  96.1 3.0 %collective-permute-start.25 = (bf16[448,128]{1,0:T(8,128)(2,1)S(1)}, bf16[448,128]{1,0:T(8,128)(2,1)S(1)}, u32[]{:S(2)}, u32[]{:S(2)}) collective-permute-start(bf16[448,128]{1,0:T(8,128)(2,1)S(1)} %get-tuple-element.127), channel_id=1, source_target_pairs={{0,2},{1,3},{2,0},{3,1},{4,6},{5,7},{6,4},{7,5},{8,10},{9,11},{10,... | collective-permute-start | bytes 344072 | tf_op jit(solution)/shard_map/ppermute | solution.py:567
  99.1 1.8 %finish.1 = (bf16[512,512]{1,0:T(8,128)(2,1)}, f32[8,128]{1,0:T(8,128)S(1)}) custom-call(s32[1,512]{1,0:T(1,128)S(1)} %copy-done, bf16[384,128]{1,0:T(8,128)(2,1)S(1)} %get-tuple-element.100.refs_1_, bf16[384,128]{1,0:T(8,128)(2,1)S(1)} %collective-permute-done.11.refs_2_.refs_7_, bf16[384,128]{1,0:T(8,128)(2,1)S(1)} %collective-permute-done.12.refs_3_.refs_5_, ...), custom_call_target="tpu_custom_call" | custom-call | tf_op jit(solution)/shard_map/finish/pallas_call | solution.py:1021
  100.9 0.5 collective-permute-done.23.refs_1_
  101.4 2.3 %collective-permute-done.24.refs_2_ = bf16[448,128]{1,0:T(8,128)(2,1)S(1)} collective-permute-done((bf16[448,128]{1,0:T(8,128)(2,1)S(1)}, bf16[448,128]{1,0:T(8,128)(2,1)S(1)}, u32[]{:S(2)}, u32[]{:S(2)}) %collective-permute-start.24) | collective-permute-done | bytes 114720 | tf_op jit(solution)/shard_map/ppermute | solution.py:567
  103.8 0.9 collective-permute-start.26
  104.7 3.9 %collective-permute-done.26.refs_1_ = bf16[448,128]{1,0:T(8,128)(2,1)S(1)} collective-permute-done((bf16[448,128]{1,0:T(8,128)(2,1)S(1)}, bf16[448,128]{1,0:T(8,128)(2,1)S(1)}, u32[]{:S(2)}, u32[]{:S(2)}) %collective-permute-start.26) | collective-permute-done | bytes 114720 | tf_op jit(solution)/shard_map/ppermute | solution.py:567
  108.8 1.5 %collective-permute-done.27.refs_1_ = bf16[448,256]{1,0:T(8,128)(2,1)S(1)} collective-permute-done((bf16[448,256]{1,0:T(8,128)(2,1)S(1)}, bf16[448,256]{1,0:T(8,128)(2,1)S(1)}, u32[]{:S(2)}, u32[]{:S(2)}) %collective-permute-start.27) | collective-permute-done | bytes 229408 | tf_op jit(solution)/shard_map/ppermute | solution.py:567
  110.3 1.0 join.3
  (25 shorter events, 0.4 us)
Async XLA Ops:
  2.7 11.0 %collective-permute-start = (bf16[400,128]{1,0:T(8,128)(2,1)S(1)}, bf16[400,128]{1,0:T(8,128)(2,1)S(1)}, u32[]{:S(2)}, u32[]{:S(2)}) collective-permute-start(bf16[400,128]{1,0:T(8,128)(2,1)S(1)} %get-tuple-element.68), channel_id=1, source_target_pairs={{0,1},{1,2},{2,3},{3,4},{4,5},{5,6},{6,7},{7,0},{8,9},{9,10},{10,1... | collective-permute-start | bytes 307208 | tf_op jit(solution)/shard_map/ppermute | solution.py:752
  5.8 9.3 %collective-permute-start.1 = (bf16[400,128]{1,0:T(8,128)(2,1)S(1)}, bf16[400,128]{1,0:T(8,128)(2,1)S(1)}, u32[]{:S(2)}, u32[]{:S(2)}) collective-permute-start(bf16[400,128]{1,0:T(8,128)(2,1)S(1)} %get-tuple-element.69), channel_id=1, source_target_pairs={{0,2},{1,3},{2,4},{3,5},{4,6},{5,7},{6,0},{7,1},{8,10},{9,11},{10,... | collective-permute-start | bytes 307208 | tf_op jit(solution)/shard_map/ppermute | solution.py:752
  7.3 13.7 %collective-permute-start.2 = (bf16[400,128]{1,0:T(8,128)(2,1)S(1)}, bf16[400,128]{1,0:T(8,128)(2,1)S(1)}, u32[]{:S(2)}, u32[]{:S(2)}) collective-permute-start(bf16[400,128]{1,0:T(8,128)(2,1)S(1)} %get-tuple-element.70), channel_id=1, source_target_pairs={{0,3},{1,4},{2,5},{3,6},{4,7},{5,0},{6,1},{7,2},{8,11},{9,12},{10,... | collective-permute-start | bytes 307208 | tf_op jit(solution)/shard_map/ppermute | solution.py:752
  9.9 11.3 %collective-permute-start.3 = (bf16[400,128]{1,0:T(8,128)(2,1)S(1)}, bf16[400,128]{1,0:T(8,128)(2,1)S(1)}, u32[]{:S(2)}, u32[]{:S(2)}) collective-permute-start(bf16[400,128]{1,0:T(8,128)(2,1)S(1)} %get-tuple-element.71), channel_id=1, source_target_pairs={{0,4},{1,5},{2,6},{3,7},{4,0},{5,1},{6,2},{7,3},{8,12},{9,13},{10,... | collective-permute-start | bytes 307208 | tf_op jit(solution)/shard_map/ppermute | solution.py:752
  11.1 10.1 %collective-permute-start.4 = (bf16[400,128]{1,0:T(8,128)(2,1)S(1)}, bf16[400,128]{1,0:T(8,128)(2,1)S(1)}, u32[]{:S(2)}, u32[]{:S(2)}) collective-permute-start(bf16[400,128]{1,0:T(8,128)(2,1)S(1)} %get-tuple-element.72), channel_id=1, source_target_pairs={{0,5},{1,6},{2,7},{3,0},{4,1},{5,2},{6,3},{7,4},{8,13},{9,14},{10,... | collective-permute-start | bytes 307208 | tf_op jit(solution)/shard_map/ppermute | solution.py:752
  13.7 7.4 %collective-permute-start.5 = (bf16[400,128]{1,0:T(8,128)(2,1)S(1)}, bf16[400,128]{1,0:T(8,128)(2,1)S(1)}, u32[]{:S(2)}, u32[]{:S(2)}) collective-permute-start(bf16[400,128]{1,0:T(8,128)(2,1)S(1)} %get-tuple-element.73), channel_id=1, source_target_pairs={{0,6},{1,7},{2,0},{3,1},{4,2},{5,3},{6,4},{7,5},{8,14},{9,15},{10,... | collective-permute-start | bytes 307208 | tf_op jit(solution)/shard_map/ppermute | solution.py:752
  15.1 6.2 %collective-permute-start.6 = (bf16[400,128]{1,0:T(8,128)(2,1)S(1)}, bf16[400,128]{1,0:T(8,128)(2,1)S(1)}, u32[]{:S(2)}, u32[]{:S(2)}) collective-permute-start(bf16[400,128]{1,0:T(8,128)(2,1)S(1)} %get-tuple-element.74), channel_id=1, source_target_pairs={{0,7},{1,0},{2,1},{3,2},{4,3},{5,4},{6,5},{7,6},{8,15},{9,8},{10,9... | collective-permute-start | bytes 307208 | tf_op jit(solution)/shard_map/ppermute | solution.py:752
  22.1 6.5 %collective-permute-start.7 = (bf16[64,512]{1,0:T(8,128)(2,1)S(1)}, bf16[64,512]{1,0:T(8,128)(2,1)S(1)}, u32[]{:S(2)}, u32[]{:S(2)}) collective-permute-start(bf16[64,512]{1,0:T(8,128)(2,1)S(1)} %get-tuple-element.78), channel_id=1, source_target_pairs={{0,1},{2,3},{4,5},{6,7},{1,0},{3,2},{5,4},{7,6},{8,9},{10,11},{12,... | collective-permute-start | bytes 196616 | tf_op jit(solution)/shard_map/ppermute | solution.py:758
  26.4 2.2 %collective-permute-start.8 = (bf16[64,512]{1,0:T(8,128)(2,1)S(1)}, bf16[64,512]{1,0:T(8,128)(2,1)S(1)}, u32[]{:S(2)}, u32[]{:S(2)}) collective-permute-start(bf16[64,512]{1,0:T(8,128)(2,1)S(1)} %get-tuple-element.79), channel_id=1, source_target_pairs={{1,2},{3,4},{5,6},{2,1},{4,3},{6,5},{9,10},{11,12},{13,14},{10,9},... | collective-permute-start | bytes 196616 | tf_op jit(solution)/shard_map/ppermute | solution.py:758
  44.5 11.9 %collective-permute-start.18 = (bf16[3584,256]{1,0:T(8,128)(2,1)S(1)}, bf16[3584,256]{1,0:T(8,128)(2,1)S(1)}, u32[]{:S(2)}, u32[]{:S(2)}) collective-permute-start(bf16[3584,256]{1,0:T(8,128)(2,1)S(1)} %get-tuple-element.112), channel_id=1, source_target_pairs={{0,8},{8,0},{16,24},{24,16},{1,9},{9,1},{17,25},{25,17},{2,10},{10... | collective-permute-start | bytes 5505032 | tf_op jit(solution)/shard_map/ppermute | solution.py:567
  45.4 10.2 %collective-permute-start.9 = (bf16[64,512]{1,0:T(8,128)(2,1)S(1)}, bf16[64,512]{1,0:T(8,128)(2,1)S(1)}, u32[]{:S(2)}, u32[]{:S(2)}) collective-permute-start(bf16[64,512]{1,0:T(8,128)(2,1)S(1)} %get-tuple-element.97), channel_id=1, source_target_pairs={{0,1},{2,3},{4,5},{6,7},{1,0},{3,2},{5,4},{7,6},{8,9},{10,11},{12,... | collective-permute-start | bytes 196616 | tf_op jit(solution)/shard_map/ppermute | solution.py:758
  52.8 2.8 %collective-permute-start.10 = (bf16[64,512]{1,0:T(8,128)(2,1)S(1)}, bf16[64,512]{1,0:T(8,128)(2,1)S(1)}, u32[]{:S(2)}, u32[]{:S(2)}) collective-permute-start(bf16[64,512]{1,0:T(8,128)(2,1)S(1)} %get-tuple-element.98), channel_id=1, source_target_pairs={{1,2},{3,4},{5,6},{2,1},{4,3},{6,5},{9,10},{11,12},{13,14},{10,9},... | collective-permute-start | bytes 196616 | tf_op jit(solution)/shard_map/ppermute | solution.py:758
  57.0 23.6 %collective-permute-start.19 = (bf16[8,224,128]{2,1,0:T(8,128)(2,1)S(1)}, bf16[8,224,128]{2,1,0:T(8,128)(2,1)S(1)}, u32[]{:S(2)}, u32[]{:S(2)}) collective-permute-start(bf16[8,224,128]{2,1,0:T(8,128)(2,1)S(1)} %get-tuple-element.117), channel_id=1, source_target_pairs={{0,16},{8,24},{16,0},{24,8},{1,17},{9,25},{17,1},{25,9},{2,18},{10... | collective-permute-start | bytes 1376264 | tf_op jit(solution)/shard_map/ppermute | solution.py:567
  58.6 29.5 %collective-permute-start.21 = (bf16[4,224,256]{2,1,0:T(8,128)(2,1)S(1)}, bf16[4,224,256]{2,1,0:T(8,128)(2,1)S(1)}, u32[]{:S(2)}, u32[]{:S(2)}) collective-permute-start(bf16[4,224,256]{2,1,0:T(8,128)(2,1)S(1)} %get-tuple-element.120), channel_id=1, source_target_pairs={{0,1},{1,0},{2,3},{3,2},{4,5},{5,4},{6,7},{7,6},{8,9},{9,8},{10,11... | collective-permute-start | bytes 1376264 | tf_op jit(solution)/shard_map/ppermute | solution.py:567
  63.4 6.7 %collective-permute-start.13 = (bf16[384,128]{1,0:T(8,128)(2,1)S(1)}, bf16[384,128]{1,0:T(8,128)(2,1)S(1)}, u32[]{:S(2)}, u32[]{:S(2)}) collective-permute-start(bf16[384,128]{1,0:T(8,128)(2,1)S(1)} %get-tuple-element.103), channel_id=1, source_target_pairs={{0,5},{1,6},{2,7},{3,0},{4,1},{5,2},{6,3},{7,4},{8,13},{9,14},{10,... | collective-permute-start | bytes 294920 | tf_op jit(solution)/shard_map/ppermute | solution.py:752
  66.8 11.8 %collective-permute-start.14 = (bf16[384,128]{1,0:T(8,128)(2,1)S(1)}, bf16[384,128]{1,0:T(8,128)(2,1)S(1)}, u32[]{:S(2)}, u32[]{:S(2)}) collective-permute-start(bf16[384,128]{1,0:T(8,128)(2,1)S(1)} %get-tuple-element.104), channel_id=1, source_target_pairs={{0,4},{1,5},{2,6},{3,7},{4,0},{5,1},{6,2},{7,3},{8,12},{9,13},{10,... | collective-permute-start | bytes 294920 | tf_op jit(solution)/shard_map/ppermute | solution.py:752
  67.1 12.9 %collective-permute-start.15 = (bf16[384,128]{1,0:T(8,128)(2,1)S(1)}, bf16[384,128]{1,0:T(8,128)(2,1)S(1)}, u32[]{:S(2)}, u32[]{:S(2)}) collective-permute-start(bf16[384,128]{1,0:T(8,128)(2,1)S(1)} %get-tuple-element.105), channel_id=1, source_target_pairs={{0,3},{1,4},{2,5},{3,6},{4,7},{5,0},{6,1},{7,2},{8,11},{9,12},{10,... | collective-permute-start | bytes 294920 | tf_op jit(solution)/shard_map/ppermute | solution.py:752
  70.0 10.8 %collective-permute-start.11 = (bf16[384,128]{1,0:T(8,128)(2,1)S(1)}, bf16[384,128]{1,0:T(8,128)(2,1)S(1)}, u32[]{:S(2)}, u32[]{:S(2)}) collective-permute-start(bf16[384,128]{1,0:T(8,128)(2,1)S(1)} %get-tuple-element.101), channel_id=1, source_target_pairs={{0,7},{1,0},{2,1},{3,2},{4,3},{5,4},{6,5},{7,6},{8,15},{9,8},{10,9... | collective-permute-start | bytes 294920 | tf_op jit(solution)/shard_map/ppermute | solution.py:752
  78.6 5.7 %collective-permute-start.12 = (bf16[384,128]{1,0:T(8,128)(2,1)S(1)}, bf16[384,128]{1,0:T(8,128)(2,1)S(1)}, u32[]{:S(2)}, u32[]{:S(2)}) collective-permute-start(bf16[384,128]{1,0:T(8,128)(2,1)S(1)} %get-tuple-element.102), channel_id=1, source_target_pairs={{0,6},{1,7},{2,0},{3,1},{4,2},{5,3},{6,4},{7,5},{8,14},{9,15},{10,... | collective-permute-start | bytes 294920 | tf_op jit(solution)/shard_map/ppermute | solution.py:752
  80.0 6.4 %collective-permute-start.16 = (bf16[384,128]{1,0:T(8,128)(2,1)S(1)}, bf16[384,128]{1,0:T(8,128)(2,1)S(1)}, u32[]{:S(2)}, u32[]{:S(2)}) collective-permute-start(bf16[384,128]{1,0:T(8,128)(2,1)S(1)} %get-tuple-element.106), channel_id=1, source_target_pairs={{0,2},{1,3},{2,4},{3,5},{4,6},{5,7},{6,0},{7,1},{8,10},{9,11},{10,... | collective-permute-start | bytes 294920 | tf_op jit(solution)/shard_map/ppermute | solution.py:752
  80.6 7.4 %collective-permute-start.17 = (bf16[384,128]{1,0:T(8,128)(2,1)S(1)}, bf16[384,128]{1,0:T(8,128)(2,1)S(1)}, u32[]{:S(2)}, u32[]{:S(2)}) collective-permute-start(bf16[384,128]{1,0:T(8,128)(2,1)S(1)} %get-tuple-element.107), channel_id=1, source_target_pairs={{0,1},{1,2},{2,3},{3,4},{4,5},{5,6},{6,7},{7,0},{8,9},{9,10},{10,1... | collective-permute-start | bytes 294920 | tf_op jit(solution)/shard_map/ppermute | solution.py:752
  80.8 12.5 %collective-permute-start.20 = (bf16[4,224,128]{2,1,0:T(8,128)(2,1)S(1)}, bf16[4,224,128]{2,1,0:T(8,128)(2,1)S(1)}, u32[]{:S(2)}, u32[]{:S(2)}) collective-permute-start(bf16[4,224,128]{2,1,0:T(8,128)(2,1)S(1)} %get-tuple-element.119), channel_id=1, source_target_pairs={{0,1},{1,0},{2,3},{3,2},{4,5},{5,4},{6,7},{7,6},{8,9},{9,8},{10,11... | collective-permute-start | bytes 688136 | tf_op jit(solution)/shard_map/ppermute | solution.py:567
  88.2 6.1 %collective-permute-start.22 = (bf16[4,224,128]{2,1,0:T(8,128)(2,1)S(1)}, bf16[4,224,128]{2,1,0:T(8,128)(2,1)S(1)}, u32[]{:S(2)}, u32[]{:S(2)}) collective-permute-start(bf16[4,224,128]{2,1,0:T(8,128)(2,1)S(1)} %get-tuple-element.122), channel_id=1, source_target_pairs={{0,16},{8,24},{16,0},{24,8},{1,17},{9,25},{17,1},{25,9},{2,18},{10... | collective-permute-start | bytes 688136 | tf_op jit(solution)/shard_map/ppermute | solution.py:567
  88.8 10.3 %copy-start = (s32[1,512]{1,0:T(1,128)S(1)}, s32[1,512]{1,0:T(1,128)}, u32[]{:S(2)}) copy-start(s32[1,512]{1,0:T(1,128)} %refs_0_.3) | copy-start | bytes 6148
  94.6 6.8 %collective-permute-start.23 = (bf16[448,128]{1,0:T(8,128)(2,1)S(1)}, bf16[448,128]{1,0:T(8,128)(2,1)S(1)}, u32[]{:S(2)}, u32[]{:S(2)}) collective-permute-start(bf16[448,128]{1,0:T(8,128)(2,1)S(1)} %get-tuple-element.125), channel_id=1, source_target_pairs={{0,6},{1,7},{2,4},{3,5},{4,2},{5,3},{6,0},{7,1},{8,14},{9,15},{10,... | collective-permute-start | bytes 344072 | tf_op jit(solution)/shard_map/ppermute | solution.py:567
  96.1 7.7 %collective-permute-start.24 = (bf16[448,128]{1,0:T(8,128)(2,1)S(1)}, bf16[448,128]{1,0:T(8,128)(2,1)S(1)}, u32[]{:S(2)}, u32[]{:S(2)}) collective-permute-start(bf16[448,128]{1,0:T(8,128)(2,1)S(1)} %get-tuple-element.126), channel_id=1, source_target_pairs={{0,4},{1,5},{2,6},{3,7},{4,0},{5,1},{6,2},{7,3},{8,12},{9,13},{10,... | collective-permute-start | bytes 344072 | tf_op jit(solution)/shard_map/ppermute | solution.py:567
  96.1 7.7 %collective-permute-start.25 = (bf16[448,128]{1,0:T(8,128)(2,1)S(1)}, bf16[448,128]{1,0:T(8,128)(2,1)S(1)}, u32[]{:S(2)}, u32[]{:S(2)}) collective-permute-start(bf16[448,128]{1,0:T(8,128)(2,1)S(1)} %get-tuple-element.127), channel_id=1, source_target_pairs={{0,2},{1,3},{2,0},{3,1},{4,6},{5,7},{6,4},{7,5},{8,10},{9,11},{10,... | collective-permute-start | bytes 344072 | tf_op jit(solution)/shard_map/ppermute | solution.py:567
  103.8 4.9 %collective-permute-start.26 = (bf16[448,128]{1,0:T(8,128)(2,1)S(1)}, bf16[448,128]{1,0:T(8,128)(2,1)S(1)}, u32[]{:S(2)}, u32[]{:S(2)}) collective-permute-start(bf16[448,128]{1,0:T(8,128)(2,1)S(1)} %sum.1.refs_0_), channel_id=1, source_target_pairs={{0,16},{8,24},{16,0},{24,8},{1,17},{9,25},{17,1},{25,9},{2,18},{10... | collective-permute-start | bytes 344072 | tf_op jit(solution)/shard_map/ppermute | solution.py:567
  108.7 1.6 %collective-permute-start.27 = (bf16[448,256]{1,0:T(8,128)(2,1)S(1)}, bf16[448,256]{1,0:T(8,128)(2,1)S(1)}, u32[]{:S(2)}, u32[]{:S(2)}) collective-permute-start(bf16[448,256]{1,0:T(8,128)(2,1)S(1)} %join.2.refs_0_), channel_id=1, source_target_pairs={{0,8},{8,0},{16,24},{24,16},{1,9},{9,1},{17,25},{25,17},{2,10},{10... | collective-permute-start | bytes 688136 | tf_op jit(solution)/shard_map/ppermute | solution.py:567

commit v4 on v3

--- a/solution.py
+++ b/solution.py
@@ -293,7 +293,6 @@
     hidden_ref,
     slope_ref,
     normed_ref,
-    inverse_ref,
     summed_ref,
     post_grad_ref,
     wide_ref,
@@ -316,6 +315,7 @@
     table_ref[:padded, :] = dot_nn(cells_ref[...], w_edge_in_ref[width : 2 * width, :]).astype(BF16)
     recv_ref[...] = dot_nn(nodes_ref[...], w_edge_in_ref[2 * width :, :]).astype(BF16)
 
+    inverses = []
     for step in range(steps):
         spot = slice(step * cells, (step + 1) * cells)
         rows = slice(step * EDGE_BLOCK, (step + 1) * EDGE_BLOCK)
@@ -328,7 +328,7 @@
         slope_ref[rows, :] = (gate * (1.0 + pre * (1.0 - gate))).astype(BF16)
         normed, inverse = normalize(dot_nn(hidden, w_edge_out_ref[...]))
         normed_ref[rows, :] = normed.astype(BF16)
-        inverse_ref[rows, :] = inverse
+        inverses.append(inverse)
         edge_new = (edges.astype(F32) + normed).astype(BF16)
         post_grad_ref[rows, :] = edge_new
         summed_ref[spot, :] = collect_rows(wide_ref, 0, edge_new.astype(F32), fan_in).astype(BF16)
@@ -362,7 +362,7 @@
             wide_ref, base, summed_grad_ref[spot, :], fan_in
         )
         post_grad = normalize_back(
-            normed_ref[rows, :].astype(F32), inverse_ref[rows, :], upstream
+            normed_ref[rows, :].astype(F32), inverses[step], upstream
         )
         post_grad = post_grad.astype(BF16)
         post_grad_ref[rows, :] = post_grad
@@ -858,7 +858,6 @@
             VMEM(by_edge, BF16),
             VMEM(by_edge, BF16),
             VMEM(by_edge, BF16),
-            VMEM((edge_count, 1), F32),
             VMEM(by_cell, BF16),
             VMEM(by_edge, BF16),
             VMEM((2 * width // LANES, EDGE_BLOCK, LANES), F32),

time: 112 us -> 111 us (level)
  no operation moved by 1% of the time
where the time goes in v4:
time: 111 us
  starting transfers between devices  59.3 us (53%)
  Pallas kernels  33.2 us (30%)
  waiting for transfers between devices  17.7 us (16%)
    ppermute x14, starting transfers between devices, shift(): lax.ppermute(value, 'dom', [(at, (at + steps) % count) for at in range(co...  30.1 us
    ppermute x10, starting transfers between devices, swap(): return lax.ppermute(value, axis, [(at, at ^ bit) for at in range(count)])  15.9 us
    pallas_call x1, Pallas kernels, run_main(): pl.pallas_call(placed(main_kernel, fan_in, scale), out_shape=[shape(by_ed...  15.5 us
    ppermute x4, starting transfers between devices, neighbour(): lax.ppermute(value, 'dom', pairs + [(right, left) for left, right in pairs])  13.3 us
    ppermute x10, waiting for transfers between devices, swap(): return lax.ppermute(value, axis, [(at, at ^ bit) for at in range(count)])  9.31 us
    ppermute x14, waiting for transfers between devices, shift(): lax.ppermute(value, 'dom', [(at, (at + steps) % count) for at in range(co...  4.88 us
    pallas_call x1, Pallas kernels, run_edges(): pl.pallas_call(functools.partial(edge_kernel, fan_in), out_shape=[shape((...  4.5 us
    pallas_call x1, Pallas kernels, run_prep(): pl.pallas_call(placed(prep_kernel, fan_in, cell_count), out_shape=[near_s...  4.47 us
  transfers between devices with their start and end apart: 28, of which 12 were waited for; matrix products, arithmetic and copies ran while one was open for 0% of the time, Pallas kernels for 11%

profile of v4, /device:TPU:0, one launch (start us, length us, event | category | flops | bytes accessed | tf_op | source)
XLA Modules:
  0.0 111.1 jit_solution(1221801742823019655)
XLA Ops:
  0.6 2.1 %pack.1 = (bf16[400,128]{1,0:T(8,128)(2,1)S(1)}, bf16[400,128]{1,0:T(8,128)(2,1)S(1)}, bf16[400,128]{1,0:T(8,128)(2,1)S(1)}, bf16[400,128]{1,0:T(8,128)(2,1)S(1)...) custom-call(bf16[512,512]{1,0:T(8,128)(2,1)} %bitcast.12, ...), custom_call_target="tpu_custom_call" | custom-call | tf_op jit(solution)/shard_map/pack/pallas_call | solution.py:921
  2.7 3.0 %collective-permute-start = (bf16[400,128]{1,0:T(8,128)(2,1)S(1)}, bf16[400,128]{1,0:T(8,128)(2,1)S(1)}, u32[]{:S(2)}, u32[]{:S(2)}) collective-permute-start(bf16[400,128]{1,0:T(8,128)(2,1)S(1)} %get-tuple-element.68), channel_id=1, source_target_pairs={{0,1},{1,2},{2,3},{3,4},{4,5},{5,6},{6,7},{7,0},{8,9},{9,10},{10,1... | collective-permute-start | bytes 307208 | tf_op jit(solution)/shard_map/ppermute | solution.py:752
  5.8 1.6 %collective-permute-start.1 = (bf16[400,128]{1,0:T(8,128)(2,1)S(1)}, bf16[400,128]{1,0:T(8,128)(2,1)S(1)}, u32[]{:S(2)}, u32[]{:S(2)}) collective-permute-start(bf16[400,128]{1,0:T(8,128)(2,1)S(1)} %get-tuple-element.69), channel_id=1, source_target_pairs={{0,2},{1,3},{2,4},{3,5},{4,6},{5,7},{6,0},{7,1},{8,10},{9,11},{10,... | collective-permute-start | bytes 307208 | tf_op jit(solution)/shard_map/ppermute | solution.py:752
  7.3 2.5 %collective-permute-start.2 = (bf16[400,128]{1,0:T(8,128)(2,1)S(1)}, bf16[400,128]{1,0:T(8,128)(2,1)S(1)}, u32[]{:S(2)}, u32[]{:S(2)}) collective-permute-start(bf16[400,128]{1,0:T(8,128)(2,1)S(1)} %get-tuple-element.70), channel_id=1, source_target_pairs={{0,3},{1,4},{2,5},{3,6},{4,7},{5,0},{6,1},{7,2},{8,11},{9,12},{10,... | collective-permute-start | bytes 307208 | tf_op jit(solution)/shard_map/ppermute | solution.py:752
  9.9 1.2 %collective-permute-start.3 = (bf16[400,128]{1,0:T(8,128)(2,1)S(1)}, bf16[400,128]{1,0:T(8,128)(2,1)S(1)}, u32[]{:S(2)}, u32[]{:S(2)}) collective-permute-start(bf16[400,128]{1,0:T(8,128)(2,1)S(1)} %get-tuple-element.71), channel_id=1, source_target_pairs={{0,4},{1,5},{2,6},{3,7},{4,0},{5,1},{6,2},{7,3},{8,12},{9,13},{10,... | collective-permute-start | bytes 307208 | tf_op jit(solution)/shard_map/ppermute | solution.py:752
  11.1 2.6 %collective-permute-start.4 = (bf16[400,128]{1,0:T(8,128)(2,1)S(1)}, bf16[400,128]{1,0:T(8,128)(2,1)S(1)}, u32[]{:S(2)}, u32[]{:S(2)}) collective-permute-start(bf16[400,128]{1,0:T(8,128)(2,1)S(1)} %get-tuple-element.72), channel_id=1, source_target_pairs={{0,5},{1,6},{2,7},{3,0},{4,1},{5,2},{6,3},{7,4},{8,13},{9,14},{10,... | collective-permute-start | bytes 307208 | tf_op jit(solution)/shard_map/ppermute | solution.py:752
  13.7 1.3 %collective-permute-start.5 = (bf16[400,128]{1,0:T(8,128)(2,1)S(1)}, bf16[400,128]{1,0:T(8,128)(2,1)S(1)}, u32[]{:S(2)}, u32[]{:S(2)}) collective-permute-start(bf16[400,128]{1,0:T(8,128)(2,1)S(1)} %get-tuple-element.73), channel_id=1, source_target_pairs={{0,6},{1,7},{2,0},{3,1},{4,2},{5,3},{6,4},{7,5},{8,14},{9,15},{10,... | collective-permute-start | bytes 307208 | tf_op jit(solution)/shard_map/ppermute | solution.py:752
  15.1 1.4 %collective-permute-start.6 = (bf16[400,128]{1,0:T(8,128)(2,1)S(1)}, bf16[400,128]{1,0:T(8,128)(2,1)S(1)}, u32[]{:S(2)}, u32[]{:S(2)}) collective-permute-start(bf16[400,128]{1,0:T(8,128)(2,1)S(1)} %get-tuple-element.74), channel_id=1, source_target_pairs={{0,7},{1,0},{2,1},{3,2},{4,3},{5,4},{6,5},{7,6},{8,15},{9,8},{10,9... | collective-permute-start | bytes 307208 | tf_op jit(solution)/shard_map/ppermute | solution.py:752
  16.5 4.5 %prep.1 = (bf16[2048,512]{1,0:T(8,128)(2,1)S(1)}, bf16[512,512]{1,0:T(8,128)(2,1)S(1)}, bf16[2048,512]{1,0:T(8,128)(2,1)S(1)}, bf16[1536,512]{1,0:T(8,128)(2,1)S...) custom-call(s32[1,2048]{1,0:T(1,128)} %refs_0_.2, ...), custom_call_target="tpu_custom_call" | custom-call | flops 2147483648 | bytes 20971520 | tf_op jit(solution)/shard_map/prep/pallas_call | solution.py:790
  21.0 0.2 collective-permute-done.3.refs_4_
  21.3 0.8 unpack.1
  22.1 4.3 %collective-permute-start.7 = (bf16[64,512]{1,0:T(8,128)(2,1)S(1)}, bf16[64,512]{1,0:T(8,128)(2,1)S(1)}, u32[]{:S(2)}, u32[]{:S(2)}) collective-permute-start(bf16[64,512]{1,0:T(8,128)(2,1)S(1)} %get-tuple-element.78), channel_id=1, source_target_pairs={{0,1},{2,3},{4,5},{6,7},{1,0},{3,2},{5,4},{7,6},{8,9},{10,11},{12,... | collective-permute-start | bytes 196616 | tf_op jit(solution)/shard_map/ppermute | solution.py:758
  26.4 0.8 collective-permute-start.8
  27.2 1.4 %collective-permute-done.7.refs_1_ = bf16[64,512]{1,0:T(8,128)(2,1)S(1)} collective-permute-done((bf16[64,512]{1,0:T(8,128)(2,1)S(1)}, bf16[64,512]{1,0:T(8,128)(2,1)S(1)}, u32[]{:S(2)}, u32[]{:S(2)}) %collective-permute-start.7) | collective-permute-done | bytes 65568 | tf_op jit(solution)/shard_map/ppermute | solution.py:758
  28.7 15.5 %main.1 = (bf16[2048,512]{1,0:T(8,128)(2,1)}, bf16[512,512]{1,0:T(8,128)(2,1)}, bf16[2048,512]{1,0:T(8,128)(2,1)}, f32[512,512]{1,0:T(8,128)}, bf16[640,512]{1,0...) custom-call(bf16[512,512]{1,0:T(8,128)(2,1)S(1)} %get-tuple-element., ...), custom_call_target="tpu_custom_call" | custom-call | flops 15032385536 | bytes 16777216 | tf_op jit(solution)/shard_map/main/pallas_call | solution.py:836
  44.3 0.8 cells.1
  45.1 7.5 %collective-permute-start.9 = (bf16[64,512]{1,0:T(8,128)(2,1)S(1)}, bf16[64,512]{1,0:T(8,128)(2,1)S(1)}, u32[]{:S(2)}, u32[]{:S(2)}) collective-permute-start(bf16[64,512]{1,0:T(8,128)(2,1)S(1)} %get-tuple-element.97), channel_id=1, source_target_pairs={{0,1},{2,3},{4,5},{6,7},{1,0},{3,2},{5,4},{7,6},{8,9},{10,11},{12,... | collective-permute-start | bytes 196616 | tf_op jit(solution)/shard_map/ppermute | solution.py:758
  52.6 0.7 collective-permute-start.10
  53.3 2.1 %collective-permute-done.9.refs_2_ = bf16[64,512]{1,0:T(8,128)(2,1)S(1)} collective-permute-done((bf16[64,512]{1,0:T(8,128)(2,1)S(1)}, bf16[64,512]{1,0:T(8,128)(2,1)S(1)}, u32[]{:S(2)}, u32[]{:S(2)}) %collective-permute-start.9) | collective-permute-done | bytes 65568 | tf_op jit(solution)/shard_map/ppermute | solution.py:758
  55.4 0.8 returning.1
  56.2 0.6 core.1
  56.8 1.5 %collective-permute-start.19 = (bf16[8,224,128]{2,1,0:T(8,128)(2,1)S(1)}, bf16[8,224,128]{2,1,0:T(8,128)(2,1)S(1)}, u32[]{:S(2)}, u32[]{:S(2)}) collective-permute-start(bf16[8,224,128]{2,1,0:T(8,128)(2,1)S(1)} %get-tuple-element.117), channel_id=1, source_target_pairs={{0,16},{8,24},{16,0},{24,8},{1,17},{9,25},{17,1},{25,9},{2,18},{10... | collective-permute-start | bytes 1376264 | tf_op jit(solution)/shard_map/ppermute | solution.py:567
  58.3 4.8 %collective-permute-start.21 = (bf16[4,224,256]{2,1,0:T(8,128)(2,1)S(1)}, bf16[4,224,256]{2,1,0:T(8,128)(2,1)S(1)}, u32[]{:S(2)}, u32[]{:S(2)}) collective-permute-start(bf16[4,224,256]{2,1,0:T(8,128)(2,1)S(1)} %get-tuple-element.120), channel_id=1, source_target_pairs={{0,1},{1,0},{2,3},{3,2},{4,5},{5,4},{6,7},{7,6},{8,9},{9,8},{10,11... | collective-permute-start | bytes 1376264 | tf_op jit(solution)/shard_map/ppermute | solution.py:567
  63.1 3.4 %collective-permute-start.13 = (bf16[384,128]{1,0:T(8,128)(2,1)S(1)}, bf16[384,128]{1,0:T(8,128)(2,1)S(1)}, u32[]{:S(2)}, u32[]{:S(2)}) collective-permute-start(bf16[384,128]{1,0:T(8,128)(2,1)S(1)} %get-tuple-element.103), channel_id=1, source_target_pairs={{0,5},{1,6},{2,7},{3,0},{4,1},{5,2},{6,3},{7,4},{8,13},{9,14},{10,... | collective-permute-start | bytes 294920 | tf_op jit(solution)/shard_map/ppermute | solution.py:752
  66.6 0.3 collective-permute-start.14
  66.9 2.9 %collective-permute-start.15 = (bf16[384,128]{1,0:T(8,128)(2,1)S(1)}, bf16[384,128]{1,0:T(8,128)(2,1)S(1)}, u32[]{:S(2)}, u32[]{:S(2)}) collective-permute-start(bf16[384,128]{1,0:T(8,128)(2,1)S(1)} %get-tuple-element.105), channel_id=1, source_target_pairs={{0,3},{1,4},{2,5},{3,6},{4,7},{5,0},{6,1},{7,2},{8,11},{9,12},{10,... | collective-permute-start | bytes 294920 | tf_op jit(solution)/shard_map/ppermute | solution.py:752
  69.8 7.7 %collective-permute-start.11 = (bf16[384,128]{1,0:T(8,128)(2,1)S(1)}, bf16[384,128]{1,0:T(8,128)(2,1)S(1)}, u32[]{:S(2)}, u32[]{:S(2)}) collective-permute-start(bf16[384,128]{1,0:T(8,128)(2,1)S(1)} %get-tuple-element.101), channel_id=1, source_target_pairs={{0,7},{1,0},{2,1},{3,2},{4,3},{5,4},{6,5},{7,6},{8,15},{9,8},{10,9... | collective-permute-start | bytes 294920 | tf_op jit(solution)/shard_map/ppermute | solution.py:752
  77.5 0.9 collective-permute-done.14.refs_5_.refs_2_
  78.3 1.4 %collective-permute-start.12 = (bf16[384,128]{1,0:T(8,128)(2,1)S(1)}, bf16[384,128]{1,0:T(8,128)(2,1)S(1)}, u32[]{:S(2)}, u32[]{:S(2)}) collective-permute-start(bf16[384,128]{1,0:T(8,128)(2,1)S(1)} %get-tuple-element.102), channel_id=1, source_target_pairs={{0,6},{1,7},{2,0},{3,1},{4,2},{5,3},{6,4},{7,5},{8,14},{9,15},{10,... | collective-permute-start | bytes 294920 | tf_op jit(solution)/shard_map/ppermute | solution.py:752
  79.7 0.6 collective-permute-start.16
  80.4 0.2 stage.2
  80.6 3.5 %collective-permute-start.20 = (bf16[4,224,128]{2,1,0:T(8,128)(2,1)S(1)}, bf16[4,224,128]{2,1,0:T(8,128)(2,1)S(1)}, u32[]{:S(2)}, u32[]{:S(2)}) collective-permute-start(bf16[4,224,128]{2,1,0:T(8,128)(2,1)S(1)} %get-tuple-element.119), channel_id=1, source_target_pairs={{0,1},{1,0},{2,3},{3,2},{4,5},{5,4},{6,7},{7,6},{8,9},{9,8},{10,11... | collective-permute-start | bytes 688136 | tf_op jit(solution)/shard_map/ppermute | solution.py:567
  84.1 2.0 %collective-permute-done.16.refs_7_.refs_6_ = bf16[384,128]{1,0:T(8,128)(2,1)S(1)} collective-permute-done((bf16[384,128]{1,0:T(8,128)(2,1)S(1)}, bf16[384,128]{1,0:T(8,128)(2,1)S(1)}, u32[]{:S(2)}, u32[]{:S(2)}) %collective-permute-start.16) | collective-permute-done | bytes 98336 | tf_op jit(solution)/shard_map/ppermute | solution.py:752
  86.1 1.7 %collective-permute-done.17.refs_8_ = bf16[384,128]{1,0:T(8,128)(2,1)S(1)} collective-permute-done((bf16[384,128]{1,0:T(8,128)(2,1)S(1)}, bf16[384,128]{1,0:T(8,128)(2,1)S(1)}, u32[]{:S(2)}, u32[]{:S(2)}) %collective-permute-start.17) | collective-permute-done | bytes 98336 | tf_op jit(solution)/shard_map/ppermute | solution.py:752
  87.8 0.2 stage.3
  88.0 0.6 collective-permute-start.22
  88.5 4.5 %edges.1 = (bf16[2048,512]{1,0:T(8,128)(2,1)}, f32[8,128]{1,0:T(8,128)S(1)}) custom-call(bf16[2048,512]{1,0:T(8,128)(2,1)} %bitcast.9, f32[512,512]{1,0:T(8,128)} %get-tuple-element.109.summed_grad_hbm, bf16[2048,512]{1,0:T(8,128)(2,1)} %get-tuple-element.110.pre_grad_hbm, bf16[1536,512]{1,0:T(8,128)(2,1)} %w_edge_in_hbm.1, f32[8,128]{1,0:T(8,128)S(1)} %get-tuple-element.114._), custom_call_target="tpu_custom_call" | custom-call | flops 1 | bytes 1 | tf_op jit(solution)/shard_map/edges/pallas_call | solution.py:876
  93.1 1.0 collective-permute-done.22.refs_3_
  94.1 0.3 split.1
  94.4 1.4 %collective-permute-start.23 = (bf16[448,128]{1,0:T(8,128)(2,1)S(1)}, bf16[448,128]{1,0:T(8,128)(2,1)S(1)}, u32[]{:S(2)}, u32[]{:S(2)}) collective-permute-start(bf16[448,128]{1,0:T(8,128)(2,1)S(1)} %get-tuple-element.125), channel_id=1, source_target_pairs={{0,6},{1,7},{2,4},{3,5},{4,2},{5,3},{6,0},{7,1},{8,14},{9,15},{10,... | collective-permute-start | bytes 344072 | tf_op jit(solution)/shard_map/ppermute | solution.py:567
  95.9 3.0 %collective-permute-start.25 = (bf16[448,128]{1,0:T(8,128)(2,1)S(1)}, bf16[448,128]{1,0:T(8,128)(2,1)S(1)}, u32[]{:S(2)}, u32[]{:S(2)}) collective-permute-start(bf16[448,128]{1,0:T(8,128)(2,1)S(1)} %get-tuple-element.127), channel_id=1, source_target_pairs={{0,2},{1,3},{2,0},{3,1},{4,6},{5,7},{6,4},{7,5},{8,10},{9,11},{10,... | collective-permute-start | bytes 344072 | tf_op jit(solution)/shard_map/ppermute | solution.py:567
  98.9 1.8 %finish.1 = (bf16[512,512]{1,0:T(8,128)(2,1)}, f32[8,128]{1,0:T(8,128)S(1)}) custom-call(s32[1,512]{1,0:T(1,128)S(1)} %copy-done, bf16[384,128]{1,0:T(8,128)(2,1)S(1)} %get-tuple-element.100.refs_1_, bf16[384,128]{1,0:T(8,128)(2,1)S(1)} %collective-permute-done.11.refs_2_.refs_7_, bf16[384,128]{1,0:T(8,128)(2,1)S(1)} %collective-permute-done.12.refs_3_.refs_5_, ...), custom_call_target="tpu_custom_call" | custom-call | tf_op jit(solution)/shard_map/finish/pallas_call | solution.py:1020
  100.7 0.5 collective-permute-done.23.refs_1_
  101.2 2.3 %collective-permute-done.24.refs_2_ = bf16[448,128]{1,0:T(8,128)(2,1)S(1)} collective-permute-done((bf16[448,128]{1,0:T(8,128)(2,1)S(1)}, bf16[448,128]{1,0:T(8,128)(2,1)S(1)}, u32[]{:S(2)}, u32[]{:S(2)}) %collective-permute-start.24) | collective-permute-done | bytes 114720 | tf_op jit(solution)/shard_map/ppermute | solution.py:567
  103.6 0.9 collective-permute-start.26
  104.5 4.0 %collective-permute-done.26.refs_1_ = bf16[448,128]{1,0:T(8,128)(2,1)S(1)} collective-permute-done((bf16[448,128]{1,0:T(8,128)(2,1)S(1)}, bf16[448,128]{1,0:T(8,128)(2,1)S(1)}, u32[]{:S(2)}, u32[]{:S(2)}) %collective-permute-start.26) | collective-permute-done | bytes 114720 | tf_op jit(solution)/shard_map/ppermute | solution.py:567
  108.6 1.5 %collective-permute-done.27.refs_1_ = bf16[448,256]{1,0:T(8,128)(2,1)S(1)} collective-permute-done((bf16[448,256]{1,0:T(8,128)(2,1)S(1)}, bf16[448,256]{1,0:T(8,128)(2,1)S(1)}, u32[]{:S(2)}, u32[]{:S(2)}) %collective-permute-start.27) | collective-permute-done | bytes 229408 | tf_op jit(solution)/shard_map/ppermute | solution.py:567
  110.1 1.0 join.3
  (25 shorter events, 0.4 us)
Async XLA Ops:
  2.7 11.0 %collective-permute-start = (bf16[400,128]{1,0:T(8,128)(2,1)S(1)}, bf16[400,128]{1,0:T(8,128)(2,1)S(1)}, u32[]{:S(2)}, u32[]{:S(2)}) collective-permute-start(bf16[400,128]{1,0:T(8,128)(2,1)S(1)} %get-tuple-element.68), channel_id=1, source_target_pairs={{0,1},{1,2},{2,3},{3,4},{4,5},{5,6},{6,7},{7,0},{8,9},{9,10},{10,1... | collective-permute-start | bytes 307208 | tf_op jit(solution)/shard_map/ppermute | solution.py:752
  5.8 9.3 %collective-permute-start.1 = (bf16[400,128]{1,0:T(8,128)(2,1)S(1)}, bf16[400,128]{1,0:T(8,128)(2,1)S(1)}, u32[]{:S(2)}, u32[]{:S(2)}) collective-permute-start(bf16[400,128]{1,0:T(8,128)(2,1)S(1)} %get-tuple-element.69), channel_id=1, source_target_pairs={{0,2},{1,3},{2,4},{3,5},{4,6},{5,7},{6,0},{7,1},{8,10},{9,11},{10,... | collective-permute-start | bytes 307208 | tf_op jit(solution)/shard_map/ppermute | solution.py:752
  7.3 13.7 %collective-permute-start.2 = (bf16[400,128]{1,0:T(8,128)(2,1)S(1)}, bf16[400,128]{1,0:T(8,128)(2,1)S(1)}, u32[]{:S(2)}, u32[]{:S(2)}) collective-permute-start(bf16[400,128]{1,0:T(8,128)(2,1)S(1)} %get-tuple-element.70), channel_id=1, source_target_pairs={{0,3},{1,4},{2,5},{3,6},{4,7},{5,0},{6,1},{7,2},{8,11},{9,12},{10,... | collective-permute-start | bytes 307208 | tf_op jit(solution)/shard_map/ppermute | solution.py:752
  9.9 11.3 %collective-permute-start.3 = (bf16[400,128]{1,0:T(8,128)(2,1)S(1)}, bf16[400,128]{1,0:T(8,128)(2,1)S(1)}, u32[]{:S(2)}, u32[]{:S(2)}) collective-permute-start(bf16[400,128]{1,0:T(8,128)(2,1)S(1)} %get-tuple-element.71), channel_id=1, source_target_pairs={{0,4},{1,5},{2,6},{3,7},{4,0},{5,1},{6,2},{7,3},{8,12},{9,13},{10,... | collective-permute-start | bytes 307208 | tf_op jit(solution)/shard_map/ppermute | solution.py:752
  11.1 10.1 %collective-permute-start.4 = (bf16[400,128]{1,0:T(8,128)(2,1)S(1)}, bf16[400,128]{1,0:T(8,128)(2,1)S(1)}, u32[]{:S(2)}, u32[]{:S(2)}) collective-permute-start(bf16[400,128]{1,0:T(8,128)(2,1)S(1)} %get-tuple-element.72), channel_id=1, source_target_pairs={{0,5},{1,6},{2,7},{3,0},{4,1},{5,2},{6,3},{7,4},{8,13},{9,14},{10,... | collective-permute-start | bytes 307208 | tf_op jit(solution)/shard_map/ppermute | solution.py:752
  13.7 7.4 %collective-permute-start.5 = (bf16[400,128]{1,0:T(8,128)(2,1)S(1)}, bf16[400,128]{1,0:T(8,128)(2,1)S(1)}, u32[]{:S(2)}, u32[]{:S(2)}) collective-permute-start(bf16[400,128]{1,0:T(8,128)(2,1)S(1)} %get-tuple-element.73), channel_id=1, source_target_pairs={{0,6},{1,7},{2,0},{3,1},{4,2},{5,3},{6,4},{7,5},{8,14},{9,15},{10,... | collective-permute-start | bytes 307208 | tf_op jit(solution)/shard_map/ppermute | solution.py:752
  15.1 6.2 %collective-permute-start.6 = (bf16[400,128]{1,0:T(8,128)(2,1)S(1)}, bf16[400,128]{1,0:T(8,128)(2,1)S(1)}, u32[]{:S(2)}, u32[]{:S(2)}) collective-permute-start(bf16[400,128]{1,0:T(8,128)(2,1)S(1)} %get-tuple-element.74), channel_id=1, source_target_pairs={{0,7},{1,0},{2,1},{3,2},{4,3},{5,4},{6,5},{7,6},{8,15},{9,8},{10,9... | collective-permute-start | bytes 307208 | tf_op jit(solution)/shard_map/ppermute | solution.py:752
  22.1 6.5 %collective-permute-start.7 = (bf16[64,512]{1,0:T(8,128)(2,1)S(1)}, bf16[64,512]{1,0:T(8,128)(2,1)S(1)}, u32[]{:S(2)}, u32[]{:S(2)}) collective-permute-start(bf16[64,512]{1,0:T(8,128)(2,1)S(1)} %get-tuple-element.78), channel_id=1, source_target_pairs={{0,1},{2,3},{4,5},{6,7},{1,0},{3,2},{5,4},{7,6},{8,9},{10,11},{12,... | collective-permute-start | bytes 196616 | tf_op jit(solution)/shard_map/ppermute | solution.py:758
  26.4 2.2 %collective-permute-start.8 = (bf16[64,512]{1,0:T(8,128)(2,1)S(1)}, bf16[64,512]{1,0:T(8,128)(2,1)S(1)}, u32[]{:S(2)}, u32[]{:S(2)}) collective-permute-start(bf16[64,512]{1,0:T(8,128)(2,1)S(1)} %get-tuple-element.79), channel_id=1, source_target_pairs={{1,2},{3,4},{5,6},{2,1},{4,3},{6,5},{9,10},{11,12},{13,14},{10,9},... | collective-permute-start | bytes 196616 | tf_op jit(solution)/shard_map/ppermute | solution.py:758
  44.2 12.0 %collective-permute-start.18 = (bf16[3584,256]{1,0:T(8,128)(2,1)S(1)}, bf16[3584,256]{1,0:T(8,128)(2,1)S(1)}, u32[]{:S(2)}, u32[]{:S(2)}) collective-permute-start(bf16[3584,256]{1,0:T(8,128)(2,1)S(1)} %get-tuple-element.112), channel_id=1, source_target_pairs={{0,8},{8,0},{16,24},{24,16},{1,9},{9,1},{17,25},{25,17},{2,10},{10... | collective-permute-start | bytes 5505032 | tf_op jit(solution)/shard_map/ppermute | solution.py:567
  45.1 10.3 %collective-permute-start.9 = (bf16[64,512]{1,0:T(8,128)(2,1)S(1)}, bf16[64,512]{1,0:T(8,128)(2,1)S(1)}, u32[]{:S(2)}, u32[]{:S(2)}) collective-permute-start(bf16[64,512]{1,0:T(8,128)(2,1)S(1)} %get-tuple-element.97), channel_id=1, source_target_pairs={{0,1},{2,3},{4,5},{6,7},{1,0},{3,2},{5,4},{7,6},{8,9},{10,11},{12,... | collective-permute-start | bytes 196616 | tf_op jit(solution)/shard_map/ppermute | solution.py:758
  52.6 2.8 %collective-permute-start.10 = (bf16[64,512]{1,0:T(8,128)(2,1)S(1)}, bf16[64,512]{1,0:T(8,128)(2,1)S(1)}, u32[]{:S(2)}, u32[]{:S(2)}) collective-permute-start(bf16[64,512]{1,0:T(8,128)(2,1)S(1)} %get-tuple-element.98), channel_id=1, source_target_pairs={{1,2},{3,4},{5,6},{2,1},{4,3},{6,5},{9,10},{11,12},{13,14},{10,9},... | collective-permute-start | bytes 196616 | tf_op jit(solution)/shard_map/ppermute | solution.py:758
  56.8 23.6 %collective-permute-start.19 = (bf16[8,224,128]{2,1,0:T(8,128)(2,1)S(1)}, bf16[8,224,128]{2,1,0:T(8,128)(2,1)S(1)}, u32[]{:S(2)}, u32[]{:S(2)}) collective-permute-start(bf16[8,224,128]{2,1,0:T(8,128)(2,1)S(1)} %get-tuple-element.117), channel_id=1, source_target_pairs={{0,16},{8,24},{16,0},{24,8},{1,17},{9,25},{17,1},{25,9},{2,18},{10... | collective-permute-start | bytes 1376264 | tf_op jit(solution)/shard_map/ppermute | solution.py:567
  58.3 29.5 %collective-permute-start.21 = (bf16[4,224,256]{2,1,0:T(8,128)(2,1)S(1)}, bf16[4,224,256]{2,1,0:T(8,128)(2,1)S(1)}, u32[]{:S(2)}, u32[]{:S(2)}) collective-permute-start(bf16[4,224,256]{2,1,0:T(8,128)(2,1)S(1)} %get-tuple-element.120), channel_id=1, source_target_pairs={{0,1},{1,0},{2,3},{3,2},{4,5},{5,4},{6,7},{7,6},{8,9},{9,8},{10,11... | collective-permute-start | bytes 1376264 | tf_op jit(solution)/shard_map/ppermute | solution.py:567
  63.1 6.7 %collective-permute-start.13 = (bf16[384,128]{1,0:T(8,128)(2,1)S(1)}, bf16[384,128]{1,0:T(8,128)(2,1)S(1)}, u32[]{:S(2)}, u32[]{:S(2)}) collective-permute-start(bf16[384,128]{1,0:T(8,128)(2,1)S(1)} %get-tuple-element.103), channel_id=1, source_target_pairs={{0,5},{1,6},{2,7},{3,0},{4,1},{5,2},{6,3},{7,4},{8,13},{9,14},{10,... | collective-permute-start | bytes 294920 | tf_op jit(solution)/shard_map/ppermute | solution.py:752
  66.6 11.8 %collective-permute-start.14 = (bf16[384,128]{1,0:T(8,128)(2,1)S(1)}, bf16[384,128]{1,0:T(8,128)(2,1)S(1)}, u32[]{:S(2)}, u32[]{:S(2)}) collective-permute-start(bf16[384,128]{1,0:T(8,128)(2,1)S(1)} %get-tuple-element.104), channel_id=1, source_target_pairs={{0,4},{1,5},{2,6},{3,7},{4,0},{5,1},{6,2},{7,3},{8,12},{9,13},{10,... | collective-permute-start | bytes 294920 | tf_op jit(solution)/shard_map/ppermute | solution.py:752
  66.9 12.9 %collective-permute-start.15 = (bf16[384,128]{1,0:T(8,128)(2,1)S(1)}, bf16[384,128]{1,0:T(8,128)(2,1)S(1)}, u32[]{:S(2)}, u32[]{:S(2)}) collective-permute-start(bf16[384,128]{1,0:T(8,128)(2,1)S(1)} %get-tuple-element.105), channel_id=1, source_target_pairs={{0,3},{1,4},{2,5},{3,6},{4,7},{5,0},{6,1},{7,2},{8,11},{9,12},{10,... | collective-permute-start | bytes 294920 | tf_op jit(solution)/shard_map/ppermute | solution.py:752
  69.8 10.8 %collective-permute-start.11 = (bf16[384,128]{1,0:T(8,128)(2,1)S(1)}, bf16[384,128]{1,0:T(8,128)(2,1)S(1)}, u32[]{:S(2)}, u32[]{:S(2)}) collective-permute-start(bf16[384,128]{1,0:T(8,128)(2,1)S(1)} %get-tuple-element.101), channel_id=1, source_target_pairs={{0,7},{1,0},{2,1},{3,2},{4,3},{5,4},{6,5},{7,6},{8,15},{9,8},{10,9... | collective-permute-start | bytes 294920 | tf_op jit(solution)/shard_map/ppermute | solution.py:752
  78.3 5.8 %collective-permute-start.12 = (bf16[384,128]{1,0:T(8,128)(2,1)S(1)}, bf16[384,128]{1,0:T(8,128)(2,1)S(1)}, u32[]{:S(2)}, u32[]{:S(2)}) collective-permute-start(bf16[384,128]{1,0:T(8,128)(2,1)S(1)} %get-tuple-element.102), channel_id=1, source_target_pairs={{0,6},{1,7},{2,0},{3,1},{4,2},{5,3},{6,4},{7,5},{8,14},{9,15},{10,... | collective-permute-start | bytes 294920 | tf_op jit(solution)/shard_map/ppermute | solution.py:752
  79.7 6.4 %collective-permute-start.16 = (bf16[384,128]{1,0:T(8,128)(2,1)S(1)}, bf16[384,128]{1,0:T(8,128)(2,1)S(1)}, u32[]{:S(2)}, u32[]{:S(2)}) collective-permute-start(bf16[384,128]{1,0:T(8,128)(2,1)S(1)} %get-tuple-element.106), channel_id=1, source_target_pairs={{0,2},{1,3},{2,4},{3,5},{4,6},{5,7},{6,0},{7,1},{8,10},{9,11},{10,... | collective-permute-start | bytes 294920 | tf_op jit(solution)/shard_map/ppermute | solution.py:752
  80.4 7.4 %collective-permute-start.17 = (bf16[384,128]{1,0:T(8,128)(2,1)S(1)}, bf16[384,128]{1,0:T(8,128)(2,1)S(1)}, u32[]{:S(2)}, u32[]{:S(2)}) collective-permute-start(bf16[384,128]{1,0:T(8,128)(2,1)S(1)} %get-tuple-element.107), channel_id=1, source_target_pairs={{0,1},{1,2},{2,3},{3,4},{4,5},{5,6},{6,7},{7,0},{8,9},{9,10},{10,1... | collective-permute-start | bytes 294920 | tf_op jit(solution)/shard_map/ppermute | solution.py:752
  80.6 12.4 %collective-permute-start.20 = (bf16[4,224,128]{2,1,0:T(8,128)(2,1)S(1)}, bf16[4,224,128]{2,1,0:T(8,128)(2,1)S(1)}, u32[]{:S(2)}, u32[]{:S(2)}) collective-permute-start(bf16[4,224,128]{2,1,0:T(8,128)(2,1)S(1)} %get-tuple-element.119), channel_id=1, source_target_pairs={{0,1},{1,0},{2,3},{3,2},{4,5},{5,4},{6,7},{7,6},{8,9},{9,8},{10,11... | collective-permute-start | bytes 688136 | tf_op jit(solution)/shard_map/ppermute | solution.py:567
  88.0 6.1 %collective-permute-start.22 = (bf16[4,224,128]{2,1,0:T(8,128)(2,1)S(1)}, bf16[4,224,128]{2,1,0:T(8,128)(2,1)S(1)}, u32[]{:S(2)}, u32[]{:S(2)}) collective-permute-start(bf16[4,224,128]{2,1,0:T(8,128)(2,1)S(1)} %get-tuple-element.122), channel_id=1, source_target_pairs={{0,16},{8,24},{16,0},{24,8},{1,17},{9,25},{17,1},{25,9},{2,18},{10... | collective-permute-start | bytes 688136 | tf_op jit(solution)/shard_map/ppermute | solution.py:567
  88.5 10.3 %copy-start = (s32[1,512]{1,0:T(1,128)S(1)}, s32[1,512]{1,0:T(1,128)}, u32[]{:S(2)}) copy-start(s32[1,512]{1,0:T(1,128)} %refs_0_.3) | copy-start | bytes 6148
  94.4 6.8 %collective-permute-start.23 = (bf16[448,128]{1,0:T(8,128)(2,1)S(1)}, bf16[448,128]{1,0:T(8,128)(2,1)S(1)}, u32[]{:S(2)}, u32[]{:S(2)}) collective-permute-start(bf16[448,128]{1,0:T(8,128)(2,1)S(1)} %get-tuple-element.125), channel_id=1, source_target_pairs={{0,6},{1,7},{2,4},{3,5},{4,2},{5,3},{6,0},{7,1},{8,14},{9,15},{10,... | collective-permute-start | bytes 344072 | tf_op jit(solution)/shard_map/ppermute | solution.py:567
  95.9 7.7 %collective-permute-start.24 = (bf16[448,128]{1,0:T(8,128)(2,1)S(1)}, bf16[448,128]{1,0:T(8,128)(2,1)S(1)}, u32[]{:S(2)}, u32[]{:S(2)}) collective-permute-start(bf16[448,128]{1,0:T(8,128)(2,1)S(1)} %get-tuple-element.126), channel_id=1, source_target_pairs={{0,4},{1,5},{2,6},{3,7},{4,0},{5,1},{6,2},{7,3},{8,12},{9,13},{10,... | collective-permute-start | bytes 344072 | tf_op jit(solution)/shard_map/ppermute | solution.py:567
  95.9 7.7 %collective-permute-start.25 = (bf16[448,128]{1,0:T(8,128)(2,1)S(1)}, bf16[448,128]{1,0:T(8,128)(2,1)S(1)}, u32[]{:S(2)}, u32[]{:S(2)}) collective-permute-start(bf16[448,128]{1,0:T(8,128)(2,1)S(1)} %get-tuple-element.127), channel_id=1, source_target_pairs={{0,2},{1,3},{2,0},{3,1},{4,6},{5,7},{6,4},{7,5},{8,10},{9,11},{10,... | collective-permute-start | bytes 344072 | tf_op jit(solution)/shard_map/ppermute | solution.py:567
  103.6 4.9 %collective-permute-start.26 = (bf16[448,128]{1,0:T(8,128)(2,1)S(1)}, bf16[448,128]{1,0:T(8,128)(2,1)S(1)}, u32[]{:S(2)}, u32[]{:S(2)}) collective-permute-start(bf16[448,128]{1,0:T(8,128)(2,1)S(1)} %sum.1.refs_0_), channel_id=1, source_target_pairs={{0,16},{8,24},{16,0},{24,8},{1,17},{9,25},{17,1},{25,9},{2,18},{10... | collective-permute-start | bytes 344072 | tf_op jit(solution)/shard_map/ppermute | solution.py:567
  108.5 1.6 %collective-permute-start.27 = (bf16[448,256]{1,0:T(8,128)(2,1)S(1)}, bf16[448,256]{1,0:T(8,128)(2,1)S(1)}, u32[]{:S(2)}, u32[]{:S(2)}) collective-permute-start(bf16[448,256]{1,0:T(8,128)(2,1)S(1)} %join.2.refs_0_), channel_id=1, source_target_pairs={{0,8},{8,0},{16,24},{24,16},{1,9},{9,1},{17,25},{25,17},{2,10},{10... | collective-permute-start | bytes 688136 | tf_op jit(solution)/shard_map/ppermute | solution.py:567
